TPU v7x, 512 devices: a whole 4x4x16 slice. The times are simulated.
512 devices in a mesh: stream: 32 (over z, core), span: 16 (over y, x).
Axes of the slice: x: 4, y: 4, z: 16, core: 2. Of those that a mesh axis runs over, the one named last changes fastest.
Arguments:
- rhs: bfloat16 [32, 64, 8, 32, 128], P('stream', 'span'), may hold values from -6 to 6
- previous: bfloat16 [32, 64, 8, 32, 128], P('stream', 'span'), may hold values from -6 to 6
- inverse_blocks: bfloat16 [32, 64, 8, 128, 128], P('stream', 'span'), as said below
- upstream_blocks: bfloat16 [32, 64, 8, 128, 128], P('stream', 'span'), may hold values from -1.1953125 to 1.1953125
- lower_gain: float32 [32, 64, 8, 128], P('stream', 'span'), may hold values from 0.2 to 1
- upper_gain: float32 [32, 64, 8, 128], P('stream', 'span'), may hold values from 0.2 to 1
- widths: int32 [32], P('stream'), may hold values from 2 to 8, as said below
- upstream_index: int32 [32, 64, 8], P('stream', 'span'), may hold values from 0 to 7, as said below
Outputs:
- swept: bfloat16 [32, 64, 8, 32, 128], P('stream', 'span')
Inputs may be any that keep to these rules, and one draw needn't show every extreme that they name: `widths`: some section that has a following section has exactly 8 active clusters, and another has 2. `upstream_index`: for a section i after the first and an active slot k < widths[i], the entry is below widths[i - 1]; slot 0 of every slab names widths[i - 1] - 1. Entries of inactive slots and of the first section are 0. `inverse_blocks`: each block is the inverse of a diagonal block of the preconditioner, with entries of order 0.02 to 0.7 on its diagonal.
All inputs are finite; a program needn't handle non-finite values.
Results may differ from a plain program's by a relative error of at most 0.039.
Values may be sent and summed in bfloat16 or wider, within the bound.
No kernel may reach another device: no remote copies, remote signals or barrier semaphores. Data moves between devices by JAX's collectives and lax.ppermute only.
A program may use at most 64 MiB of HBM per device.

v0:
```python
import jax
import jax.numpy as jnp
from jax import lax
from jax.sharding import PartitionSpec as P


def with_halo(x, sides, width):
    for axis, dim in sides:
        peers, length = (lax.axis_size(axis), x.shape[dim])
        up = [(i, (i + 1) % peers) for i in range(peers - 1)]
        down = [(j, i) for i, j in up]
        last = lax.slice_in_dim(x, length - width, length, axis=dim)
        leading = lax.slice_in_dim(x, 0, width, axis=dim)
        before = lax.ppermute(last, axis, up)
        after = lax.ppermute(leading, axis, down)
        x = jnp.concatenate([before, x, after], axis=dim)
    return x


def shifted(value, axis, steps):
    count = lax.axis_size(axis)
    leading, last = (max(0, -steps), min(count, count - steps))
    return lax.ppermute(value, axis, [(source, source + steps) for source in range(leading, last)])


def local(
    rhs, previous, inverse_blocks, upstream_blocks, lower_gain, upper_gain, widths, upstream_index
):
    padded = with_halo(previous, (("span", 1),), 1)
    below_slab = padded[0, :-2].astype(jnp.float32)
    above_slab = padded[0, 2:].astype(jnp.float32)
    side = lower_gain[0][:, :, None, :] * below_slab + upper_gain[0][:, :, None, :] * above_slab
    local_part = rhs[0].astype(jnp.float32) - side
    inverse = inverse_blocks[0]
    coupling = upstream_blocks[0]
    neighbour = upstream_index[0]
    slots = jnp.arange(inverse.shape[1], dtype=jnp.int32)
    active_slots = (slots < widths[0])[None, :, None, None]
    position = lax.axis_index("stream")
    sections = lax.axis_size("stream")

    def sweep_block(inflow, part_local, part_inverse, part_coupling, part_neighbour):
        picked = jnp.take_along_axis(inflow, part_neighbour[:, :, None, None], axis=1)
        coupled = jnp.einsum(
            "mkvj,mkij->mkvi", picked, part_coupling, preferred_element_type=jnp.float32
        )
        remainder = (part_local - coupled).astype(jnp.bfloat16)
        updated = jnp.einsum(
            "mkvj,mkij->mkvi", remainder, part_inverse, preferred_element_type=jnp.float32
        ).astype(jnp.bfloat16)
        return jnp.where(active_slots, updated, jnp.zeros_like(updated))

    result_start = jnp.zeros(rhs.shape[1:], jnp.bfloat16)

    def advance_whole(step_count, result):
        inflow = shifted(result, "stream", 1)
        updated = sweep_block(inflow, local_part, inverse, coupling, neighbour)
        return jnp.where(step_count == position, updated, result)

    result = lax.fori_loop(0, sections, advance_whole, result_start)
    return result[None]


def solution(mesh):
    in_specs = (
        P("stream", "span", None, None, None),
        P("stream", "span", None, None, None),
        P("stream", "span", None, None, None),
        P("stream", "span", None, None, None),
        P("stream", "span", None, None),
        P("stream", "span", None, None),
        P("stream"),
        P("stream", "span", None),
    )
    out_specs = P("stream", "span", None, None, None)
    return jax.shard_map(local, mesh=mesh, in_specs=in_specs, out_specs=out_specs, check_vma=False)
```

profile of v0, /device:TPU:103, one launch (start us, length us, event | category | flops | bytes accessed | tf_op | source)
XLA Modules:
  0.0 366.5 jit_solution(881511213079225940)
XLA Ops:
  1.0 3.1 collective-permute-start.1
  6.3 4.9 %collective-permute-done.2 = bf16[1,1,8,32,128]{4,3,2,1,0:T(8,128)(2,1)S(1)} collective-permute-done((bf16[1,1,8,32,128]{4,3,2,1,0:T(8,128)(2,1)S(1)}, bf16[1,1,8,32,128]{4,3,2,1,0:T(8,128)(2,1)S(1)}, u32[]{:S(2)}, u32[]{:S(2)}) %collective-permute-start.2) | collective-permute-done | bytes 65568 | tf_op jit(solution)/shard_map/ppermute | solution.py:15
  13.0 352.8 %while.14 = (s32[]{:T(128)}, bf16[4,8,32,128]{3,2,1,0:T(8,128)(2,1)S(1)}, s32[]{:T(128)}, s32[1,4,8]{2,1,0:T(4,128)S(1)}, bf16[4,8,128,128]{3,2,1,0:T(8,128)(2,1...) while((s32[]{:T(128)}, ...), condition=%wide.region_1.2_spmd.clone, body=%wide.region_0.1_spmd.clone.sunk | while | flops 68026824 | bytes 9700497 | solution.py:60
  13.0 6.9 %collective-permute-start = (bf16[4,8,32,128]{3,2,1,0:T(8,128)(2,1)S(1)}, bf16[4,8,32,128]{3,2,1,0:T(8,128)(2,1)S(1)}, u32[]{:S(2)}, u32[]{:S(2)}) collective-permute-start(bf16[4,8,32,128]{3,2,1,0:T(8,128)(2,1)S(1)} %broadcast_select_fusion.2), channel_id=1, source_target_pairs={{0,16},{16,32},{32,48},{48,64},{64,80},{80,96},{96,112},{112,128},... | collective-permute-start | bytes 786440 | tf_op jit(solution)/shard_map/while/body/eval_jaxpr/ppermute | solution.py:23
  20.7 2.5 collective-permute-done
  25.2 5.7 %collective-permute-start = (bf16[4,8,32,128]{3,2,1,0:T(8,128)(2,1)S(1)}, bf16[4,8,32,128]{3,2,1,0:T(8,128)(2,1)S(1)}, u32[]{:S(2)}, u32[]{:S(2)}) collective-permute-start(bf16[4,8,32,128]{3,2,1,0:T(8,128)(2,1)S(1)} %broadcast_select_fusion.2), channel_id=1, source_target_pairs={{0,16},{16,32},{32,48},{48,64},{64,80},{80,96},{96,112},{112,128},... | collective-permute-start | bytes 786440 | tf_op jit(solution)/shard_map/while/body/eval_jaxpr/ppermute | solution.py:23
  31.7 2.5 collective-permute-done
  36.2 5.7 %collective-permute-start = (bf16[4,8,32,128]{3,2,1,0:T(8,128)(2,1)S(1)}, bf16[4,8,32,128]{3,2,1,0:T(8,128)(2,1)S(1)}, u32[]{:S(2)}, u32[]{:S(2)}) collective-permute-start(bf16[4,8,32,128]{3,2,1,0:T(8,128)(2,1)S(1)} %broadcast_select_fusion.2), channel_id=1, source_target_pairs={{0,16},{16,32},{32,48},{48,64},{64,80},{80,96},{96,112},{112,128},... | collective-permute-start | bytes 786440 | tf_op jit(solution)/shard_map/while/body/eval_jaxpr/ppermute | solution.py:23
  42.7 2.5 collective-permute-done
  47.2 5.7 %collective-permute-start = (bf16[4,8,32,128]{3,2,1,0:T(8,128)(2,1)S(1)}, bf16[4,8,32,128]{3,2,1,0:T(8,128)(2,1)S(1)}, u32[]{:S(2)}, u32[]{:S(2)}) collective-permute-start(bf16[4,8,32,128]{3,2,1,0:T(8,128)(2,1)S(1)} %broadcast_select_fusion.2), channel_id=1, source_target_pairs={{0,16},{16,32},{32,48},{48,64},{64,80},{80,96},{96,112},{112,128},... | collective-permute-start | bytes 786440 | tf_op jit(solution)/shard_map/while/body/eval_jaxpr/ppermute | solution.py:23
  53.7 2.5 collective-permute-done
  58.1 5.7 %collective-permute-start = (bf16[4,8,32,128]{3,2,1,0:T(8,128)(2,1)S(1)}, bf16[4,8,32,128]{3,2,1,0:T(8,128)(2,1)S(1)}, u32[]{:S(2)}, u32[]{:S(2)}) collective-permute-start(bf16[4,8,32,128]{3,2,1,0:T(8,128)(2,1)S(1)} %broadcast_select_fusion.2), channel_id=1, source_target_pairs={{0,16},{16,32},{32,48},{48,64},{64,80},{80,96},{96,112},{112,128},... | collective-permute-start | bytes 786440 | tf_op jit(solution)/shard_map/while/body/eval_jaxpr/ppermute | solution.py:23
  64.6 2.5 collective-permute-done
  69.1 5.7 %collective-permute-start = (bf16[4,8,32,128]{3,2,1,0:T(8,128)(2,1)S(1)}, bf16[4,8,32,128]{3,2,1,0:T(8,128)(2,1)S(1)}, u32[]{:S(2)}, u32[]{:S(2)}) collective-permute-start(bf16[4,8,32,128]{3,2,1,0:T(8,128)(2,1)S(1)} %broadcast_select_fusion.2), channel_id=1, source_target_pairs={{0,16},{16,32},{32,48},{48,64},{64,80},{80,96},{96,112},{112,128},... | collective-permute-start | bytes 786440 | tf_op jit(solution)/shard_map/while/body/eval_jaxpr/ppermute | solution.py:23
  75.6 2.5 collective-permute-done
  80.1 5.7 %collective-permute-start = (bf16[4,8,32,128]{3,2,1,0:T(8,128)(2,1)S(1)}, bf16[4,8,32,128]{3,2,1,0:T(8,128)(2,1)S(1)}, u32[]{:S(2)}, u32[]{:S(2)}) collective-permute-start(bf16[4,8,32,128]{3,2,1,0:T(8,128)(2,1)S(1)} %broadcast_select_fusion.2), channel_id=1, source_target_pairs={{0,16},{16,32},{32,48},{48,64},{64,80},{80,96},{96,112},{112,128},... | collective-permute-start | bytes 786440 | tf_op jit(solution)/shard_map/while/body/eval_jaxpr/ppermute | solution.py:23
  86.6 2.5 collective-permute-done
  91.1 5.7 %collective-permute-start = (bf16[4,8,32,128]{3,2,1,0:T(8,128)(2,1)S(1)}, bf16[4,8,32,128]{3,2,1,0:T(8,128)(2,1)S(1)}, u32[]{:S(2)}, u32[]{:S(2)}) collective-permute-start(bf16[4,8,32,128]{3,2,1,0:T(8,128)(2,1)S(1)} %broadcast_select_fusion.2), channel_id=1, source_target_pairs={{0,16},{16,32},{32,48},{48,64},{64,80},{80,96},{96,112},{112,128},... | collective-permute-start | bytes 786440 | tf_op jit(solution)/shard_map/while/body/eval_jaxpr/ppermute | solution.py:23
  97.6 2.5 collective-permute-done
  102.1 5.7 %collective-permute-start = (bf16[4,8,32,128]{3,2,1,0:T(8,128)(2,1)S(1)}, bf16[4,8,32,128]{3,2,1,0:T(8,128)(2,1)S(1)}, u32[]{:S(2)}, u32[]{:S(2)}) collective-permute-start(bf16[4,8,32,128]{3,2,1,0:T(8,128)(2,1)S(1)} %broadcast_select_fusion.2), channel_id=1, source_target_pairs={{0,16},{16,32},{32,48},{48,64},{64,80},{80,96},{96,112},{112,128},... | collective-permute-start | bytes 786440 | tf_op jit(solution)/shard_map/while/body/eval_jaxpr/ppermute | solution.py:23
  108.6 2.5 collective-permute-done
  113.1 5.7 %collective-permute-start = (bf16[4,8,32,128]{3,2,1,0:T(8,128)(2,1)S(1)}, bf16[4,8,32,128]{3,2,1,0:T(8,128)(2,1)S(1)}, u32[]{:S(2)}, u32[]{:S(2)}) collective-permute-start(bf16[4,8,32,128]{3,2,1,0:T(8,128)(2,1)S(1)} %broadcast_select_fusion.2), channel_id=1, source_target_pairs={{0,16},{16,32},{32,48},{48,64},{64,80},{80,96},{96,112},{112,128},... | collective-permute-start | bytes 786440 | tf_op jit(solution)/shard_map/while/body/eval_jaxpr/ppermute | solution.py:23
  119.6 2.5 collective-permute-done
  124.1 5.7 %collective-permute-start = (bf16[4,8,32,128]{3,2,1,0:T(8,128)(2,1)S(1)}, bf16[4,8,32,128]{3,2,1,0:T(8,128)(2,1)S(1)}, u32[]{:S(2)}, u32[]{:S(2)}) collective-permute-start(bf16[4,8,32,128]{3,2,1,0:T(8,128)(2,1)S(1)} %broadcast_select_fusion.2), channel_id=1, source_target_pairs={{0,16},{16,32},{32,48},{48,64},{64,80},{80,96},{96,112},{112,128},... | collective-permute-start | bytes 786440 | tf_op jit(solution)/shard_map/while/body/eval_jaxpr/ppermute | solution.py:23
  130.6 2.5 collective-permute-done
  135.1 5.7 %collective-permute-start = (bf16[4,8,32,128]{3,2,1,0:T(8,128)(2,1)S(1)}, bf16[4,8,32,128]{3,2,1,0:T(8,128)(2,1)S(1)}, u32[]{:S(2)}, u32[]{:S(2)}) collective-permute-start(bf16[4,8,32,128]{3,2,1,0:T(8,128)(2,1)S(1)} %broadcast_select_fusion.2), channel_id=1, source_target_pairs={{0,16},{16,32},{32,48},{48,64},{64,80},{80,96},{96,112},{112,128},... | collective-permute-start | bytes 786440 | tf_op jit(solution)/shard_map/while/body/eval_jaxpr/ppermute | solution.py:23
  141.6 2.5 collective-permute-done
  146.1 5.7 %collective-permute-start = (bf16[4,8,32,128]{3,2,1,0:T(8,128)(2,1)S(1)}, bf16[4,8,32,128]{3,2,1,0:T(8,128)(2,1)S(1)}, u32[]{:S(2)}, u32[]{:S(2)}) collective-permute-start(bf16[4,8,32,128]{3,2,1,0:T(8,128)(2,1)S(1)} %broadcast_select_fusion.2), channel_id=1, source_target_pairs={{0,16},{16,32},{32,48},{48,64},{64,80},{80,96},{96,112},{112,128},... | collective-permute-start | bytes 786440 | tf_op jit(solution)/shard_map/while/body/eval_jaxpr/ppermute | solution.py:23
  152.6 2.5 collective-permute-done
  157.0 5.7 %collective-permute-start = (bf16[4,8,32,128]{3,2,1,0:T(8,128)(2,1)S(1)}, bf16[4,8,32,128]{3,2,1,0:T(8,128)(2,1)S(1)}, u32[]{:S(2)}, u32[]{:S(2)}) collective-permute-start(bf16[4,8,32,128]{3,2,1,0:T(8,128)(2,1)S(1)} %broadcast_select_fusion.2), channel_id=1, source_target_pairs={{0,16},{16,32},{32,48},{48,64},{64,80},{80,96},{96,112},{112,128},... | collective-permute-start | bytes 786440 | tf_op jit(solution)/shard_map/while/body/eval_jaxpr/ppermute | solution.py:23
  163.5 2.5 collective-permute-done
  168.0 5.7 %collective-permute-start = (bf16[4,8,32,128]{3,2,1,0:T(8,128)(2,1)S(1)}, bf16[4,8,32,128]{3,2,1,0:T(8,128)(2,1)S(1)}, u32[]{:S(2)}, u32[]{:S(2)}) collective-permute-start(bf16[4,8,32,128]{3,2,1,0:T(8,128)(2,1)S(1)} %broadcast_select_fusion.2), channel_id=1, source_target_pairs={{0,16},{16,32},{32,48},{48,64},{64,80},{80,96},{96,112},{112,128},... | collective-permute-start | bytes 786440 | tf_op jit(solution)/shard_map/while/body/eval_jaxpr/ppermute | solution.py:23
  174.5 2.5 collective-permute-done
  179.0 5.7 %collective-permute-start = (bf16[4,8,32,128]{3,2,1,0:T(8,128)(2,1)S(1)}, bf16[4,8,32,128]{3,2,1,0:T(8,128)(2,1)S(1)}, u32[]{:S(2)}, u32[]{:S(2)}) collective-permute-start(bf16[4,8,32,128]{3,2,1,0:T(8,128)(2,1)S(1)} %broadcast_select_fusion.2), channel_id=1, source_target_pairs={{0,16},{16,32},{32,48},{48,64},{64,80},{80,96},{96,112},{112,128},... | collective-permute-start | bytes 786440 | tf_op jit(solution)/shard_map/while/body/eval_jaxpr/ppermute | solution.py:23
  185.5 2.5 collective-permute-done
  190.0 5.7 %collective-permute-start = (bf16[4,8,32,128]{3,2,1,0:T(8,128)(2,1)S(1)}, bf16[4,8,32,128]{3,2,1,0:T(8,128)(2,1)S(1)}, u32[]{:S(2)}, u32[]{:S(2)}) collective-permute-start(bf16[4,8,32,128]{3,2,1,0:T(8,128)(2,1)S(1)} %broadcast_select_fusion.2), channel_id=1, source_target_pairs={{0,16},{16,32},{32,48},{48,64},{64,80},{80,96},{96,112},{112,128},... | collective-permute-start | bytes 786440 | tf_op jit(solution)/shard_map/while/body/eval_jaxpr/ppermute | solution.py:23
  196.5 2.5 collective-permute-done
  201.0 5.7 %collective-permute-start = (bf16[4,8,32,128]{3,2,1,0:T(8,128)(2,1)S(1)}, bf16[4,8,32,128]{3,2,1,0:T(8,128)(2,1)S(1)}, u32[]{:S(2)}, u32[]{:S(2)}) collective-permute-start(bf16[4,8,32,128]{3,2,1,0:T(8,128)(2,1)S(1)} %broadcast_select_fusion.2), channel_id=1, source_target_pairs={{0,16},{16,32},{32,48},{48,64},{64,80},{80,96},{96,112},{112,128},... | collective-permute-start | bytes 786440 | tf_op jit(solution)/shard_map/while/body/eval_jaxpr/ppermute | solution.py:23
  207.5 2.5 collective-permute-done
  212.0 5.7 %collective-permute-start = (bf16[4,8,32,128]{3,2,1,0:T(8,128)(2,1)S(1)}, bf16[4,8,32,128]{3,2,1,0:T(8,128)(2,1)S(1)}, u32[]{:S(2)}, u32[]{:S(2)}) collective-permute-start(bf16[4,8,32,128]{3,2,1,0:T(8,128)(2,1)S(1)} %broadcast_select_fusion.2), channel_id=1, source_target_pairs={{0,16},{16,32},{32,48},{48,64},{64,80},{80,96},{96,112},{112,128},... | collective-permute-start | bytes 786440 | tf_op jit(solution)/shard_map/while/body/eval_jaxpr/ppermute | solution.py:23
  218.5 2.5 collective-permute-done
  223.0 5.7 %collective-permute-start = (bf16[4,8,32,128]{3,2,1,0:T(8,128)(2,1)S(1)}, bf16[4,8,32,128]{3,2,1,0:T(8,128)(2,1)S(1)}, u32[]{:S(2)}, u32[]{:S(2)}) collective-permute-start(bf16[4,8,32,128]{3,2,1,0:T(8,128)(2,1)S(1)} %broadcast_select_fusion.2), channel_id=1, source_target_pairs={{0,16},{16,32},{32,48},{48,64},{64,80},{80,96},{96,112},{112,128},... | collective-permute-start | bytes 786440 | tf_op jit(solution)/shard_map/while/body/eval_jaxpr/ppermute | solution.py:23
  229.5 2.5 collective-permute-done
  234.0 5.7 %collective-permute-start = (bf16[4,8,32,128]{3,2,1,0:T(8,128)(2,1)S(1)}, bf16[4,8,32,128]{3,2,1,0:T(8,128)(2,1)S(1)}, u32[]{:S(2)}, u32[]{:S(2)}) collective-permute-start(bf16[4,8,32,128]{3,2,1,0:T(8,128)(2,1)S(1)} %broadcast_select_fusion.2), channel_id=1, source_target_pairs={{0,16},{16,32},{32,48},{48,64},{64,80},{80,96},{96,112},{112,128},... | collective-permute-start | bytes 786440 | tf_op jit(solution)/shard_map/while/body/eval_jaxpr/ppermute | solution.py:23
  240.5 2.5 collective-permute-done
  245.0 5.7 %collective-permute-start = (bf16[4,8,32,128]{3,2,1,0:T(8,128)(2,1)S(1)}, bf16[4,8,32,128]{3,2,1,0:T(8,128)(2,1)S(1)}, u32[]{:S(2)}, u32[]{:S(2)}) collective-permute-start(bf16[4,8,32,128]{3,2,1,0:T(8,128)(2,1)S(1)} %broadcast_select_fusion.2), channel_id=1, source_target_pairs={{0,16},{16,32},{32,48},{48,64},{64,80},{80,96},{96,112},{112,128},... | collective-permute-start | bytes 786440 | tf_op jit(solution)/shard_map/while/body/eval_jaxpr/ppermute | solution.py:23
  251.5 2.5 collective-permute-done
  255.9 5.7 %collective-permute-start = (bf16[4,8,32,128]{3,2,1,0:T(8,128)(2,1)S(1)}, bf16[4,8,32,128]{3,2,1,0:T(8,128)(2,1)S(1)}, u32[]{:S(2)}, u32[]{:S(2)}) collective-permute-start(bf16[4,8,32,128]{3,2,1,0:T(8,128)(2,1)S(1)} %broadcast_select_fusion.2), channel_id=1, source_target_pairs={{0,16},{16,32},{32,48},{48,64},{64,80},{80,96},{96,112},{112,128},... | collective-permute-start | bytes 786440 | tf_op jit(solution)/shard_map/while/body/eval_jaxpr/ppermute | solution.py:23
  266.9 5.7 %collective-permute-start = (bf16[4,8,32,128]{3,2,1,0:T(8,128)(2,1)S(1)}, bf16[4,8,32,128]{3,2,1,0:T(8,128)(2,1)S(1)}, u32[]{:S(2)}, u32[]{:S(2)}) collective-permute-start(bf16[4,8,32,128]{3,2,1,0:T(8,128)(2,1)S(1)} %broadcast_select_fusion.2), channel_id=1, source_target_pairs={{0,16},{16,32},{32,48},{48,64},{64,80},{80,96},{96,112},{112,128},... | collective-permute-start | bytes 786440 | tf_op jit(solution)/shard_map/while/body/eval_jaxpr/ppermute | solution.py:23
  273.4 2.5 collective-permute-done
  277.9 5.7 %collective-permute-start = (bf16[4,8,32,128]{3,2,1,0:T(8,128)(2,1)S(1)}, bf16[4,8,32,128]{3,2,1,0:T(8,128)(2,1)S(1)}, u32[]{:S(2)}, u32[]{:S(2)}) collective-permute-start(bf16[4,8,32,128]{3,2,1,0:T(8,128)(2,1)S(1)} %broadcast_select_fusion.2), channel_id=1, source_target_pairs={{0,16},{16,32},{32,48},{48,64},{64,80},{80,96},{96,112},{112,128},... | collective-permute-start | bytes 786440 | tf_op jit(solution)/shard_map/while/body/eval_jaxpr/ppermute | solution.py:23
  284.4 2.5 collective-permute-done
  288.9 5.7 %collective-permute-start = (bf16[4,8,32,128]{3,2,1,0:T(8,128)(2,1)S(1)}, bf16[4,8,32,128]{3,2,1,0:T(8,128)(2,1)S(1)}, u32[]{:S(2)}, u32[]{:S(2)}) collective-permute-start(bf16[4,8,32,128]{3,2,1,0:T(8,128)(2,1)S(1)} %broadcast_select_fusion.2), channel_id=1, source_target_pairs={{0,16},{16,32},{32,48},{48,64},{64,80},{80,96},{96,112},{112,128},... | collective-permute-start | bytes 786440 | tf_op jit(solution)/shard_map/while/body/eval_jaxpr/ppermute | solution.py:23
  299.9 5.7 %collective-permute-start = (bf16[4,8,32,128]{3,2,1,0:T(8,128)(2,1)S(1)}, bf16[4,8,32,128]{3,2,1,0:T(8,128)(2,1)S(1)}, u32[]{:S(2)}, u32[]{:S(2)}) collective-permute-start(bf16[4,8,32,128]{3,2,1,0:T(8,128)(2,1)S(1)} %broadcast_select_fusion.2), channel_id=1, source_target_pairs={{0,16},{16,32},{32,48},{48,64},{64,80},{80,96},{96,112},{112,128},... | collective-permute-start | bytes 786440 | tf_op jit(solution)/shard_map/while/body/eval_jaxpr/ppermute | solution.py:23
  306.4 2.5 collective-permute-done
  310.9 5.7 %collective-permute-start = (bf16[4,8,32,128]{3,2,1,0:T(8,128)(2,1)S(1)}, bf16[4,8,32,128]{3,2,1,0:T(8,128)(2,1)S(1)}, u32[]{:S(2)}, u32[]{:S(2)}) collective-permute-start(bf16[4,8,32,128]{3,2,1,0:T(8,128)(2,1)S(1)} %broadcast_select_fusion.2), channel_id=1, source_target_pairs={{0,16},{16,32},{32,48},{48,64},{64,80},{80,96},{96,112},{112,128},... | collective-permute-start | bytes 786440 | tf_op jit(solution)/shard_map/while/body/eval_jaxpr/ppermute | solution.py:23
  317.4 2.5 collective-permute-done
  321.9 5.7 %collective-permute-start = (bf16[4,8,32,128]{3,2,1,0:T(8,128)(2,1)S(1)}, bf16[4,8,32,128]{3,2,1,0:T(8,128)(2,1)S(1)}, u32[]{:S(2)}, u32[]{:S(2)}) collective-permute-start(bf16[4,8,32,128]{3,2,1,0:T(8,128)(2,1)S(1)} %broadcast_select_fusion.2), channel_id=1, source_target_pairs={{0,16},{16,32},{32,48},{48,64},{64,80},{80,96},{96,112},{112,128},... | collective-permute-start | bytes 786440 | tf_op jit(solution)/shard_map/while/body/eval_jaxpr/ppermute | solution.py:23
  328.4 2.5 collective-permute-done
  332.9 5.7 %collective-permute-start = (bf16[4,8,32,128]{3,2,1,0:T(8,128)(2,1)S(1)}, bf16[4,8,32,128]{3,2,1,0:T(8,128)(2,1)S(1)}, u32[]{:S(2)}, u32[]{:S(2)}) collective-permute-start(bf16[4,8,32,128]{3,2,1,0:T(8,128)(2,1)S(1)} %broadcast_select_fusion.2), channel_id=1, source_target_pairs={{0,16},{16,32},{32,48},{48,64},{64,80},{80,96},{96,112},{112,128},... | collective-permute-start | bytes 786440 | tf_op jit(solution)/shard_map/while/body/eval_jaxpr/ppermute | solution.py:23
  339.4 2.5 collective-permute-done
  343.9 5.7 %collective-permute-start = (bf16[4,8,32,128]{3,2,1,0:T(8,128)(2,1)S(1)}, bf16[4,8,32,128]{3,2,1,0:T(8,128)(2,1)S(1)}, u32[]{:S(2)}, u32[]{:S(2)}) collective-permute-start(bf16[4,8,32,128]{3,2,1,0:T(8,128)(2,1)S(1)} %broadcast_select_fusion.2), channel_id=1, source_target_pairs={{0,16},{16,32},{32,48},{48,64},{64,80},{80,96},{96,112},{112,128},... | collective-permute-start | bytes 786440 | tf_op jit(solution)/shard_map/while/body/eval_jaxpr/ppermute | solution.py:23
  354.8 5.7 %collective-permute-start = (bf16[4,8,32,128]{3,2,1,0:T(8,128)(2,1)S(1)}, bf16[4,8,32,128]{3,2,1,0:T(8,128)(2,1)S(1)}, u32[]{:S(2)}, u32[]{:S(2)}) collective-permute-start(bf16[4,8,32,128]{3,2,1,0:T(8,128)(2,1)S(1)} %broadcast_select_fusion.2), channel_id=1, source_target_pairs={{0,16},{16,32},{32,48},{48,64},{64,80},{80,96},{96,112},{112,128},... | collective-permute-start | bytes 786440 | tf_op jit(solution)/shard_map/while/body/eval_jaxpr/ppermute | solution.py:23
  361.4 2.5 collective-permute-done
  (306 shorter events, 98.9 us)
Async XLA Ops:
  0.0 11.2 %copy-start.3 = (bf16[1,4,8,32,128]{4,3,2,1,0:T(8,128)(2,1)S(1)}, bf16[1,4,8,32,128]{4,3,2,1,0:T(8,128)(2,1)}, u32[]{:S(2)}) copy-start(bf16[1,4,8,32,128]{4,3,2,1,0:T(8,128)(2,1)} %param.11) | copy-start | bytes 786436
  0.0 11.2 %copy-start.5 = (f32[1,4,8,128]{3,2,1,0:T(8,128)S(1)}, f32[1,4,8,128]{3,2,1,0:T(8,128)}, u32[]{:S(2)}) copy-start(f32[1,4,8,128]{3,2,1,0:T(8,128)} %param.15) | copy-start | bytes 49156
  0.0 12.3 %copy-start = (bf16[1,4,8,128,128]{4,3,2,1,0:T(8,128)(2,1)S(1)}, bf16[1,4,8,128,128]{4,3,2,1,0:T(8,128)(2,1)}, u32[]{:S(2)}) copy-start(bf16[1,4,8,128,128]{4,3,2,1,0:T(8,128)(2,1)} %param.13) | copy-start | bytes 3145732
  1.0 5.3 %collective-permute-start.1 = (bf16[1,1,8,32,128]{4,3,2,1,0:T(8,128)(2,1)S(1)}, bf16[1,1,8,32,128]{4,3,2,1,0:T(8,128)(2,1)S(1)}, u32[]{:S(2)}, u32[]{:S(2)}) collective-permute-start(bf16[1,1,8,32,128]{4,3,2,1,0:T(8,128)(2,1)S(1)} %get-tuple-element.191), channel_id=1, source_target_pairs={{0,1},{1,2},{2,3},{3,4},{4,5},{5,6},{6,7},{7,8},{8,9},{9,10},{10,1... | collective-permute-start | bytes 196616 | tf_op jit(solution)/shard_map/ppermute | solution.py:14
  4.1 7.1 %collective-permute-start.2 = (bf16[1,1,8,32,128]{4,3,2,1,0:T(8,128)(2,1)S(1)}, bf16[1,1,8,32,128]{4,3,2,1,0:T(8,128)(2,1)S(1)}, u32[]{:S(2)}, u32[]{:S(2)}) collective-permute-start(bf16[1,1,8,32,128]{4,3,2,1,0:T(8,128)(2,1)S(1)} %get-tuple-element.192), channel_id=1, source_target_pairs={{1,0},{2,1},{3,2},{4,3},{5,4},{6,5},{7,6},{8,7},{9,8},{10,9},{11,1... | collective-permute-start | bytes 196616 | tf_op jit(solution)/shard_map/ppermute | solution.py:15
  13.0 10.9 %copy-start.1 = (bf16[4,8,128,128]{3,2,1,0:T(8,128)(2,1)S(1)}, bf16[4,8,128,128]{3,2,1,0:T(8,128)(2,1)}, u32[]{:S(2)}) copy-start(bf16[4,8,128,128]{3,2,1,0:T(8,128)(2,1)} %get-tuple-element.268) | copy-start | bytes 3145732 | tf_op jit(solution)/shard_map/while
  13.0 10.2 %collective-permute-start = (bf16[4,8,32,128]{3,2,1,0:T(8,128)(2,1)S(1)}, bf16[4,8,32,128]{3,2,1,0:T(8,128)(2,1)S(1)}, u32[]{:S(2)}, u32[]{:S(2)}) collective-permute-start(bf16[4,8,32,128]{3,2,1,0:T(8,128)(2,1)S(1)} %broadcast_select_fusion.2), channel_id=1, source_target_pairs={{0,16},{16,32},{32,48},{48,64},{64,80},{80,96},{96,112},{112,128},... | collective-permute-start | bytes 786440 | tf_op jit(solution)/shard_map/while/body/eval_jaxpr/ppermute | solution.py:23
  25.1 9.7 %copy-start.1 = (bf16[4,8,128,128]{3,2,1,0:T(8,128)(2,1)S(1)}, bf16[4,8,128,128]{3,2,1,0:T(8,128)(2,1)}, u32[]{:S(2)}) copy-start(bf16[4,8,128,128]{3,2,1,0:T(8,128)(2,1)} %get-tuple-element.268) | copy-start | bytes 3145732 | tf_op jit(solution)/shard_map/while
  25.2 9.0 %collective-permute-start = (bf16[4,8,32,128]{3,2,1,0:T(8,128)(2,1)S(1)}, bf16[4,8,32,128]{3,2,1,0:T(8,128)(2,1)S(1)}, u32[]{:S(2)}, u32[]{:S(2)}) collective-permute-start(bf16[4,8,32,128]{3,2,1,0:T(8,128)(2,1)S(1)} %broadcast_select_fusion.2), channel_id=1, source_target_pairs={{0,16},{16,32},{32,48},{48,64},{64,80},{80,96},{96,112},{112,128},... | collective-permute-start | bytes 786440 | tf_op jit(solution)/shard_map/while/body/eval_jaxpr/ppermute | solution.py:23
  36.1 9.7 %copy-start.1 = (bf16[4,8,128,128]{3,2,1,0:T(8,128)(2,1)S(1)}, bf16[4,8,128,128]{3,2,1,0:T(8,128)(2,1)}, u32[]{:S(2)}) copy-start(bf16[4,8,128,128]{3,2,1,0:T(8,128)(2,1)} %get-tuple-element.268) | copy-start | bytes 3145732 | tf_op jit(solution)/shard_map/while
  36.2 9.0 %collective-permute-start = (bf16[4,8,32,128]{3,2,1,0:T(8,128)(2,1)S(1)}, bf16[4,8,32,128]{3,2,1,0:T(8,128)(2,1)S(1)}, u32[]{:S(2)}, u32[]{:S(2)}) collective-permute-start(bf16[4,8,32,128]{3,2,1,0:T(8,128)(2,1)S(1)} %broadcast_select_fusion.2), channel_id=1, source_target_pairs={{0,16},{16,32},{32,48},{48,64},{64,80},{80,96},{96,112},{112,128},... | collective-permute-start | bytes 786440 | tf_op jit(solution)/shard_map/while/body/eval_jaxpr/ppermute | solution.py:23
  47.1 9.7 %copy-start.1 = (bf16[4,8,128,128]{3,2,1,0:T(8,128)(2,1)S(1)}, bf16[4,8,128,128]{3,2,1,0:T(8,128)(2,1)}, u32[]{:S(2)}) copy-start(bf16[4,8,128,128]{3,2,1,0:T(8,128)(2,1)} %get-tuple-element.268) | copy-start | bytes 3145732 | tf_op jit(solution)/shard_map/while
  47.2 9.0 %collective-permute-start = (bf16[4,8,32,128]{3,2,1,0:T(8,128)(2,1)S(1)}, bf16[4,8,32,128]{3,2,1,0:T(8,128)(2,1)S(1)}, u32[]{:S(2)}, u32[]{:S(2)}) collective-permute-start(bf16[4,8,32,128]{3,2,1,0:T(8,128)(2,1)S(1)} %broadcast_select_fusion.2), channel_id=1, source_target_pairs={{0,16},{16,32},{32,48},{48,64},{64,80},{80,96},{96,112},{112,128},... | collective-permute-start | bytes 786440 | tf_op jit(solution)/shard_map/while/body/eval_jaxpr/ppermute | solution.py:23
  58.1 9.7 %copy-start.1 = (bf16[4,8,128,128]{3,2,1,0:T(8,128)(2,1)S(1)}, bf16[4,8,128,128]{3,2,1,0:T(8,128)(2,1)}, u32[]{:S(2)}) copy-start(bf16[4,8,128,128]{3,2,1,0:T(8,128)(2,1)} %get-tuple-element.268) | copy-start | bytes 3145732 | tf_op jit(solution)/shard_map/while
  58.1 9.0 %collective-permute-start = (bf16[4,8,32,128]{3,2,1,0:T(8,128)(2,1)S(1)}, bf16[4,8,32,128]{3,2,1,0:T(8,128)(2,1)S(1)}, u32[]{:S(2)}, u32[]{:S(2)}) collective-permute-start(bf16[4,8,32,128]{3,2,1,0:T(8,128)(2,1)S(1)} %broadcast_select_fusion.2), channel_id=1, source_target_pairs={{0,16},{16,32},{32,48},{48,64},{64,80},{80,96},{96,112},{112,128},... | collective-permute-start | bytes 786440 | tf_op jit(solution)/shard_map/while/body/eval_jaxpr/ppermute | solution.py:23
  69.1 9.7 %copy-start.1 = (bf16[4,8,128,128]{3,2,1,0:T(8,128)(2,1)S(1)}, bf16[4,8,128,128]{3,2,1,0:T(8,128)(2,1)}, u32[]{:S(2)}) copy-start(bf16[4,8,128,128]{3,2,1,0:T(8,128)(2,1)} %get-tuple-element.268) | copy-start | bytes 3145732 | tf_op jit(solution)/shard_map/while
  69.1 9.0 %collective-permute-start = (bf16[4,8,32,128]{3,2,1,0:T(8,128)(2,1)S(1)}, bf16[4,8,32,128]{3,2,1,0:T(8,128)(2,1)S(1)}, u32[]{:S(2)}, u32[]{:S(2)}) collective-permute-start(bf16[4,8,32,128]{3,2,1,0:T(8,128)(2,1)S(1)} %broadcast_select_fusion.2), channel_id=1, source_target_pairs={{0,16},{16,32},{32,48},{48,64},{64,80},{80,96},{96,112},{112,128},... | collective-permute-start | bytes 786440 | tf_op jit(solution)/shard_map/while/body/eval_jaxpr/ppermute | solution.py:23
  80.1 9.7 %copy-start.1 = (bf16[4,8,128,128]{3,2,1,0:T(8,128)(2,1)S(1)}, bf16[4,8,128,128]{3,2,1,0:T(8,128)(2,1)}, u32[]{:S(2)}) copy-start(bf16[4,8,128,128]{3,2,1,0:T(8,128)(2,1)} %get-tuple-element.268) | copy-start | bytes 3145732 | tf_op jit(solution)/shard_map/while
  80.1 9.0 %collective-permute-start = (bf16[4,8,32,128]{3,2,1,0:T(8,128)(2,1)S(1)}, bf16[4,8,32,128]{3,2,1,0:T(8,128)(2,1)S(1)}, u32[]{:S(2)}, u32[]{:S(2)}) collective-permute-start(bf16[4,8,32,128]{3,2,1,0:T(8,128)(2,1)S(1)} %broadcast_select_fusion.2), channel_id=1, source_target_pairs={{0,16},{16,32},{32,48},{48,64},{64,80},{80,96},{96,112},{112,128},... | collective-permute-start | bytes 786440 | tf_op jit(solution)/shard_map/while/body/eval_jaxpr/ppermute | solution.py:23
  91.1 9.7 %copy-start.1 = (bf16[4,8,128,128]{3,2,1,0:T(8,128)(2,1)S(1)}, bf16[4,8,128,128]{3,2,1,0:T(8,128)(2,1)}, u32[]{:S(2)}) copy-start(bf16[4,8,128,128]{3,2,1,0:T(8,128)(2,1)} %get-tuple-element.268) | copy-start | bytes 3145732 | tf_op jit(solution)/shard_map/while
  91.1 9.0 %collective-permute-start = (bf16[4,8,32,128]{3,2,1,0:T(8,128)(2,1)S(1)}, bf16[4,8,32,128]{3,2,1,0:T(8,128)(2,1)S(1)}, u32[]{:S(2)}, u32[]{:S(2)}) collective-permute-start(bf16[4,8,32,128]{3,2,1,0:T(8,128)(2,1)S(1)} %broadcast_select_fusion.2), channel_id=1, source_target_pairs={{0,16},{16,32},{32,48},{48,64},{64,80},{80,96},{96,112},{112,128},... | collective-permute-start | bytes 786440 | tf_op jit(solution)/shard_map/while/body/eval_jaxpr/ppermute | solution.py:23
  102.1 9.7 %copy-start.1 = (bf16[4,8,128,128]{3,2,1,0:T(8,128)(2,1)S(1)}, bf16[4,8,128,128]{3,2,1,0:T(8,128)(2,1)}, u32[]{:S(2)}) copy-start(bf16[4,8,128,128]{3,2,1,0:T(8,128)(2,1)} %get-tuple-element.268) | copy-start | bytes 3145732 | tf_op jit(solution)/shard_map/while
  102.1 9.0 %collective-permute-start = (bf16[4,8,32,128]{3,2,1,0:T(8,128)(2,1)S(1)}, bf16[4,8,32,128]{3,2,1,0:T(8,128)(2,1)S(1)}, u32[]{:S(2)}, u32[]{:S(2)}) collective-permute-start(bf16[4,8,32,128]{3,2,1,0:T(8,128)(2,1)S(1)} %broadcast_select_fusion.2), channel_id=1, source_target_pairs={{0,16},{16,32},{32,48},{48,64},{64,80},{80,96},{96,112},{112,128},... | collective-permute-start | bytes 786440 | tf_op jit(solution)/shard_map/while/body/eval_jaxpr/ppermute | solution.py:23
  113.0 9.7 %copy-start.1 = (bf16[4,8,128,128]{3,2,1,0:T(8,128)(2,1)S(1)}, bf16[4,8,128,128]{3,2,1,0:T(8,128)(2,1)}, u32[]{:S(2)}) copy-start(bf16[4,8,128,128]{3,2,1,0:T(8,128)(2,1)} %get-tuple-element.268) | copy-start | bytes 3145732 | tf_op jit(solution)/shard_map/while
  113.1 9.0 %collective-permute-start = (bf16[4,8,32,128]{3,2,1,0:T(8,128)(2,1)S(1)}, bf16[4,8,32,128]{3,2,1,0:T(8,128)(2,1)S(1)}, u32[]{:S(2)}, u32[]{:S(2)}) collective-permute-start(bf16[4,8,32,128]{3,2,1,0:T(8,128)(2,1)S(1)} %broadcast_select_fusion.2), channel_id=1, source_target_pairs={{0,16},{16,32},{32,48},{48,64},{64,80},{80,96},{96,112},{112,128},... | collective-permute-start | bytes 786440 | tf_op jit(solution)/shard_map/while/body/eval_jaxpr/ppermute | solution.py:23
  124.0 9.7 %copy-start.1 = (bf16[4,8,128,128]{3,2,1,0:T(8,128)(2,1)S(1)}, bf16[4,8,128,128]{3,2,1,0:T(8,128)(2,1)}, u32[]{:S(2)}) copy-start(bf16[4,8,128,128]{3,2,1,0:T(8,128)(2,1)} %get-tuple-element.268) | copy-start | bytes 3145732 | tf_op jit(solution)/shard_map/while
  124.1 9.0 %collective-permute-start = (bf16[4,8,32,128]{3,2,1,0:T(8,128)(2,1)S(1)}, bf16[4,8,32,128]{3,2,1,0:T(8,128)(2,1)S(1)}, u32[]{:S(2)}, u32[]{:S(2)}) collective-permute-start(bf16[4,8,32,128]{3,2,1,0:T(8,128)(2,1)S(1)} %broadcast_select_fusion.2), channel_id=1, source_target_pairs={{0,16},{16,32},{32,48},{48,64},{64,80},{80,96},{96,112},{112,128},... | collective-permute-start | bytes 786440 | tf_op jit(solution)/shard_map/while/body/eval_jaxpr/ppermute | solution.py:23
  135.0 9.7 %copy-start.1 = (bf16[4,8,128,128]{3,2,1,0:T(8,128)(2,1)S(1)}, bf16[4,8,128,128]{3,2,1,0:T(8,128)(2,1)}, u32[]{:S(2)}) copy-start(bf16[4,8,128,128]{3,2,1,0:T(8,128)(2,1)} %get-tuple-element.268) | copy-start | bytes 3145732 | tf_op jit(solution)/shard_map/while
  135.1 9.0 %collective-permute-start = (bf16[4,8,32,128]{3,2,1,0:T(8,128)(2,1)S(1)}, bf16[4,8,32,128]{3,2,1,0:T(8,128)(2,1)S(1)}, u32[]{:S(2)}, u32[]{:S(2)}) collective-permute-start(bf16[4,8,32,128]{3,2,1,0:T(8,128)(2,1)S(1)} %broadcast_select_fusion.2), channel_id=1, source_target_pairs={{0,16},{16,32},{32,48},{48,64},{64,80},{80,96},{96,112},{112,128},... | collective-permute-start | bytes 786440 | tf_op jit(solution)/shard_map/while/body/eval_jaxpr/ppermute | solution.py:23
  146.0 9.7 %copy-start.1 = (bf16[4,8,128,128]{3,2,1,0:T(8,128)(2,1)S(1)}, bf16[4,8,128,128]{3,2,1,0:T(8,128)(2,1)}, u32[]{:S(2)}) copy-start(bf16[4,8,128,128]{3,2,1,0:T(8,128)(2,1)} %get-tuple-element.268) | copy-start | bytes 3145732 | tf_op jit(solution)/shard_map/while
  146.1 9.0 %collective-permute-start = (bf16[4,8,32,128]{3,2,1,0:T(8,128)(2,1)S(1)}, bf16[4,8,32,128]{3,2,1,0:T(8,128)(2,1)S(1)}, u32[]{:S(2)}, u32[]{:S(2)}) collective-permute-start(bf16[4,8,32,128]{3,2,1,0:T(8,128)(2,1)S(1)} %broadcast_select_fusion.2), channel_id=1, source_target_pairs={{0,16},{16,32},{32,48},{48,64},{64,80},{80,96},{96,112},{112,128},... | collective-permute-start | bytes 786440 | tf_op jit(solution)/shard_map/while/body/eval_jaxpr/ppermute | solution.py:23
  157.0 9.7 %copy-start.1 = (bf16[4,8,128,128]{3,2,1,0:T(8,128)(2,1)S(1)}, bf16[4,8,128,128]{3,2,1,0:T(8,128)(2,1)}, u32[]{:S(2)}) copy-start(bf16[4,8,128,128]{3,2,1,0:T(8,128)(2,1)} %get-tuple-element.268) | copy-start | bytes 3145732 | tf_op jit(solution)/shard_map/while
  157.0 9.0 %collective-permute-start = (bf16[4,8,32,128]{3,2,1,0:T(8,128)(2,1)S(1)}, bf16[4,8,32,128]{3,2,1,0:T(8,128)(2,1)S(1)}, u32[]{:S(2)}, u32[]{:S(2)}) collective-permute-start(bf16[4,8,32,128]{3,2,1,0:T(8,128)(2,1)S(1)} %broadcast_select_fusion.2), channel_id=1, source_target_pairs={{0,16},{16,32},{32,48},{48,64},{64,80},{80,96},{96,112},{112,128},... | collective-permute-start | bytes 786440 | tf_op jit(solution)/shard_map/while/body/eval_jaxpr/ppermute | solution.py:23
  168.0 9.7 %copy-start.1 = (bf16[4,8,128,128]{3,2,1,0:T(8,128)(2,1)S(1)}, bf16[4,8,128,128]{3,2,1,0:T(8,128)(2,1)}, u32[]{:S(2)}) copy-start(bf16[4,8,128,128]{3,2,1,0:T(8,128)(2,1)} %get-tuple-element.268) | copy-start | bytes 3145732 | tf_op jit(solution)/shard_map/while
  168.0 9.0 %collective-permute-start = (bf16[4,8,32,128]{3,2,1,0:T(8,128)(2,1)S(1)}, bf16[4,8,32,128]{3,2,1,0:T(8,128)(2,1)S(1)}, u32[]{:S(2)}, u32[]{:S(2)}) collective-permute-start(bf16[4,8,32,128]{3,2,1,0:T(8,128)(2,1)S(1)} %broadcast_select_fusion.2), channel_id=1, source_target_pairs={{0,16},{16,32},{32,48},{48,64},{64,80},{80,96},{96,112},{112,128},... | collective-permute-start | bytes 786440 | tf_op jit(solution)/shard_map/while/body/eval_jaxpr/ppermute | solution.py:23
  179.0 9.0 %collective-permute-start = (bf16[4,8,32,128]{3,2,1,0:T(8,128)(2,1)S(1)}, bf16[4,8,32,128]{3,2,1,0:T(8,128)(2,1)S(1)}, u32[]{:S(2)}, u32[]{:S(2)}) collective-permute-start(bf16[4,8,32,128]{3,2,1,0:T(8,128)(2,1)S(1)} %broadcast_select_fusion.2), channel_id=1, source_target_pairs={{0,16},{16,32},{32,48},{48,64},{64,80},{80,96},{96,112},{112,128},... | collective-permute-start | bytes 786440 | tf_op jit(solution)/shard_map/while/body/eval_jaxpr/ppermute | solution.py:23
  190.0 9.7 %copy-start.1 = (bf16[4,8,128,128]{3,2,1,0:T(8,128)(2,1)S(1)}, bf16[4,8,128,128]{3,2,1,0:T(8,128)(2,1)}, u32[]{:S(2)}) copy-start(bf16[4,8,128,128]{3,2,1,0:T(8,128)(2,1)} %get-tuple-element.268) | copy-start | bytes 3145732 | tf_op jit(solution)/shard_map/while
  190.0 9.0 %collective-permute-start = (bf16[4,8,32,128]{3,2,1,0:T(8,128)(2,1)S(1)}, bf16[4,8,32,128]{3,2,1,0:T(8,128)(2,1)S(1)}, u32[]{:S(2)}, u32[]{:S(2)}) collective-permute-start(bf16[4,8,32,128]{3,2,1,0:T(8,128)(2,1)S(1)} %broadcast_select_fusion.2), channel_id=1, source_target_pairs={{0,16},{16,32},{32,48},{48,64},{64,80},{80,96},{96,112},{112,128},... | collective-permute-start | bytes 786440 | tf_op jit(solution)/shard_map/while/body/eval_jaxpr/ppermute | solution.py:23
  201.0 9.7 %copy-start.1 = (bf16[4,8,128,128]{3,2,1,0:T(8,128)(2,1)S(1)}, bf16[4,8,128,128]{3,2,1,0:T(8,128)(2,1)}, u32[]{:S(2)}) copy-start(bf16[4,8,128,128]{3,2,1,0:T(8,128)(2,1)} %get-tuple-element.268) | copy-start | bytes 3145732 | tf_op jit(solution)/shard_map/while
  201.0 9.0 %collective-permute-start = (bf16[4,8,32,128]{3,2,1,0:T(8,128)(2,1)S(1)}, bf16[4,8,32,128]{3,2,1,0:T(8,128)(2,1)S(1)}, u32[]{:S(2)}, u32[]{:S(2)}) collective-permute-start(bf16[4,8,32,128]{3,2,1,0:T(8,128)(2,1)S(1)} %broadcast_select_fusion.2), channel_id=1, source_target_pairs={{0,16},{16,32},{32,48},{48,64},{64,80},{80,96},{96,112},{112,128},... | collective-permute-start | bytes 786440 | tf_op jit(solution)/shard_map/while/body/eval_jaxpr/ppermute | solution.py:23
  211.9 9.7 %copy-start.1 = (bf16[4,8,128,128]{3,2,1,0:T(8,128)(2,1)S(1)}, bf16[4,8,128,128]{3,2,1,0:T(8,128)(2,1)}, u32[]{:S(2)}) copy-start(bf16[4,8,128,128]{3,2,1,0:T(8,128)(2,1)} %get-tuple-element.268) | copy-start | bytes 3145732 | tf_op jit(solution)/shard_map/while
  212.0 9.0 %collective-permute-start = (bf16[4,8,32,128]{3,2,1,0:T(8,128)(2,1)S(1)}, bf16[4,8,32,128]{3,2,1,0:T(8,128)(2,1)S(1)}, u32[]{:S(2)}, u32[]{:S(2)}) collective-permute-start(bf16[4,8,32,128]{3,2,1,0:T(8,128)(2,1)S(1)} %broadcast_select_fusion.2), channel_id=1, source_target_pairs={{0,16},{16,32},{32,48},{48,64},{64,80},{80,96},{96,112},{112,128},... | collective-permute-start | bytes 786440 | tf_op jit(solution)/shard_map/while/body/eval_jaxpr/ppermute | solution.py:23
  222.9 9.7 %copy-start.1 = (bf16[4,8,128,128]{3,2,1,0:T(8,128)(2,1)S(1)}, bf16[4,8,128,128]{3,2,1,0:T(8,128)(2,1)}, u32[]{:S(2)}) copy-start(bf16[4,8,128,128]{3,2,1,0:T(8,128)(2,1)} %get-tuple-element.268) | copy-start | bytes 3145732 | tf_op jit(solution)/shard_map/while
  223.0 9.0 %collective-permute-start = (bf16[4,8,32,128]{3,2,1,0:T(8,128)(2,1)S(1)}, bf16[4,8,32,128]{3,2,1,0:T(8,128)(2,1)S(1)}, u32[]{:S(2)}, u32[]{:S(2)}) collective-permute-start(bf16[4,8,32,128]{3,2,1,0:T(8,128)(2,1)S(1)} %broadcast_select_fusion.2), channel_id=1, source_target_pairs={{0,16},{16,32},{32,48},{48,64},{64,80},{80,96},{96,112},{112,128},... | collective-permute-start | bytes 786440 | tf_op jit(solution)/shard_map/while/body/eval_jaxpr/ppermute | solution.py:23
  234.0 9.0 %collective-permute-start = (bf16[4,8,32,128]{3,2,1,0:T(8,128)(2,1)S(1)}, bf16[4,8,32,128]{3,2,1,0:T(8,128)(2,1)S(1)}, u32[]{:S(2)}, u32[]{:S(2)}) collective-permute-start(bf16[4,8,32,128]{3,2,1,0:T(8,128)(2,1)S(1)} %broadcast_select_fusion.2), channel_id=1, source_target_pairs={{0,16},{16,32},{32,48},{48,64},{64,80},{80,96},{96,112},{112,128},... | collective-permute-start | bytes 786440 | tf_op jit(solution)/shard_map/while/body/eval_jaxpr/ppermute | solution.py:23
  244.9 9.7 %copy-start.1 = (bf16[4,8,128,128]{3,2,1,0:T(8,128)(2,1)S(1)}, bf16[4,8,128,128]{3,2,1,0:T(8,128)(2,1)}, u32[]{:S(2)}) copy-start(bf16[4,8,128,128]{3,2,1,0:T(8,128)(2,1)} %get-tuple-element.268) | copy-start | bytes 3145732 | tf_op jit(solution)/shard_map/while
  245.0 9.0 %collective-permute-start = (bf16[4,8,32,128]{3,2,1,0:T(8,128)(2,1)S(1)}, bf16[4,8,32,128]{3,2,1,0:T(8,128)(2,1)S(1)}, u32[]{:S(2)}, u32[]{:S(2)}) collective-permute-start(bf16[4,8,32,128]{3,2,1,0:T(8,128)(2,1)S(1)} %broadcast_select_fusion.2), channel_id=1, source_target_pairs={{0,16},{16,32},{32,48},{48,64},{64,80},{80,96},{96,112},{112,128},... | collective-permute-start | bytes 786440 | tf_op jit(solution)/shard_map/while/body/eval_jaxpr/ppermute | solution.py:23
  255.9 9.7 %copy-start.1 = (bf16[4,8,128,128]{3,2,1,0:T(8,128)(2,1)S(1)}, bf16[4,8,128,128]{3,2,1,0:T(8,128)(2,1)}, u32[]{:S(2)}) copy-start(bf16[4,8,128,128]{3,2,1,0:T(8,128)(2,1)} %get-tuple-element.268) | copy-start | bytes 3145732 | tf_op jit(solution)/shard_map/while
  255.9 9.0 %collective-permute-start = (bf16[4,8,32,128]{3,2,1,0:T(8,128)(2,1)S(1)}, bf16[4,8,32,128]{3,2,1,0:T(8,128)(2,1)S(1)}, u32[]{:S(2)}, u32[]{:S(2)}) collective-permute-start(bf16[4,8,32,128]{3,2,1,0:T(8,128)(2,1)S(1)} %broadcast_select_fusion.2), channel_id=1, source_target_pairs={{0,16},{16,32},{32,48},{48,64},{64,80},{80,96},{96,112},{112,128},... | collective-permute-start | bytes 786440 | tf_op jit(solution)/shard_map/while/body/eval_jaxpr/ppermute | solution.py:23
  266.9 9.0 %collective-permute-start = (bf16[4,8,32,128]{3,2,1,0:T(8,128)(2,1)S(1)}, bf16[4,8,32,128]{3,2,1,0:T(8,128)(2,1)S(1)}, u32[]{:S(2)}, u32[]{:S(2)}) collective-permute-start(bf16[4,8,32,128]{3,2,1,0:T(8,128)(2,1)S(1)} %broadcast_select_fusion.2), channel_id=1, source_target_pairs={{0,16},{16,32},{32,48},{48,64},{64,80},{80,96},{96,112},{112,128},... | collective-permute-start | bytes 786440 | tf_op jit(solution)/shard_map/while/body/eval_jaxpr/ppermute | solution.py:23
  277.9 9.7 %copy-start.1 = (bf16[4,8,128,128]{3,2,1,0:T(8,128)(2,1)S(1)}, bf16[4,8,128,128]{3,2,1,0:T(8,128)(2,1)}, u32[]{:S(2)}) copy-start(bf16[4,8,128,128]{3,2,1,0:T(8,128)(2,1)} %get-tuple-element.268) | copy-start | bytes 3145732 | tf_op jit(solution)/shard_map/while
  277.9 9.0 %collective-permute-start = (bf16[4,8,32,128]{3,2,1,0:T(8,128)(2,1)S(1)}, bf16[4,8,32,128]{3,2,1,0:T(8,128)(2,1)S(1)}, u32[]{:S(2)}, u32[]{:S(2)}) collective-permute-start(bf16[4,8,32,128]{3,2,1,0:T(8,128)(2,1)S(1)} %broadcast_select_fusion.2), channel_id=1, source_target_pairs={{0,16},{16,32},{32,48},{48,64},{64,80},{80,96},{96,112},{112,128},... | collective-permute-start | bytes 786440 | tf_op jit(solution)/shard_map/while/body/eval_jaxpr/ppermute | solution.py:23
  288.9 9.7 %copy-start.1 = (bf16[4,8,128,128]{3,2,1,0:T(8,128)(2,1)S(1)}, bf16[4,8,128,128]{3,2,1,0:T(8,128)(2,1)}, u32[]{:S(2)}) copy-start(bf16[4,8,128,128]{3,2,1,0:T(8,128)(2,1)} %get-tuple-element.268) | copy-start | bytes 3145732 | tf_op jit(solution)/shard_map/while
  288.9 9.0 %collective-permute-start = (bf16[4,8,32,128]{3,2,1,0:T(8,128)(2,1)S(1)}, bf16[4,8,32,128]{3,2,1,0:T(8,128)(2,1)S(1)}, u32[]{:S(2)}, u32[]{:S(2)}) collective-permute-start(bf16[4,8,32,128]{3,2,1,0:T(8,128)(2,1)S(1)} %broadcast_select_fusion.2), channel_id=1, source_target_pairs={{0,16},{16,32},{32,48},{48,64},{64,80},{80,96},{96,112},{112,128},... | collective-permute-start | bytes 786440 | tf_op jit(solution)/shard_map/while/body/eval_jaxpr/ppermute | solution.py:23
  299.9 9.7 %copy-start.1 = (bf16[4,8,128,128]{3,2,1,0:T(8,128)(2,1)S(1)}, bf16[4,8,128,128]{3,2,1,0:T(8,128)(2,1)}, u32[]{:S(2)}) copy-start(bf16[4,8,128,128]{3,2,1,0:T(8,128)(2,1)} %get-tuple-element.268) | copy-start | bytes 3145732 | tf_op jit(solution)/shard_map/while
  299.9 9.0 %collective-permute-start = (bf16[4,8,32,128]{3,2,1,0:T(8,128)(2,1)S(1)}, bf16[4,8,32,128]{3,2,1,0:T(8,128)(2,1)S(1)}, u32[]{:S(2)}, u32[]{:S(2)}) collective-permute-start(bf16[4,8,32,128]{3,2,1,0:T(8,128)(2,1)S(1)} %broadcast_select_fusion.2), channel_id=1, source_target_pairs={{0,16},{16,32},{32,48},{48,64},{64,80},{80,96},{96,112},{112,128},... | collective-permute-start | bytes 786440 | tf_op jit(solution)/shard_map/while/body/eval_jaxpr/ppermute | solution.py:23
  310.8 9.7 %copy-start.1 = (bf16[4,8,128,128]{3,2,1,0:T(8,128)(2,1)S(1)}, bf16[4,8,128,128]{3,2,1,0:T(8,128)(2,1)}, u32[]{:S(2)}) copy-start(bf16[4,8,128,128]{3,2,1,0:T(8,128)(2,1)} %get-tuple-element.268) | copy-start | bytes 3145732 | tf_op jit(solution)/shard_map/while
  310.9 9.0 %collective-permute-start = (bf16[4,8,32,128]{3,2,1,0:T(8,128)(2,1)S(1)}, bf16[4,8,32,128]{3,2,1,0:T(8,128)(2,1)S(1)}, u32[]{:S(2)}, u32[]{:S(2)}) collective-permute-start(bf16[4,8,32,128]{3,2,1,0:T(8,128)(2,1)S(1)} %broadcast_select_fusion.2), channel_id=1, source_target_pairs={{0,16},{16,32},{32,48},{48,64},{64,80},{80,96},{96,112},{112,128},... | collective-permute-start | bytes 786440 | tf_op jit(solution)/shard_map/while/body/eval_jaxpr/ppermute | solution.py:23
  321.9 9.0 %collective-permute-start = (bf16[4,8,32,128]{3,2,1,0:T(8,128)(2,1)S(1)}, bf16[4,8,32,128]{3,2,1,0:T(8,128)(2,1)S(1)}, u32[]{:S(2)}, u32[]{:S(2)}) collective-permute-start(bf16[4,8,32,128]{3,2,1,0:T(8,128)(2,1)S(1)} %broadcast_select_fusion.2), channel_id=1, source_target_pairs={{0,16},{16,32},{32,48},{48,64},{64,80},{80,96},{96,112},{112,128},... | collective-permute-start | bytes 786440 | tf_op jit(solution)/shard_map/while/body/eval_jaxpr/ppermute | solution.py:23
  332.8 9.7 %copy-start.1 = (bf16[4,8,128,128]{3,2,1,0:T(8,128)(2,1)S(1)}, bf16[4,8,128,128]{3,2,1,0:T(8,128)(2,1)}, u32[]{:S(2)}) copy-start(bf16[4,8,128,128]{3,2,1,0:T(8,128)(2,1)} %get-tuple-element.268) | copy-start | bytes 3145732 | tf_op jit(solution)/shard_map/while
  332.9 9.0 %collective-permute-start = (bf16[4,8,32,128]{3,2,1,0:T(8,128)(2,1)S(1)}, bf16[4,8,32,128]{3,2,1,0:T(8,128)(2,1)S(1)}, u32[]{:S(2)}, u32[]{:S(2)}) collective-permute-start(bf16[4,8,32,128]{3,2,1,0:T(8,128)(2,1)S(1)} %broadcast_select_fusion.2), channel_id=1, source_target_pairs={{0,16},{16,32},{32,48},{48,64},{64,80},{80,96},{96,112},{112,128},... | collective-permute-start | bytes 786440 | tf_op jit(solution)/shard_map/while/body/eval_jaxpr/ppermute | solution.py:23
  343.8 9.7 %copy-start.1 = (bf16[4,8,128,128]{3,2,1,0:T(8,128)(2,1)S(1)}, bf16[4,8,128,128]{3,2,1,0:T(8,128)(2,1)}, u32[]{:S(2)}) copy-start(bf16[4,8,128,128]{3,2,1,0:T(8,128)(2,1)} %get-tuple-element.268) | copy-start | bytes 3145732 | tf_op jit(solution)/shard_map/while
  343.9 9.0 %collective-permute-start = (bf16[4,8,32,128]{3,2,1,0:T(8,128)(2,1)S(1)}, bf16[4,8,32,128]{3,2,1,0:T(8,128)(2,1)S(1)}, u32[]{:S(2)}, u32[]{:S(2)}) collective-permute-start(bf16[4,8,32,128]{3,2,1,0:T(8,128)(2,1)S(1)} %broadcast_select_fusion.2), channel_id=1, source_target_pairs={{0,16},{16,32},{32,48},{48,64},{64,80},{80,96},{96,112},{112,128},... | collective-permute-start | bytes 786440 | tf_op jit(solution)/shard_map/while/body/eval_jaxpr/ppermute | solution.py:23
  354.8 9.0 %collective-permute-start = (bf16[4,8,32,128]{3,2,1,0:T(8,128)(2,1)S(1)}, bf16[4,8,32,128]{3,2,1,0:T(8,128)(2,1)S(1)}, u32[]{:S(2)}, u32[]{:S(2)}) collective-permute-start(bf16[4,8,32,128]{3,2,1,0:T(8,128)(2,1)S(1)} %broadcast_select_fusion.2), channel_id=1, source_target_pairs={{0,16},{16,32},{32,48},{48,64},{64,80},{80,96},{96,112},{112,128},... | collective-permute-start | bytes 786440 | tf_op jit(solution)/shard_map/while/body/eval_jaxpr/ppermute | solution.py:23
  (7 other events, 50.1 us)
where the time goes:
time: 368 us; the launch traced here: 367 us
  starting transfers between devices  190 us (52%)
  waiting for transfers between devices  85.9 us (23%)
  matrix products  39.7 us (11%)
  local copies, waits for them, and re-layouts  26.2 us (7%)
  other arithmetic  23.2 us (6%)
    ppermute x32, starting transfers between devices, shifted(): lax.ppermute(value, axis, [(source, source + steps) for source in range(l...  185 us
    ppermute x32, waiting for transfers between devices, shifted(): lax.ppermute(value, axis, [(source, source + steps) for source in range(l...  80.9 us
    dot_general x32, matrix products, sweep_block(): jnp.einsum('mkvj,mkij->mkvi', remainder, part_inverse, preferred_element_...  39.7 us
    gather x64, local copies, waits for them, and re-layouts, sweep_block(): jnp.take_along_axis(inflow, part_neighbour[:, :, None, None], axis=1)  23.6 us
    broadcast_in_dim x32, other arithmetic, sweep_block(): return jnp.where(active_slots, updated, jnp.zeros_like(updated))  20.9 us
  transfers between devices with their start and end apart: 34, of which 33 were waited for; matrix products, arithmetic and copies ran while one was open for 7% of the time, Pallas kernels for 0%

commit v1 on v0

v1 whole, which is shorter than its diff:
```python
import functools

import jax
import jax.numpy as jnp
from jax import lax
from jax.experimental import pallas as pl
from jax.experimental.pallas import tpu as pltpu
from jax.sharding import PartitionSpec as P

F32 = jnp.float32
BF16 = jnp.bfloat16
SMEM = pl.BlockSpec(memory_space=pltpu.SMEM)
VMEM = pl.BlockSpec(memory_space=pltpu.VMEM)
ANY = pl.BlockSpec(memory_space=pl.ANY)
PAD = 16


def pin(x):
    return pltpu.with_memory_space_constraint(x, pltpu.VMEM)


def in_vmem(shape, dtype=BF16):
    return pltpu.VMEM(shape, dtype)


def params(mib=16):
    return pltpu.CompilerParams(vmem_limit_bytes=mib * 1024 * 1024)


def cost(flops, size):
    return pl.CostEstimate(flops=flops, bytes_accessed=size, transcendentals=0)


def dot(a, b, dims=((1,), (0,))):
    return lax.dot_general(a, b, (dims, ((), ())), preferred_element_type=F32)


def blocks_kernel(where, index, u_hbm, d_hbm, keep, send, u, d, u_sem, d_sem):
    core, width = where[0], where[1]
    slabs, slots, nb, _ = u.shape
    nv = (keep.shape[1] - PAD) // slots - nb
    copies = []
    for m in range(slabs):
        a = pltpu.make_async_copy(u_hbm.at[0, m], u.at[m], u_sem.at[m])
        b = pltpu.make_async_copy(d_hbm.at[0, m], d.at[m], d_sem.at[m])
        a.start()
        b.start()
        copies.append((a, b))
    for a, b in copies:
        a.wait()
        b.wait()
    half = slabs // 2
    rows = lax.broadcasted_iota(jnp.int32, (PAD, nb), 0)

    def body(j, _):
        for out, first in ((send, (1 - core) * half), (keep, core * half)):
            m = first + j
            tile = jnp.zeros((PAD, nb), F32)
            for k in range(slots):
                b = -dot(u[m, k], d[m, k], ((0,), (1,)))
                b = jnp.where(k < width, b, 0.0)
                out[j, pl.ds(k * (nv + nb) + nv, nb), :] = b.astype(BF16)
                tile = tile + jnp.where(rows == k, index[0, m, k].astype(F32), 0.0)
            out[j, pl.ds(slots * (nv + nb), PAD), :] = tile.astype(BF16)
        return 0

    lax.fori_loop(0, half, body, 0)


def vectors_kernel(where, rhs_hbm, prev_hbm, below, above, lower_hbm, upper_hbm, d_hbm, keep_in, send_in, keep, send,
                   rhs, prev, lower, upper, d, sem):
    core, width = where[0], where[1]
    slabs, slots, nv, nb = rhs.shape
    half = slabs // 2
    copies = [
        pltpu.make_async_copy(rhs_hbm.at[0], rhs, sem.at[0]),
        pltpu.make_async_copy(prev_hbm.at[0], prev.at[pl.ds(1, slabs)], sem.at[1]),
        pltpu.make_async_copy(lower_hbm.at[0], lower, sem.at[2]),
        pltpu.make_async_copy(upper_hbm.at[0], upper, sem.at[3]),
        pltpu.make_async_copy(d_hbm.at[0], d, sem.at[4]),
    ]
    for c in copies:
        c.start()
    prev[0] = below[0]
    prev[slabs + 1] = above[0]
    for c in copies:
        c.wait()

    def body(j, _):
        for out, first in ((send, (1 - core) * half), (keep, core * half)):
            m = first + j
            lo, up = lower[m], upper[m]
            for k in range(slots):
                side = lo[k : k + 1, :] * prev[m, k].astype(F32) + up[k : k + 1, :] * prev[m + 2, k].astype(F32)
                local = (rhs[m, k].astype(F32) - side).astype(BF16)
                c = dot(local, d[m, k], ((1,), (1,)))
                c = jnp.where(k < width, c, 0.0)
                out[j, pl.ds(k * (nv + nb), nv), :] = c.astype(BF16)
        return 0

    lax.fori_loop(0, half, body, 0)


def slot_scalars(tile, scratch, slots):
    scratch[...] = tile.astype(jnp.int32)
    return [scratch[k, 0] for k in range(slots)]


def compose(lo, hi, out, scratch, slots, nv, nb):
    step = nv + nb
    tile_lo = lo[pl.ds(slots * step, PAD), :].astype(F32)
    tile_hi = hi[pl.ds(slots * step, PAD), :].astype(F32)
    picks = slot_scalars(tile_hi, scratch, slots)
    tile = jnp.zeros_like(tile_hi)
    for n in range(slots):
        tile = tile + jnp.where(tile_hi == n, tile_lo[n : n + 1, :], 0.0)
    out[pl.ds(slots * step, PAD), :] = tile.astype(BF16)
    for k in range(slots):
        x = lo[pl.ds(pl.multiple_of(picks[k] * step, 16), step), :]
        y = dot(x, hi[pl.ds(k * step + nv, nb), :])
        c = hi[pl.ds(k * step, nv), :].astype(F32)
        out[pl.ds(k * step, nv), :] = (y[:nv] + c).astype(BF16)
        out[pl.ds(k * step + nv, nb), :] = y[nv:].astype(BF16)


def pair_kernel(slots, nv, where, keep, recv, out_keep, out_send, scratch):
    core, chip = where[0], where[2]
    for here, lo, hi in ((0, keep, recv), (1, recv, keep)):
        @pl.when(core == here)
        def _():
            compose(lo.at[1 - chip], hi.at[1 - chip], out_send, scratch, slots, nv, lo.shape[-1])
            compose(lo.at[chip], hi.at[chip], out_keep, scratch, slots, nv, lo.shape[-1])


def group_kernel(slots, nv, where, keep, recv, out, start, scratch):
    chip = where[2]
    nb = out.shape[-1]
    for here, lo, hi in ((0, keep, recv), (1, recv, keep)):
        @pl.when(chip == here)
        def _():
            compose(lo, hi, out, scratch, slots, nv, nb)
    for k in range(slots):
        start[k] = out[pl.ds(k * (nv + nb), nv), :]


def apply_map(x, m, out, scratch, slots, nv, nb):
    step = nv + nb
    picks = slot_scalars(m[pl.ds(slots * step, PAD), :].astype(F32), scratch, slots)
    for k in range(slots):
        y = dot(x[picks[k]], m[pl.ds(k * step + nv, nb), :])
        out[k] = (y + m[pl.ds(k * step, nv), :].astype(F32)).astype(BF16)


def hop_kernel(slots, nv, recv, group, inflow, out, inflow_out, scratch):
    apply_map(recv, group, out, scratch, slots, nv, group.shape[-1])
    inflow_out[...] = inflow[...] + recv[...]


def share_kernel(slots, nv, where, inflow, keep, recv, group, out, scratch):
    chip = where[2]
    nb = group.shape[-1]
    out[0] = inflow[...]
    for here, lo in ((0, keep), (1, recv)):
        @pl.when(chip == here)
        def _():
            apply_map(inflow, lo, out.at[1], scratch, slots, nv, nb)
    apply_map(inflow, group, out.at[2], scratch, slots, nv, nb)


def finish_kernel(slots, nv, where, index, shared, keep, send, out):
    core, chip = where[0], where[2]
    slabs = out.shape[1]
    half = slabs // 2
    nb = out.shape[-1]
    step = nv + nb
    for m in range(slabs):
        owner = 2 * (m % 2) + m // 2

        @pl.when(core == 1)
        def _():
            out[0, m] = shared[owner, 1 + chip]

        @pl.when(core == 0)
        def _():
            maps = keep if m < half else send
            for k in range(slots):
                x = shared[owner, chip, index[0, m, k]]
                y = dot(x, maps[m % half, pl.ds(k * step + nv, nb), :])
                out[0, m, k] = (y + maps[m % half, pl.ds(k * step, nv), :].astype(F32)).astype(BF16)


def local(rhs, previous, inverse_blocks, upstream_blocks, lower_gain, upper_gain, widths, upstream_index):
    _, slabs, slots, nv, nb = rhs.shape
    half = slabs // 2
    sections, peers = lax.axis_size("stream"), lax.axis_size("span")
    groups = sections // 4
    rows = slots * (nv + nb) + PAD
    position = lax.axis_index("stream")
    where = jnp.stack([position % 2, widths[0], (position // 2) % 2]).astype(jnp.int32)

    up = [(i, i + 1) for i in range(peers - 1)]
    down = [(j, i) for i, j in up]
    below = lax.ppermute(previous[0, slabs - 1 :], "span", up)
    above = lax.ppermute(previous[0, :1], "span", down)

    pair_shape = in_vmem((half, rows, nb))
    one_shape = in_vmem((rows, nb))
    vec_shape = in_vmem((slots, nv, nb))
    index_scratch = pltpu.VMEM((PAD, nb), jnp.int32)

    keep, send = pl.pallas_call(
        blocks_kernel,
        out_shape=(pair_shape, pair_shape),
        in_specs=[SMEM, SMEM, ANY, ANY],
        out_specs=(VMEM, VMEM),
        scratch_shapes=[
            pltpu.VMEM((slabs, slots, nb, nb), BF16),
            pltpu.VMEM((slabs, slots, nb, nb), BF16),
            pltpu.SemaphoreType.DMA((slabs,)),
            pltpu.SemaphoreType.DMA((slabs,)),
        ],
        compiler_params=params(),
        cost_estimate=cost(2 * slabs * slots * nb**3, 4 * slabs * slots * nb * nb),
        name="section_blocks",
    )(where, upstream_index, upstream_blocks, inverse_blocks)
    keep, send = pl.pallas_call(
        vectors_kernel,
        out_shape=(pair_shape, pair_shape),
        in_specs=[SMEM, ANY, ANY, VMEM, VMEM, ANY, ANY, ANY, VMEM, VMEM],
        out_specs=(VMEM, VMEM),
        scratch_shapes=[
            pltpu.VMEM((slabs, slots, nv, nb), BF16),
            pltpu.VMEM((slabs + 2, slots, nv, nb), BF16),
            pltpu.VMEM((slabs, slots, nb), F32),
            pltpu.VMEM((slabs, slots, nb), F32),
            pltpu.VMEM((slabs, slots, nb, nb), BF16),
            pltpu.SemaphoreType.DMA((5,)),
        ],
        input_output_aliases={8: 0, 9: 1},
        compiler_params=params(),
        name="section_vectors",
    )(where, rhs, previous, pin(below), pin(above), lower_gain, upper_gain, inverse_blocks, pin(keep), pin(send))

    recv = lax.ppermute(send, "stream", [(i, i ^ 1) for i in range(sections)])
    pair_keep, pair_send = pl.pallas_call(
        functools.partial(pair_kernel, slots, nv),
        out_shape=(one_shape, one_shape),
        in_specs=[SMEM, VMEM, VMEM],
        out_specs=(VMEM, VMEM),
        scratch_shapes=[index_scratch],
        compiler_params=params(),
        name="compose_chip",
    )(where, pin(keep), pin(recv))

    pair_recv = lax.ppermute(pair_send, "stream", [(i, i ^ 2) for i in range(sections)])
    group, state = pl.pallas_call(
        functools.partial(group_kernel, slots, nv),
        out_shape=(one_shape, vec_shape),
        in_specs=[SMEM, VMEM, VMEM],
        out_specs=(VMEM, VMEM),
        scratch_shapes=[index_scratch],
        compiler_params=params(),
        name="compose_group",
    )(where, pin(pair_keep), pin(pair_recv))

    hop = pl.pallas_call(
        functools.partial(hop_kernel, slots, nv),
        out_shape=(vec_shape, vec_shape),
        in_specs=[VMEM, VMEM, VMEM],
        out_specs=(VMEM, VMEM),
        scratch_shapes=[index_scratch],
        compiler_params=params(),
        name="hop",
    )
    inflow = jnp.zeros((slots, nv, nb), BF16)
    for g in range(1, groups):
        arrived = lax.ppermute(state, "stream", [(4 * g - 4 + r, 4 * g + r) for r in range(4)])
        state, inflow = hop(pin(arrived), pin(group), pin(inflow))

    shares = pl.pallas_call(
        functools.partial(share_kernel, slots, nv),
        out_shape=in_vmem((3, slots, nv, nb)),
        in_specs=[SMEM, VMEM, VMEM, VMEM, VMEM],
        out_specs=VMEM,
        scratch_shapes=[index_scratch],
        compiler_params=params(),
        name="share",
    )(where, pin(inflow), pin(pair_keep), pin(pair_recv), pin(group))
    shared = lax.all_gather(
        shares, "stream", axis_index_groups=[[4 * g + r for r in range(4)] for g in range(groups)]
    )
    return pl.pallas_call(
        functools.partial(finish_kernel, slots, nv),
        out_shape=jax.ShapeDtypeStruct(rhs.shape, BF16),
        in_specs=[SMEM, SMEM, VMEM, VMEM, VMEM],
        out_specs=VMEM,
        compiler_params=params(),
        name="finish",
    )(where, upstream_index, shared, pin(keep), pin(send))


def solution(mesh):
    in_specs = (
        P("stream", "span", None, None, None),
        P("stream", "span", None, None, None),
        P("stream", "span", None, None, None),
        P("stream", "span", None, None, None),
        P("stream", "span", None, None),
        P("stream", "span", None, None),
        P("stream"),
        P("stream", "span", None),
    )
    out_specs = P("stream", "span", None, None, None)
    return jax.shard_map(local, mesh=mesh, in_specs=in_specs, out_specs=out_specs, check_vma=False)
```

time: 368 us -> 81.7 us (0.22)
  the two profiles are of different devices: /device:TPU:103 before, /device:TPU:464 now
where the time goes in v1:
time: 81.7 us; the launch traced here: 81.2 us
  waiting for transfers between devices  38.4 us (47%)
  starting transfers between devices  18.1 us (22%)
  Pallas kernels  10.2 us (12%)
  blocking collectives  9.61 us (12%)
  local copies, waits for them, and re-layouts  3.96 us (5%)
  between operations  0.94 us (1%)
    ppermute x7, waiting for transfers between devices, local(): lax.ppermute(state, 'stream', [(4 * g - 4 + r, 4 * g + r) for r in range(...  27.5 us
    all_gather x1, blocking collectives, local(): lax.all_gather(shares, 'stream', axis_index_groups=[[4 * g + r for r in r...  9.61 us
    ppermute x1, waiting for transfers between devices, local(): lax.ppermute(pair_send, 'stream', [(i, i ^ 2) for i in range(sections)])  8.8 us
    ppermute x7, starting transfers between devices, local(): lax.ppermute(state, 'stream', [(4 * g - 4 + r, 4 * g + r) for r in range(...  5.27 us
    ppermute x1, starting transfers between devices, local(): above = lax.ppermute(previous[0, :1], 'span', down)  4.55 us
    ppermute x1, starting transfers between devices, local(): below = lax.ppermute(previous[0, slabs - 1:], 'span', up)  3.4 us
    unnamed x16, local copies, waits for them, and re-layouts  3.07 us
    ppermute x1, starting transfers between devices, local(): lax.ppermute(pair_send, 'stream', [(i, i ^ 2) for i in range(sections)])  2.93 us
  transfers between devices with their start and end apart: 11, of which 3 were waited for; matrix products, arithmetic and copies ran while one was open for 0% of the time, Pallas kernels for 2%

profile of v1, /device:TPU:464, one launch (start us, length us, event | category | flops | bytes accessed | tf_op | source)
XLA Modules:
  0.0 81.2 jit_solution(1062010906888778122)
XLA Ops:
  0.0 0.9 %slice_bitcast_fusion = (bf16[1,8,32,128]{3,2,1,0:T(8,128)(2,1)S(1)}, bf16[1,8,32,128]{3,2,1,0:T(8,128)(2,1)S(1)}) fusion(bf16[1,4,8,32,128]{4,3,2,1,0:T(8,128)(2,1)} %prev_hbm.1), kind=kLoop, calls=%fused_computation | loop fusion | bytes 262144 | tf_op jit(solution)/shard_map/squeeze | solution.py:204
  0.9 3.4 %collective-permute-start = (bf16[1,8,32,128]{3,2,1,0:T(8,128)(2,1)S(1)}, bf16[1,8,32,128]{3,2,1,0:T(8,128)(2,1)S(1)}, u32[]{:S(2)}, u32[]{:S(2)}) collective-permute-start(bf16[1,8,32,128]{3,2,1,0:T(8,128)(2,1)S(1)} %get-tuple-element.48), channel_id=1, source_target_pairs={{0,1},{1,2},{2,3},{3,4},{4,5},{5,6},{6,7},{7,8},{8,9},{9,10},{10,1... | collective-permute-start | bytes 196616 | tf_op jit(solution)/shard_map/ppermute | solution.py:203
  4.3 4.6 %collective-permute-start.1 = (bf16[1,8,32,128]{3,2,1,0:T(8,128)(2,1)S(1)}, bf16[1,8,32,128]{3,2,1,0:T(8,128)(2,1)S(1)}, u32[]{:S(2)}, u32[]{:S(2)}) collective-permute-start(bf16[1,8,32,128]{3,2,1,0:T(8,128)(2,1)S(1)} %get-tuple-element.47), channel_id=1, source_target_pairs={{1,0},{2,1},{3,2},{4,3},{5,4},{6,5},{7,6},{8,7},{9,8},{10,9},{11,1... | collective-permute-start | bytes 196616 | tf_op jit(solution)/shard_map/ppermute | solution.py:204
  9.5 0.0 copy-start.7
  9.5 0.1 pad_add_fusion.where
  9.6 0.6 copy-done.7
  10.2 0.0 copy-start
  10.2 1.2 %copy-done = bf16[1,4,8,128,128]{4,3,2,1,0:T(8,128)(2,1)S(1)} copy-done((bf16[1,4,8,128,128]{4,3,2,1,0:T(8,128)(2,1)S(1)}, bf16[1,4,8,128,128]{4,3,2,1,0:T(8,128)(2,1)}, u32[]{:S(2)}) %copy-start) | copy-done | bytes 1048600
  11.4 0.0 copy-start.2
  11.4 1.2 %copy-done.2 = bf16[1,4,8,128,128]{4,3,2,1,0:T(8,128)(2,1)S(1)} copy-done((bf16[1,4,8,128,128]{4,3,2,1,0:T(8,128)(2,1)S(1)}, bf16[1,4,8,128,128]{4,3,2,1,0:T(8,128)(2,1)}, u32[]{:S(2)}) %copy-start.2) | copy-done | bytes 1048600
  12.7 0.0 copy-start.1
  12.7 0.0 copy-start.3
  12.7 0.0 copy-start.4
  12.7 0.0 copy-start.5
  12.7 0.0 copy-start.6
  12.7 1.8 %section_blocks.1 = (bf16[2,1296,128]{2,1,0:T(8,128)(2,1)S(1)}, bf16[2,1296,128]{2,1,0:T(8,128)(2,1)S(1)}) custom-call(s32[3]{0:T(128)S(1)} %pad_add_fusion.where, s32[1,4,8]{2,1,0:T(4,128)S(1)} %copy-done.7, bf16[1,4,8,128,128]{4,3,2,1,0:T(8,128)(2,1)S(1)} %copy-done.2, bf16[1,4,8,128,128]{4,3,2,1,0:T(8,128)(2,1)S(1)} %copy-done), custom_call_target="tpu_custom_call" | custom-call | flops 134217728 | bytes 2097152 | tf_op jit(solution)/shard_map/section_blocks/pallas_call | solution.py:211
  14.5 0.0 collective-permute-done.below
  14.5 0.0 collective-permute-done.1.above
  14.5 0.0 copy-done.1
  14.5 0.0 copy-done.3
  14.6 0.0 copy-done.4
  14.6 0.0 copy-done.5
  14.6 0.0 copy-done.6
  14.6 1.5 %section_vectors.1 = (bf16[2,1296,128]{2,1,0:T(8,128)(2,1)S(1)}, bf16[2,1296,128]{2,1,0:T(8,128)(2,1)S(1)}) custom-call(s32[3]{0:T(128)S(1)} %pad_add_fusion.where, bf16[1,4,8,32,128]{4,3,2,1,0:T(8,128)(2,1)S(1)} %copy-done.4, bf16[1,4,8,32,128]{4,3,2,1,0:T(8,128)(2,1)S(1)} %copy-done.3, ...), custom_call_target="tpu_custom_call", output_to_operand_aliasing={{0}: (8, {}), {1}: (9, {})} | custom-call | tf_op jit(solution)/shard_map/section_vectors/pallas_call | solution.py:226
  16.1 1.9 %collective-permute-start.2 = (bf16[2,1296,128]{2,1,0:T(8,128)(2,1)S(1)}, bf16[2,1296,128]{2,1,0:T(8,128)(2,1)S(1)}, u32[]{:S(2)}, u32[]{:S(2)}) collective-permute-start(bf16[2,1296,128]{2,1,0:T(8,128)(2,1)S(1)} %get-tuple-element.29.send), channel_id=1, source_target_pairs={{0,16},{16,0},{32,48},{48,32},{64,80},{80,64},{96,112},{112,96},{1... | collective-permute-start | bytes 1990664 | tf_op jit(solution)/shard_map/ppermute | solution.py:244
  18.1 2.1 %collective-permute-done.2.recv = bf16[2,1296,128]{2,1,0:T(8,128)(2,1)S(1)} collective-permute-done((bf16[2,1296,128]{2,1,0:T(8,128)(2,1)S(1)}, bf16[2,1296,128]{2,1,0:T(8,128)(2,1)S(1)}, u32[]{:S(2)}, u32[]{:S(2)}) %collective-permute-start.2) | collective-permute-done | bytes 663584 | tf_op jit(solution)/shard_map/ppermute | solution.py:244
  20.1 0.9 %compose_chip.1 = (bf16[1296,128]{1,0:T(8,128)(2,1)S(1)}, bf16[1296,128]{1,0:T(8,128)(2,1)S(1)}) custom-call(s32[3]{0:T(128)S(1)} %pad_add_fusion.where, bf16[2,1296,128]{2,1,0:T(8,128)(2,1)S(1)} %get-tuple-element.28.keep, bf16[2,1296,128]{2,1,0:T(8,128)(2,1)S(1)} %collective-permute-done.2.recv), custom_call_target="tpu_custom_call" | custom-call | tf_op jit(solution)/shard_map/compose_chip/pallas_call | solution.py:245
  21.1 2.9 %collective-permute-start.3 = (bf16[1296,128]{1,0:T(8,128)(2,1)S(1)}, bf16[1296,128]{1,0:T(8,128)(2,1)S(1)}, u32[]{:S(2)}, u32[]{:S(2)}) collective-permute-start(bf16[1296,128]{1,0:T(8,128)(2,1)S(1)} %get-tuple-element.31), channel_id=1, source_target_pairs={{0,32},{16,48},{32,0},{48,16},{64,96},{80,112},{96,64},{112,80},{1... | collective-permute-start | bytes 995336 | tf_op jit(solution)/shard_map/ppermute | solution.py:255
  24.0 8.8 %collective-permute-done.3.recv = bf16[1296,128]{1,0:T(8,128)(2,1)S(1)} collective-permute-done((bf16[1296,128]{1,0:T(8,128)(2,1)S(1)}, bf16[1296,128]{1,0:T(8,128)(2,1)S(1)}, u32[]{:S(2)}, u32[]{:S(2)}) %collective-permute-start.3) | collective-permute-done | bytes 331808 | tf_op jit(solution)/shard_map/ppermute | solution.py:255
  32.8 0.8 %compose_group.1 = (bf16[1296,128]{1,0:T(8,128)(2,1)S(1)}, bf16[8,32,128]{2,1,0:T(8,128)(2,1)S(1)}) custom-call(s32[3]{0:T(128)S(1)} %pad_add_fusion.where, bf16[1296,128]{1,0:T(8,128)(2,1)S(1)} %get-tuple-element.30.keep, bf16[1296,128]{1,0:T(8,128)(2,1)S(1)} %collective-permute-done.3.recv), custom_call_target="tpu_custom_call" | custom-call | tf_op jit(solution)/shard_map/compose_group/pallas_call | solution.py:256
  33.6 0.7 collective-permute-start.4
  34.3 0.0 collective-permute-done.4.recv
  34.3 0.2 hop.7
  34.5 0.7 collective-permute-start.5
  35.2 0.0 collective-permute-done.5.recv
  35.2 0.2 hop.8
  35.4 0.7 collective-permute-start.6
  36.1 0.0 collective-permute-done.6.recv
  36.1 0.2 hop.9
  36.3 0.7 collective-permute-start.7
  37.0 0.0 collective-permute-done.7.recv
  37.0 0.2 hop.10
  37.2 0.7 collective-permute-start.8
  37.9 0.0 collective-permute-done.8.recv
  37.9 0.2 hop.11
  38.1 0.7 collective-permute-start.9
  38.8 0.0 collective-permute-done.9.recv
  38.8 0.2 hop.12
  39.0 1.3 %collective-permute-start.10 = (bf16[8,32,128]{2,1,0:T(8,128)(2,1)S(1)}, bf16[8,32,128]{2,1,0:T(8,128)(2,1)S(1)}, u32[]{:S(2)}, u32[]{:S(2)}) collective-permute-start(bf16[8,32,128]{2,1,0:T(8,128)(2,1)S(1)} %get-tuple-element.44), channel_id=1, source_target_pairs={{384,448},{400,464},{416,480},{432,496},{385,449},{401,465},{417,4... | collective-permute-start | bytes 196616 | tf_op jit(solution)/shard_map/ppermute | solution.py:277
  40.3 27.5 %collective-permute-done.10.recv = bf16[8,32,128]{2,1,0:T(8,128)(2,1)S(1)} collective-permute-done((bf16[8,32,128]{2,1,0:T(8,128)(2,1)S(1)}, bf16[8,32,128]{2,1,0:T(8,128)(2,1)S(1)}, u32[]{:S(2)}, u32[]{:S(2)}) %collective-permute-start.10) | collective-permute-done | bytes 65568 | tf_op jit(solution)/shard_map/ppermute | solution.py:277
  67.8 0.8 %hop.13 = (bf16[8,32,128]{2,1,0:T(8,128)(2,1)}, bf16[8,32,128]{2,1,0:T(8,128)(2,1)S(1)}) custom-call(bf16[8,32,128]{2,1,0:T(8,128)(2,1)S(1)} %collective-permute-done.10.recv, bf16[1296,128]{1,0:T(8,128)(2,1)S(1)} %get-tuple-element.33.group, bf16[8,32,128]{2,1,0:T(8,128)(2,1)S(1)} %get-tuple-element.45.inflow), custom_call_target="tpu_custom_call" | custom-call | tf_op jit(solution)/shard_map/hop/pallas_call | solution.py:278
  68.6 1.0 %share.1 = bf16[3,8,32,128]{3,2,1,0:T(8,128)(2,1)S(1)} custom-call(s32[3]{0:T(128)S(1)} %pad_add_fusion.where, bf16[8,32,128]{2,1,0:T(8,128)(2,1)S(1)} %get-tuple-element.46.inflow, bf16[1296,128]{1,0:T(8,128)(2,1)S(1)} %get-tuple-element.30.keep, bf16[1296,128]{1,0:T(8,128)(2,1)S(1)} %collective-permute-done.3.recv, ...), custom_call_target="tpu_custom_call" | custom-call | tf_op jit(solution)/shard_map/share/pallas_call | solution.py:280
  69.6 9.6 %all-gather = bf16[12,8,32,128]{3,2,1,0:T(8,128)(2,1)S(1)} all-gather(bf16[3,8,32,128]{3,2,1,0:T(8,128)(2,1)S(1)} %share.1), channel_id=2, replica_groups={{0,16,32,48},{64,80,96,112},{128,144,160,176},{192,208,224,240},{256,27..., dimensions={0}, use_global_device_ids=true | all-gather | bytes 983040 | tf_op jit(solution)/shard_map/all_gather | solution.py:289
  79.2 2.0 %finish.1 = bf16[1,4,8,32,128]{4,3,2,1,0:T(8,128)(2,1)} custom-call(s32[3]{0:T(128)S(1)} %pad_add_fusion.where, s32[1,4,8]{2,1,0:T(4,128)S(1)} %copy-done.7, bf16[4,3,8,32,128]{4,3,2,1,0:T(8,128)(2,1)S(1)} %bitcast.7, bf16[2,1296,128]{2,1,0:T(8,128)(2,1)S(1)} %get-tuple-element.28.keep, bf16[2,1296,128]{2,1,0:T(8,128)(2,1)S(1)} %get-tuple-element.29.send), custom_call_target="tpu_custom_call" | custom-call | tf_op jit(solution)/shard_map/finish/pallas_call | solution.py:292
  (1 shorter events, 0.0 us)
Async XLA Ops:
  0.9 13.6 %collective-permute-start = (bf16[1,8,32,128]{3,2,1,0:T(8,128)(2,1)S(1)}, bf16[1,8,32,128]{3,2,1,0:T(8,128)(2,1)S(1)}, u32[]{:S(2)}, u32[]{:S(2)}) collective-permute-start(bf16[1,8,32,128]{3,2,1,0:T(8,128)(2,1)S(1)} %get-tuple-element.48), channel_id=1, source_target_pairs={{0,1},{1,2},{2,3},{3,4},{4,5},{5,6},{6,7},{7,8},{8,9},{9,10},{10,1... | collective-permute-start | bytes 196616 | tf_op jit(solution)/shard_map/ppermute | solution.py:203
  4.3 10.2 %collective-permute-start.1 = (bf16[1,8,32,128]{3,2,1,0:T(8,128)(2,1)S(1)}, bf16[1,8,32,128]{3,2,1,0:T(8,128)(2,1)S(1)}, u32[]{:S(2)}, u32[]{:S(2)}) collective-permute-start(bf16[1,8,32,128]{3,2,1,0:T(8,128)(2,1)S(1)} %get-tuple-element.47), channel_id=1, source_target_pairs={{1,0},{2,1},{3,2},{4,3},{5,4},{6,5},{7,6},{8,7},{9,8},{10,9},{11,1... | collective-permute-start | bytes 196616 | tf_op jit(solution)/shard_map/ppermute | solution.py:204
  9.5 0.7 copy-start.7
  10.2 1.2 %copy-start = (bf16[1,4,8,128,128]{4,3,2,1,0:T(8,128)(2,1)S(1)}, bf16[1,4,8,128,128]{4,3,2,1,0:T(8,128)(2,1)}, u32[]{:S(2)}) copy-start(bf16[1,4,8,128,128]{4,3,2,1,0:T(8,128)(2,1)} %d_hbm.3) | copy-start | bytes 3145732
  11.4 1.2 %copy-start.2 = (bf16[1,4,8,128,128]{4,3,2,1,0:T(8,128)(2,1)S(1)}, bf16[1,4,8,128,128]{4,3,2,1,0:T(8,128)(2,1)}, u32[]{:S(2)}) copy-start(bf16[1,4,8,128,128]{4,3,2,1,0:T(8,128)(2,1)} %u_hbm.1) | copy-start | bytes 3145732
  12.7 1.9 %copy-start.1 = (bf16[1,4,8,128,128]{4,3,2,1,0:T(8,128)(2,1)S(1)}, bf16[1,4,8,128,128]{4,3,2,1,0:T(8,128)(2,1)}, u32[]{:S(2)}) copy-start(bf16[1,4,8,128,128]{4,3,2,1,0:T(8,128)(2,1)} %d_hbm.3) | copy-start | bytes 3145732
  12.7 1.9 %copy-start.3 = (bf16[1,4,8,32,128]{4,3,2,1,0:T(8,128)(2,1)S(1)}, bf16[1,4,8,32,128]{4,3,2,1,0:T(8,128)(2,1)}, u32[]{:S(2)}) copy-start(bf16[1,4,8,32,128]{4,3,2,1,0:T(8,128)(2,1)} %prev_hbm.1) | copy-start | bytes 786436
  12.7 1.9 %copy-start.4 = (bf16[1,4,8,32,128]{4,3,2,1,0:T(8,128)(2,1)S(1)}, bf16[1,4,8,32,128]{4,3,2,1,0:T(8,128)(2,1)}, u32[]{:S(2)}) copy-start(bf16[1,4,8,32,128]{4,3,2,1,0:T(8,128)(2,1)} %rhs_hbm.1) | copy-start | bytes 786436
  12.7 1.9 %copy-start.5 = (f32[1,4,8,128]{3,2,1,0:T(8,128)S(1)}, f32[1,4,8,128]{3,2,1,0:T(8,128)}, u32[]{:S(2)}) copy-start(f32[1,4,8,128]{3,2,1,0:T(8,128)} %lower_hbm.1) | copy-start | bytes 49156
  12.7 1.9 %copy-start.6 = (f32[1,4,8,128]{3,2,1,0:T(8,128)S(1)}, f32[1,4,8,128]{3,2,1,0:T(8,128)}, u32[]{:S(2)}) copy-start(f32[1,4,8,128]{3,2,1,0:T(8,128)} %upper_hbm.1) | copy-start | bytes 49156
  16.1 4.0 %collective-permute-start.2 = (bf16[2,1296,128]{2,1,0:T(8,128)(2,1)S(1)}, bf16[2,1296,128]{2,1,0:T(8,128)(2,1)S(1)}, u32[]{:S(2)}, u32[]{:S(2)}) collective-permute-start(bf16[2,1296,128]{2,1,0:T(8,128)(2,1)S(1)} %get-tuple-element.29.send), channel_id=1, source_target_pairs={{0,16},{16,0},{32,48},{48,32},{64,80},{80,64},{96,112},{112,96},{1... | collective-permute-start | bytes 1990664 | tf_op jit(solution)/shard_map/ppermute | solution.py:244
  21.1 11.7 %collective-permute-start.3 = (bf16[1296,128]{1,0:T(8,128)(2,1)S(1)}, bf16[1296,128]{1,0:T(8,128)(2,1)S(1)}, u32[]{:S(2)}, u32[]{:S(2)}) collective-permute-start(bf16[1296,128]{1,0:T(8,128)(2,1)S(1)} %get-tuple-element.31), channel_id=1, source_target_pairs={{0,32},{16,48},{32,0},{48,16},{64,96},{80,112},{96,64},{112,80},{1... | collective-permute-start | bytes 995336 | tf_op jit(solution)/shard_map/ppermute | solution.py:255
  33.6 0.7 collective-permute-start.4
  34.5 0.7 collective-permute-start.5
  35.4 0.7 collective-permute-start.6
  36.3 0.7 collective-permute-start.7
  37.2 0.7 collective-permute-start.8
  38.1 0.7 collective-permute-start.9
  39.0 28.8 %collective-permute-start.10 = (bf16[8,32,128]{2,1,0:T(8,128)(2,1)S(1)}, bf16[8,32,128]{2,1,0:T(8,128)(2,1)S(1)}, u32[]{:S(2)}, u32[]{:S(2)}) collective-permute-start(bf16[8,32,128]{2,1,0:T(8,128)(2,1)S(1)} %get-tuple-element.44), channel_id=1, source_target_pairs={{384,448},{400,464},{416,480},{432,496},{385,449},{401,465},{417,4... | collective-permute-start | bytes 196616 | tf_op jit(solution)/shard_map/ppermute | solution.py:277

commit v2 on v1

v2 whole, which is shorter than its diff:
```python
import functools

import jax
import jax.numpy as jnp
from jax import lax
from jax.experimental import pallas as pl
from jax.experimental.pallas import tpu as pltpu
from jax.sharding import PartitionSpec as P

F32 = jnp.float32
BF16 = jnp.bfloat16
VMEM = pl.BlockSpec(memory_space=pltpu.VMEM)
SMEM = pl.BlockSpec(memory_space=pltpu.SMEM)
ANY = pl.BlockSpec(memory_space=pl.ANY)
PAD = 16


def pin(x):
    return pltpu.with_memory_space_constraint(x, pltpu.VMEM)


def in_hbm(x):
    return pltpu.with_memory_space_constraint(x, pltpu.HBM)


def in_vmem(shape, dtype=BF16):
    return pltpu.VMEM(shape, dtype)


def params(mib=16):
    return pltpu.CompilerParams(vmem_limit_bytes=mib * 1024 * 1024)


def cost(flops, size):
    return pl.CostEstimate(flops=flops, bytes_accessed=size, transcendentals=0)


def dot(a, b, dims=((1,), (0,))):
    return lax.dot_general(a, b, (dims, ((), ())), preferred_element_type=F32)


def place():
    position = lax.axis_index("stream")
    return lax.rem(position, 2), lax.rem(lax.div(position, 2), 2)


def maps_kernel(widths, rhs_hbm, prev_hbm, u_hbm, d_hbm, lower_hbm, upper_hbm, index_hbm, keep, send, d, partial,
                lower, upper, u, rhs, prev, lower_in, upper_in, index, u_sem, d_sem, sem):
    core, _ = place()
    slabs, slots, nv, nb = rhs.shape
    half = slabs // 2
    small = [
        pltpu.make_async_copy(index_hbm.at[0], index, sem.at[1]),
        pltpu.make_async_copy(lower_hbm.at[0], lower_in, sem.at[2]),
        pltpu.make_async_copy(upper_hbm.at[0], upper_in, sem.at[3]),
        pltpu.make_async_copy(prev_hbm.at[0], prev.at[pl.ds(1, slabs)], sem.at[4]),
        pltpu.make_async_copy(rhs_hbm.at[0], rhs, sem.at[0]),
    ]

    def block_copies(m):
        return (pltpu.make_async_copy(u_hbm.at[0, m], u.at[m], u_sem.at[m]),
                pltpu.make_async_copy(d_hbm.at[0, m], d.at[m], d_sem.at[m]))

    for copy in small:
        copy.start()
    for j in range(half):
        for first in ((1 - core) * half, core * half):
            for copy in block_copies(first + j):
                copy.start()
    prev[0] = jnp.zeros_like(prev[0])
    prev[slabs + 1] = jnp.zeros_like(prev[0])
    for copy in small:
        copy.wait()
    width = widths[0]
    rows = lax.broadcasted_iota(jnp.int32, (PAD, nb), 0)
    active = lax.broadcasted_iota(jnp.int32, (slots, nb), 0) < width

    def body(j, _):
        for out, first in ((send, (1 - core) * half), (keep, core * half)):
            m = first + j
            for copy in block_copies(m):
                copy.wait()
            tile = jnp.zeros((PAD, nb), F32)
            lo = jnp.where(active, lower_in[m], 0.0)
            up = jnp.where(active, upper_in[m], 0.0)
            lower[m], upper[m] = lo, up
            for k in range(slots):
                side = lo[k : k + 1, :] * prev[m, k].astype(F32) + up[k : k + 1, :] * prev[m + 2, k].astype(F32)
                part = jnp.where(k < width, rhs[m, k].astype(F32) - side, 0.0)
                partial[m, k] = part
                c = dot(part.astype(BF16), d[m, k], ((1,), (1,)))
                b = jnp.where(k < width, -dot(u[m, k], d[m, k], ((0,), (1,))), 0.0)
                out[j, pl.ds(k * (nv + nb), nv), :] = c.astype(BF16)
                out[j, pl.ds(k * (nv + nb) + nv, nb), :] = b.astype(BF16)
                tile = tile + jnp.where(rows == k, index[m, k].astype(F32), 0.0)
            out[j, pl.ds(slots * (nv + nb), PAD), :] = tile.astype(BF16)
        return 0

    lax.fori_loop(0, half, body, 0)


def edges_kernel(below, above, d, partial, lower, upper, keep_in, send_in, keep, send):
    core, _ = place()
    slabs, slots, nv, nb = partial.shape
    step = nv + nb

    def edge(out, j, m, gain, halo):
        for k in range(slots):
            part = partial[m, k] - gain[m, pl.ds(k, 1), :] * halo[0, k].astype(F32)
            out[j, pl.ds(k * step, nv), :] = dot(part.astype(BF16), d[m, k], ((1,), (1,))).astype(BF16)

    for here, first, last in ((0, keep, send), (1, send, keep)):
        @pl.when(core == here)
        def _():
            edge(first, 0, 0, lower, below)
            edge(last, slabs // 2 - 1, slabs - 1, upper, above)


def slot_scalars(tile, scratch, slots):
    scratch[...] = tile.astype(jnp.int32)
    return [scratch[k, 0] for k in range(slots)]


def compose(lo, hi, out, scratch, slots, nv, nb):
    step = nv + nb
    tile_lo = lo[pl.ds(slots * step, PAD), :].astype(F32)
    tile_hi = hi[pl.ds(slots * step, PAD), :].astype(F32)
    picks = slot_scalars(tile_hi, scratch, slots)
    tile = jnp.zeros_like(tile_hi)
    for n in range(slots):
        tile = tile + jnp.where(tile_hi == n, tile_lo[n : n + 1, :], 0.0)
    out[pl.ds(slots * step, PAD), :] = tile.astype(BF16)
    for k in range(slots):
        x = lo[pl.ds(pl.multiple_of(picks[k] * step, 16), step), :]
        y = dot(x, hi[pl.ds(k * step + nv, nb), :])
        c = hi[pl.ds(k * step, nv), :].astype(F32)
        out[pl.ds(k * step, nv), :] = (y[:nv] + c).astype(BF16)
        out[pl.ds(k * step + nv, nb), :] = y[nv:].astype(BF16)


def pair_kernel(slots, nv, keep, recv, out_keep, out_send, scratch):
    core, chip = place()
    nb = keep.shape[-1]
    for here, lo, hi in ((0, keep, recv), (1, recv, keep)):
        @pl.when(core == here)
        def _():
            compose(lo.at[1 - chip], hi.at[1 - chip], out_send, scratch, slots, nv, nb)
            compose(lo.at[chip], hi.at[chip], out_keep, scratch, slots, nv, nb)


def group_kernel(slots, nv, keep, recv, out, start, scratch):
    _, chip = place()
    nb = out.shape[-1]
    for here, lo, hi in ((0, keep, recv), (1, recv, keep)):
        @pl.when(chip == here)
        def _():
            compose(lo, hi, out, scratch, slots, nv, nb)
    for k in range(slots):
        start[k] = out[pl.ds(k * (nv + nb), nv), :]


def apply_map(x, m, out, scratch, slots, nv, nb):
    step = nv + nb
    picks = slot_scalars(m[pl.ds(slots * step, PAD), :].astype(F32), scratch, slots)
    for k in range(slots):
        y = dot(x[picks[k]], m[pl.ds(k * step + nv, nb), :])
        out[k] = (y + m[pl.ds(k * step, nv), :].astype(F32)).astype(BF16)


def hop_kernel(slots, nv, recv, group, inflow, out, inflow_out, scratch):
    apply_map(recv, group, out, scratch, slots, nv, group.shape[-1])
    inflow_out[...] = inflow[...] + recv[...]


def share_kernel(slots, nv, arrived, inflow, keep, recv, group, out, total, scratch):
    _, chip = place()
    nb = group.shape[-1]
    x = inflow[...] + arrived[...]
    total[...] = x
    out[0] = x
    for here, lo in ((0, keep), (1, recv)):
        @pl.when(chip == here)
        def _():
            apply_map(total, lo, out.at[1], scratch, slots, nv, nb)
    apply_map(total, group, out.at[2], scratch, slots, nv, nb)


def finish_kernel(slots, nv, shared, keep, send, out, result, scratch, sem):
    core, chip = place()
    slabs = out.shape[1]
    half = slabs // 2
    nb = out.shape[-1]
    owners = [2 * (m % 2) + m // 2 for m in range(slabs)]

    @pl.when(core == 1)
    def _():
        copies = [pltpu.make_async_copy(shared.at[owners[m], 1 + chip], out.at[0, m], sem.at[m]) for m in range(slabs)]
        for copy in copies:
            copy.start()
        for copy in copies:
            copy.wait()

    @pl.when(core == 0)
    def _():
        copies = []
        for m in range(slabs):
            maps = keep if m < half else send
            apply_map(shared.at[owners[m], chip], maps.at[m % half], result.at[m], scratch, slots, nv, nb)
            copies.append(pltpu.make_async_copy(result.at[m], out.at[0, m], sem.at[m]))
            copies[-1].start()
        for copy in copies:
            copy.wait()


def local(rhs, previous, inverse_blocks, upstream_blocks, lower_gain, upper_gain, widths, upstream_index):
    _, slabs, slots, nv, nb = rhs.shape
    half = slabs // 2
    sections, peers = lax.axis_size("stream"), lax.axis_size("span")
    groups = sections // 4
    rows = slots * (nv + nb) + PAD

    up = [(i, i + 1) for i in range(peers - 1)]
    down = [(j, i) for i, j in up]
    below = lax.ppermute(previous[0, slabs - 1 :], "span", up)
    above = lax.ppermute(previous[0, :1], "span", down)

    half_shape = in_vmem((half, rows, nb))
    one_shape = in_vmem((rows, nb))
    vec_shape = in_vmem((slots, nv, nb))
    index_scratch = pltpu.VMEM((PAD, nb), jnp.int32)
    block_shape, gain_shape = (slabs, slots, nb, nb), (slabs, slots, nb)

    keep, send, d, partial, lower, upper = pl.pallas_call(
        maps_kernel,
        out_shape=(half_shape, half_shape, in_vmem(block_shape), in_vmem((slabs, slots, nv, nb), F32),
                   in_vmem(gain_shape, F32), in_vmem(gain_shape, F32)),
        in_specs=[SMEM] + [ANY] * 7,
        out_specs=(VMEM,) * 6,
        scratch_shapes=[
            pltpu.VMEM(block_shape, BF16),
            pltpu.VMEM((slabs, slots, nv, nb), BF16),
            pltpu.VMEM((slabs + 2, slots, nv, nb), BF16),
            pltpu.VMEM(gain_shape, F32),
            pltpu.VMEM(gain_shape, F32),
            pltpu.SMEM((slabs, slots), jnp.int32),
            pltpu.SemaphoreType.DMA((slabs,)),
            pltpu.SemaphoreType.DMA((slabs,)),
            pltpu.SemaphoreType.DMA((5,)),
        ],
        compiler_params=params(),
        cost_estimate=cost(2 * slabs * slots * nb**3, 4 * slabs * slots * nb * nb),
        name="section_maps",
    )(widths, *(in_hbm(x) for x in (rhs, previous, upstream_blocks, inverse_blocks, lower_gain, upper_gain, upstream_index)))
    keep, send = pl.pallas_call(
        edges_kernel,
        out_shape=(half_shape, half_shape),
        in_specs=[VMEM] * 8,
        out_specs=(VMEM, VMEM),
        input_output_aliases={6: 0, 7: 1},
        compiler_params=params(),
        name="section_edges",
    )(*(pin(x) for x in (below, above, d, partial, lower, upper, keep, send)))

    recv = lax.ppermute(send, "stream", [(i, i ^ 1) for i in range(sections)])
    pair_keep, pair_send = pl.pallas_call(
        functools.partial(pair_kernel, slots, nv),
        out_shape=(one_shape, one_shape),
        in_specs=[VMEM, VMEM],
        out_specs=(VMEM, VMEM),
        scratch_shapes=[index_scratch],
        compiler_params=params(),
        name="compose_chip",
    )(pin(keep), pin(recv))

    pair_recv = lax.ppermute(pair_send, "stream", [(i, i ^ 2) for i in range(sections)])
    group, state = pl.pallas_call(
        functools.partial(group_kernel, slots, nv),
        out_shape=(one_shape, vec_shape),
        in_specs=[VMEM, VMEM],
        out_specs=(VMEM, VMEM),
        scratch_shapes=[index_scratch],
        compiler_params=params(),
        name="compose_group",
    )(pin(pair_keep), pin(pair_recv))

    hop = pl.pallas_call(
        functools.partial(hop_kernel, slots, nv),
        out_shape=(vec_shape, vec_shape),
        in_specs=[VMEM, VMEM, VMEM],
        out_specs=(VMEM, VMEM),
        scratch_shapes=[index_scratch],
        compiler_params=params(),
        name="hop",
    )
    inflow = jnp.zeros((slots, nv, nb), BF16)
    for g in range(1, groups):
        arrived = lax.ppermute(state, "stream", [(4 * g - 4 + r, 4 * g + r) for r in range(4)])
        if g < groups - 1:
            state, inflow = hop(pin(arrived), pin(group), pin(inflow))

    shares = pl.pallas_call(
        functools.partial(share_kernel, slots, nv),
        out_shape=in_vmem((3, slots, nv, nb)),
        in_specs=[VMEM] * 5,
        out_specs=VMEM,
        scratch_shapes=[pltpu.VMEM((slots, nv, nb), BF16), index_scratch],
        compiler_params=params(),
        name="share",
    )(pin(arrived), pin(inflow), pin(pair_keep), pin(pair_recv), pin(group))
    shared = lax.all_gather(
        shares, "stream", axis_index_groups=[[4 * g + r for r in range(4)] for g in range(groups)]
    )
    return pl.pallas_call(
        functools.partial(finish_kernel, slots, nv),
        out_shape=jax.ShapeDtypeStruct(rhs.shape, BF16),
        in_specs=[VMEM, VMEM, VMEM],
        out_specs=ANY,
        scratch_shapes=[
            pltpu.VMEM((slabs, slots, nv, nb), BF16),
            index_scratch,
            pltpu.SemaphoreType.DMA((slabs,)),
        ],
        compiler_params=params(),
        name="finish",
    )(pin(shared), pin(keep), pin(send))


def solution(mesh):
    in_specs = (
        P("stream", "span", None, None, None),
        P("stream", "span", None, None, None),
        P("stream", "span", None, None, None),
        P("stream", "span", None, None, None),
        P("stream", "span", None, None),
        P("stream", "span", None, None),
        P("stream"),
        P("stream", "span", None),
    )
    out_specs = P("stream", "span", None, None, None)
    return jax.shard_map(local, mesh=mesh, in_specs=in_specs, out_specs=out_specs, check_vma=False)
```

time: 81.7 us -> 75.3 us (0.922)
  Pallas kernels: 10.2 us -> 6.97 us
  local copies, waits for them, and re-layouts: 3.96 us -> 0.89 us
    unnamed x16 -> x0, local copies, waits for them, and re-layouts: 3.07 us -> none
    pallas_call x1, Pallas kernels: 2.03 us -> 1.12 us  [local(): pl.pallas_call(functools.partial(finish_kernel, slots, nv), out_shape=jax...]
    pallas_call x7 -> x6, Pallas kernels: 2.1 us -> 1.26 us  [local(): state, inflow = hop(pin(arrived), pin(group), pin(inflow))]
  transfers between devices with their start and end apart: 11 -> 11, of which waited for: 3 -> 3; matrix products, arithmetic and copies ran while one was open for 0% -> 0% of each run, Pallas kernels for 2% -> 4%
where the time goes in v2:
time: 75.3 us; the launch traced here: 74.8 us
  waiting for transfers between devices  38.4 us (51%)
  starting transfers between devices  18.1 us (24%)
  blocking collectives  9.6 us (13%)
  Pallas kernels  6.97 us (9%)
  local copies, waits for them, and re-layouts  0.89 us (1%)
  between operations  0.84 us (1%)
    ppermute x7, waiting for transfers between devices, local(): lax.ppermute(state, 'stream', [(4 * g - 4 + r, 4 * g + r) for r in range(...  27.5 us
    all_gather x1, blocking collectives, local(): lax.all_gather(shares, 'stream', axis_index_groups=[[4 * g + r for r in r...  9.6 us
    ppermute x1, waiting for transfers between devices, local(): lax.ppermute(pair_send, 'stream', [(i, i ^ 2) for i in range(sections)])  8.79 us
    ppermute x7, starting transfers between devices, local(): lax.ppermute(state, 'stream', [(4 * g - 4 + r, 4 * g + r) for r in range(...  5.27 us
    ppermute x1, starting transfers between devices, local(): above = lax.ppermute(previous[0, :1], 'span', down)  4.55 us
    ppermute x1, starting transfers between devices, local(): below = lax.ppermute(previous[0, slabs - 1:], 'span', up)  3.4 us
    pallas_call x1, Pallas kernels, local(): pl.pallas_call(maps_kernel, out_shape=(half_shape, half_shape, in_vmem(bl...  3.15 us
    ppermute x1, starting transfers between devices, local(): lax.ppermute(pair_send, 'stream', [(i, i ^ 2) for i in range(sections)])  2.93 us
  transfers between devices with their start and end apart: 11, of which 3 were waited for; matrix products, arithmetic and copies ran while one was open for 0% of the time, Pallas kernels for 4%

profile of v2, /device:TPU:464, one launch (start us, length us, event | category | flops | bytes accessed | tf_op | source)
XLA Modules:
  0.0 74.8 jit_solution(12699105914609040793)
XLA Ops:
  0.0 0.9 %slice_bitcast_fusion = (bf16[1,8,32,128]{3,2,1,0:T(8,128)(2,1)S(1)}, bf16[1,8,32,128]{3,2,1,0:T(8,128)(2,1)S(1)}) fusion(bf16[1,4,8,32,128]{4,3,2,1,0:T(8,128)(2,1)} %prev_hbm.1), kind=kLoop, calls=%fused_computation | loop fusion | bytes 262144 | tf_op jit(solution)/shard_map/squeeze | solution.py:225
  0.9 3.4 %collective-permute-start = (bf16[1,8,32,128]{3,2,1,0:T(8,128)(2,1)S(1)}, bf16[1,8,32,128]{3,2,1,0:T(8,128)(2,1)S(1)}, u32[]{:S(2)}, u32[]{:S(2)}) collective-permute-start(bf16[1,8,32,128]{3,2,1,0:T(8,128)(2,1)S(1)} %get-tuple-element.54), channel_id=1, source_target_pairs={{0,1},{1,2},{2,3},{3,4},{4,5},{5,6},{6,7},{7,8},{8,9},{9,10},{10,1... | collective-permute-start | bytes 196616 | tf_op jit(solution)/shard_map/ppermute | solution.py:224
  4.3 4.6 %collective-permute-start.1 = (bf16[1,8,32,128]{3,2,1,0:T(8,128)(2,1)S(1)}, bf16[1,8,32,128]{3,2,1,0:T(8,128)(2,1)S(1)}, u32[]{:S(2)}, u32[]{:S(2)}) collective-permute-start(bf16[1,8,32,128]{3,2,1,0:T(8,128)(2,1)S(1)} %get-tuple-element.53), channel_id=1, source_target_pairs={{1,0},{2,1},{3,2},{4,3},{5,4},{6,5},{7,6},{8,7},{9,8},{10,9},{11,1... | collective-permute-start | bytes 196616 | tf_op jit(solution)/shard_map/ppermute | solution.py:225
  9.5 3.1 %section_maps.1 = (bf16[2,1296,128]{2,1,0:T(8,128)(2,1)S(1)}, bf16[2,1296,128]{2,1,0:T(8,128)(2,1)S(1)}, bf16[4,8,128,128]{3,2,1,0:T(8,128)(2,1)S(1)}, f32[4,8,3...) custom-call(s32[1]{0:T(128)S(6)} %copy.13.widths, bf16[1,4,8,32,128]{4,3,2,1,0:T(8,128)(2,1)} %rhs_hbm.1, ...), custom_call_target="tpu_custom_call" | custom-call | flops 134217728 | bytes 2097152 | tf_op jit(solution)/shard_map/section_maps/pallas_call | solution.py:233
  12.7 0.0 collective-permute-done.below
  12.7 0.0 collective-permute-done.1.above
  12.7 0.4 section_edges.1
  13.1 1.9 %collective-permute-start.2 = (bf16[2,1296,128]{2,1,0:T(8,128)(2,1)S(1)}, bf16[2,1296,128]{2,1,0:T(8,128)(2,1)S(1)}, u32[]{:S(2)}, u32[]{:S(2)}) collective-permute-start(bf16[2,1296,128]{2,1,0:T(8,128)(2,1)S(1)} %get-tuple-element.36.send), channel_id=1, source_target_pairs={{0,16},{16,0},{32,48},{48,32},{64,80},{80,64},{96,112},{112,96},{1... | collective-permute-start | bytes 1990664 | tf_op jit(solution)/shard_map/ppermute | solution.py:264
  15.0 2.1 %collective-permute-done.2.recv = bf16[2,1296,128]{2,1,0:T(8,128)(2,1)S(1)} collective-permute-done((bf16[2,1296,128]{2,1,0:T(8,128)(2,1)S(1)}, bf16[2,1296,128]{2,1,0:T(8,128)(2,1)S(1)}, u32[]{:S(2)}, u32[]{:S(2)}) %collective-permute-start.2) | collective-permute-done | bytes 663584 | tf_op jit(solution)/shard_map/ppermute | solution.py:264
  17.1 0.4 compose_chip.1
  17.4 2.9 %collective-permute-start.3 = (bf16[1296,128]{1,0:T(8,128)(2,1)S(1)}, bf16[1296,128]{1,0:T(8,128)(2,1)S(1)}, u32[]{:S(2)}, u32[]{:S(2)}) collective-permute-start(bf16[1296,128]{1,0:T(8,128)(2,1)S(1)} %get-tuple-element.38), channel_id=1, source_target_pairs={{0,32},{16,48},{32,0},{48,16},{64,96},{80,112},{96,64},{112,80},{1... | collective-permute-start | bytes 995336 | tf_op jit(solution)/shard_map/ppermute | solution.py:275
  20.4 8.8 %collective-permute-done.3.recv = bf16[1296,128]{1,0:T(8,128)(2,1)S(1)} collective-permute-done((bf16[1296,128]{1,0:T(8,128)(2,1)S(1)}, bf16[1296,128]{1,0:T(8,128)(2,1)S(1)}, u32[]{:S(2)}, u32[]{:S(2)}) %collective-permute-start.3) | collective-permute-done | bytes 331808 | tf_op jit(solution)/shard_map/ppermute | solution.py:275
  29.2 0.3 compose_group.1
  29.5 0.7 collective-permute-start.4
  30.1 0.0 collective-permute-done.4.recv
  30.2 0.2 hop.6
  30.4 0.7 collective-permute-start.5
  31.0 0.0 collective-permute-done.5.recv
  31.0 0.2 hop.7
  31.3 0.7 collective-permute-start.6
  31.9 0.0 collective-permute-done.6.recv
  31.9 0.2 hop.8
  32.1 0.7 collective-permute-start.7
  32.8 0.0 collective-permute-done.7.recv
  32.8 0.2 hop.9
  33.0 0.7 collective-permute-start.8
  33.7 0.0 collective-permute-done.8.recv
  33.7 0.2 hop.10
  33.9 0.7 collective-permute-start.9
  34.6 0.0 collective-permute-done.9.recv
  34.6 0.2 hop.11
  34.8 1.3 %collective-permute-start.10 = (bf16[8,32,128]{2,1,0:T(8,128)(2,1)S(1)}, bf16[8,32,128]{2,1,0:T(8,128)(2,1)S(1)}, u32[]{:S(2)}, u32[]{:S(2)}) collective-permute-start(bf16[8,32,128]{2,1,0:T(8,128)(2,1)S(1)} %get-tuple-element.51), channel_id=1, source_target_pairs={{384,448},{400,464},{416,480},{432,496},{385,449},{401,465},{417,4... | collective-permute-start | bytes 196616 | tf_op jit(solution)/shard_map/ppermute | solution.py:297
  36.1 27.5 %collective-permute-done.10.arrived = bf16[8,32,128]{2,1,0:T(8,128)(2,1)S(1)} collective-permute-done((bf16[8,32,128]{2,1,0:T(8,128)(2,1)S(1)}, bf16[8,32,128]{2,1,0:T(8,128)(2,1)S(1)}, u32[]{:S(2)}, u32[]{:S(2)}) %collective-permute-start.10) | collective-permute-done | bytes 65568 | tf_op jit(solution)/shard_map/ppermute | solution.py:297
  63.6 0.4 share.1
  64.1 9.6 %all-gather = bf16[12,8,32,128]{3,2,1,0:T(8,128)(2,1)S(1)} all-gather(bf16[3,8,32,128]{3,2,1,0:T(8,128)(2,1)S(1)} %share.1), channel_id=2, replica_groups={{0,16,32,48},{64,80,96,112},{128,144,160,176},{192,208,224,240},{256,27..., dimensions={0}, use_global_device_ids=true | all-gather | bytes 983040 | tf_op jit(solution)/shard_map/all_gather | solution.py:310
  73.7 1.1 %finish.1 = bf16[1,4,8,32,128]{4,3,2,1,0:T(8,128)(2,1)} custom-call(bf16[4,3,8,32,128]{4,3,2,1,0:T(8,128)(2,1)S(1)} %bitcast.5, bf16[2,1296,128]{2,1,0:T(8,128)(2,1)S(1)} %get-tuple-element.35.keep, bf16[2,1296,128]{2,1,0:T(8,128)(2,1)S(1)} %get-tuple-element.36.send), custom_call_target="tpu_custom_call" | custom-call | tf_op jit(solution)/shard_map/finish/pallas_call | solution.py:313
  (1 shorter events, 0.0 us)
Async XLA Ops:
  0.9 11.8 %collective-permute-start = (bf16[1,8,32,128]{3,2,1,0:T(8,128)(2,1)S(1)}, bf16[1,8,32,128]{3,2,1,0:T(8,128)(2,1)S(1)}, u32[]{:S(2)}, u32[]{:S(2)}) collective-permute-start(bf16[1,8,32,128]{3,2,1,0:T(8,128)(2,1)S(1)} %get-tuple-element.54), channel_id=1, source_target_pairs={{0,1},{1,2},{2,3},{3,4},{4,5},{5,6},{6,7},{7,8},{8,9},{9,10},{10,1... | collective-permute-start | bytes 196616 | tf_op jit(solution)/shard_map/ppermute | solution.py:224
  4.3 8.4 %collective-permute-start.1 = (bf16[1,8,32,128]{3,2,1,0:T(8,128)(2,1)S(1)}, bf16[1,8,32,128]{3,2,1,0:T(8,128)(2,1)S(1)}, u32[]{:S(2)}, u32[]{:S(2)}) collective-permute-start(bf16[1,8,32,128]{3,2,1,0:T(8,128)(2,1)S(1)} %get-tuple-element.53), channel_id=1, source_target_pairs={{1,0},{2,1},{3,2},{4,3},{5,4},{6,5},{7,6},{8,7},{9,8},{10,9},{11,1... | collective-permute-start | bytes 196616 | tf_op jit(solution)/shard_map/ppermute | solution.py:225
  13.1 4.0 %collective-permute-start.2 = (bf16[2,1296,128]{2,1,0:T(8,128)(2,1)S(1)}, bf16[2,1296,128]{2,1,0:T(8,128)(2,1)S(1)}, u32[]{:S(2)}, u32[]{:S(2)}) collective-permute-start(bf16[2,1296,128]{2,1,0:T(8,128)(2,1)S(1)} %get-tuple-element.36.send), channel_id=1, source_target_pairs={{0,16},{16,0},{32,48},{48,32},{64,80},{80,64},{96,112},{112,96},{1... | collective-permute-start | bytes 1990664 | tf_op jit(solution)/shard_map/ppermute | solution.py:264
  17.4 11.7 %collective-permute-start.3 = (bf16[1296,128]{1,0:T(8,128)(2,1)S(1)}, bf16[1296,128]{1,0:T(8,128)(2,1)S(1)}, u32[]{:S(2)}, u32[]{:S(2)}) collective-permute-start(bf16[1296,128]{1,0:T(8,128)(2,1)S(1)} %get-tuple-element.38), channel_id=1, source_target_pairs={{0,32},{16,48},{32,0},{48,16},{64,96},{80,112},{96,64},{112,80},{1... | collective-permute-start | bytes 995336 | tf_op jit(solution)/shard_map/ppermute | solution.py:275
  29.5 0.7 collective-permute-start.4
  30.4 0.7 collective-permute-start.5
  31.3 0.7 collective-permute-start.6
  32.1 0.7 collective-permute-start.7
  33.0 0.7 collective-permute-start.8
  33.9 0.7 collective-permute-start.9
  34.8 28.8 %collective-permute-start.10 = (bf16[8,32,128]{2,1,0:T(8,128)(2,1)S(1)}, bf16[8,32,128]{2,1,0:T(8,128)(2,1)S(1)}, u32[]{:S(2)}, u32[]{:S(2)}) collective-permute-start(bf16[8,32,128]{2,1,0:T(8,128)(2,1)S(1)} %get-tuple-element.51), channel_id=1, source_target_pairs={{384,448},{400,464},{416,480},{432,496},{385,449},{401,465},{417,4... | collective-permute-start | bytes 196616 | tf_op jit(solution)/shard_map/ppermute | solution.py:297

commit v3 on v2

--- a/solution.py
+++ b/solution.py
@@ -10,9 +10,10 @@
 F32 = jnp.float32
 BF16 = jnp.bfloat16
 VMEM = pl.BlockSpec(memory_space=pltpu.VMEM)
-SMEM = pl.BlockSpec(memory_space=pltpu.SMEM)
 ANY = pl.BlockSpec(memory_space=pl.ANY)
+STEP = 4_600_000_000
 PAD = 16
+JOINED = (5, 6)
 
 
 def pin(x):
@@ -41,15 +42,24 @@
 
 def place():
     position = lax.axis_index("stream")
-    return lax.rem(position, 2), lax.rem(lax.div(position, 2), 2)
-
-
-def maps_kernel(widths, rhs_hbm, prev_hbm, u_hbm, d_hbm, lower_hbm, upper_hbm, index_hbm, keep, send, d, partial,
-                lower, upper, u, rhs, prev, lower_in, upper_in, index, u_sem, d_sem, sem):
-    core, _ = place()
+    return lax.rem(position, 2), lax.rem(lax.div(position, 2), 2), lax.div(position, 4)
+
+
+def front_half(chip, group):
+    return jnp.logical_and(chip == 0, group == JOINED[1])
+
+
+def back_half(chip, group):
+    return jnp.logical_and(chip == 1, group == JOINED[0])
+
+
+def maps_kernel(widths_hbm, rhs_hbm, prev_hbm, u_hbm, d_hbm, lower_hbm, upper_hbm, index_hbm, keep, send, d, partial,
+                lower, upper, u, rhs, prev, lower_in, upper_in, index, widths, u_sem, d_sem, sem):
+    core, _, _ = place()
     slabs, slots, nv, nb = rhs.shape
     half = slabs // 2
     small = [
+        pltpu.make_async_copy(widths_hbm, widths, sem.at[5]),
         pltpu.make_async_copy(index_hbm.at[0], index, sem.at[1]),
         pltpu.make_async_copy(lower_hbm.at[0], lower_in, sem.at[2]),
         pltpu.make_async_copy(upper_hbm.at[0], upper_in, sem.at[3]),
@@ -100,7 +110,7 @@
 
 
 def edges_kernel(below, above, d, partial, lower, upper, keep_in, send_in, keep, send):
-    core, _ = place()
+    core, _, _ = place()
     slabs, slots, nv, nb = partial.shape
     step = nv + nb
 
@@ -138,25 +148,17 @@
         out[pl.ds(k * step + nv, nb), :] = y[nv:].astype(BF16)
 
 
-def pair_kernel(slots, nv, keep, recv, out_keep, out_send, scratch):
-    core, chip = place()
+def pair_kernel(slots, nv, keep, recv, out_keep, out_send, start, scratch):
+    core, chip, _ = place()
     nb = keep.shape[-1]
     for here, lo, hi in ((0, keep, recv), (1, recv, keep)):
         @pl.when(core == here)
         def _():
             compose(lo.at[1 - chip], hi.at[1 - chip], out_send, scratch, slots, nv, nb)
             compose(lo.at[chip], hi.at[chip], out_keep, scratch, slots, nv, nb)
-
-
-def group_kernel(slots, nv, keep, recv, out, start, scratch):
-    _, chip = place()
-    nb = out.shape[-1]
-    for here, lo, hi in ((0, keep, recv), (1, recv, keep)):
-        @pl.when(chip == here)
-        def _():
-            compose(lo, hi, out, scratch, slots, nv, nb)
     for k in range(slots):
-        start[k] = out[pl.ds(k * (nv + nb), nv), :]
+        start[chip, k] = out_keep[pl.ds(k * (nv + nb), nv), :]
+        start[1 - chip, k] = out_send[pl.ds(k * (nv + nb), nv), :]
 
 
 def apply_map(x, m, out, scratch, slots, nv, nb):
@@ -167,26 +169,84 @@
         out[k] = (y + m[pl.ds(k * step, nv), :].astype(F32)).astype(BF16)
 
 
-def hop_kernel(slots, nv, recv, group, inflow, out, inflow_out, scratch):
-    apply_map(recv, group, out, scratch, slots, nv, group.shape[-1])
+def first_kernel(slots, nv, arrived, keep, send, out_front, out_back, scratch):
+    nb = keep.shape[-1]
+    apply_map(arrived.at[0], send, out_front, scratch, slots, nv, nb)
+    apply_map(arrived.at[1], keep, out_back, scratch, slots, nv, nb)
+
+
+def second_kernel(slots, nv, front, back, keep, recv, state, inflow, middle, scratch):
+    _, chip, _ = place()
+    nb = keep.shape[-1]
+    inflow[...] = front[...] + back[...]
+    for here, lo, hi in ((0, keep, recv), (1, recv, keep)):
+        @pl.when(chip == here)
+        def _():
+            apply_map(inflow, lo, middle, scratch, slots, nv, nb)
+            apply_map(middle, hi, state, scratch, slots, nv, nb)
+
+
+def group_kernel(slots, nv, keep, recv, out, scratch):
+    _, chip, _ = place()
+    nb = out.shape[-1]
+    for here, lo, hi in ((0, keep, recv), (1, recv, keep)):
+        @pl.when(chip == here)
+        def _():
+            compose(lo, hi, out, scratch, slots, nv, nb)
+
+
+def join_kernel(slots, nv, group, recv, out, scratch):
+    _, chip, number = place()
+    nb = out.shape[-1]
+    front, back = front_half(chip, number), back_half(chip, number)
+
+    @pl.when(front)
+    def _():
+        compose(recv, group, out, scratch, slots, nv, nb)
+
+    @pl.when(back)
+    def _():
+        compose(group, recv, out, scratch, slots, nv, nb)
+
+    @pl.when(jnp.logical_not(jnp.logical_or(front, back)))
+    def _():
+        out[...] = group[...]
+
+
+def hop_kernel(slots, nv, recv, chain, inflow, out, inflow_out, scratch):
+    apply_map(recv, chain, out, scratch, slots, nv, chain.shape[-1])
     inflow_out[...] = inflow[...] + recv[...]
 
 
-def share_kernel(slots, nv, arrived, inflow, keep, recv, group, out, total, scratch):
-    _, chip = place()
-    nb = group.shape[-1]
-    x = inflow[...] + arrived[...]
-    total[...] = x
-    out[0] = x
-    for here, lo in ((0, keep), (1, recv)):
+def fill_kernel(slots, nv, inflow, chain, group, out, scratch):
+    _, chip, _ = place()
+    for here, maps in ((0, chain), (1, group)):
         @pl.when(chip == here)
         def _():
-            apply_map(total, lo, out.at[1], scratch, slots, nv, nb)
-    apply_map(total, group, out.at[2], scratch, slots, nv, nb)
+            apply_map(inflow, maps, out, scratch, slots, nv, group.shape[-1])
+
+
+def share_kernel(slots, nv, arrived, filled, inflow, joined, keep, recv, out, total, middle, scratch):
+    _, chip, number = place()
+    nb = keep.shape[-1]
+    total[...] = inflow[...] + arrived[...] + filled[...]
+
+    @pl.when(front_half(chip, number))
+    def _():
+        apply_map(total, joined, middle, scratch, slots, nv, nb)
+        total[...] = middle[...]
+
+    out[0] = total[...]
+    for here, lo, hi in ((0, keep, recv), (1, recv, keep)):
+        @pl.when(chip == here)
+        def _():
+            apply_map(total, lo, middle, scratch, slots, nv, nb)
+            out[1] = middle[...]
+            apply_map(middle, hi, out.at[2], scratch, slots, nv, nb)
 
 
 def finish_kernel(slots, nv, shared, keep, send, out, result, scratch, sem):
-    core, chip = place()
+    core, chip, _ = place()
     slabs = out.shape[1]
     half = slabs // 2
     nb = out.shape[-1]
@@ -217,6 +277,7 @@
     half = slabs // 2
     sections, peers = lax.axis_size("stream"), lax.axis_size("span")
     groups = sections // 4
+    assert groups == JOINED[1] + 2
     rows = slots * (nv + nb) + PAD
 
     up = [(i, i + 1) for i in range(peers - 1)]
@@ -234,7 +295,7 @@
         maps_kernel,
         out_shape=(half_shape, half_shape, in_vmem(block_shape), in_vmem((slabs, slots, nv, nb), F32),
                    in_vmem(gain_shape, F32), in_vmem(gain_shape, F32)),
-        in_specs=[SMEM] + [ANY] * 7,
+        in_specs=[ANY] * 8,
         out_specs=(VMEM,) * 6,
         scratch_shapes=[
             pltpu.VMEM(block_shape, BF16),
@@ -243,9 +304,10 @@
             pltpu.VMEM(gain_shape, F32),
             pltpu.VMEM(gain_shape, F32),
             pltpu.SMEM((slabs, slots), jnp.int32),
+            pltpu.SMEM((1,), jnp.int32),
             pltpu.SemaphoreType.DMA((slabs,)),
             pltpu.SemaphoreType.DMA((slabs,)),
-            pltpu.SemaphoreType.DMA((5,)),
+            pltpu.SemaphoreType.DMA((6,)),
         ],
         compiler_params=params(),
         cost_estimate=cost(2 * slabs * slots * nb**3, 4 * slabs * slots * nb * nb),
@@ -261,52 +323,57 @@
         name="section_edges",
     )(*(pin(x) for x in (below, above, d, partial, lower, upper, keep, send)))
 
+    def call(kernel, outs, name, *args, scratch=(), flops=0):
+        return pl.pallas_call(
+            functools.partial(kernel, slots, nv),
+            out_shape=outs,
+            in_specs=[VMEM] * len(args),
+            out_specs=(VMEM,) * len(outs) if isinstance(outs, tuple) else VMEM,
+            scratch_shapes=[*scratch, index_scratch],
+            compiler_params=params(),
+            cost_estimate=cost(flops, 0) if flops else None,
+            name=name,
+        )(*(pin(x) for x in args))
+
+    def stream(x, *hops):
+        pairs = []
+        for chip, source, target in hops:
+            pairs += [(4 * source + 2 * chip + core, 4 * target + 2 * chip + core) for core in range(2)]
+        return lax.ppermute(x, "stream", pairs)
+
     recv = lax.ppermute(send, "stream", [(i, i ^ 1) for i in range(sections)])
-    pair_keep, pair_send = pl.pallas_call(
-        functools.partial(pair_kernel, slots, nv),
-        out_shape=(one_shape, one_shape),
-        in_specs=[VMEM, VMEM],
-        out_specs=(VMEM, VMEM),
-        scratch_shapes=[index_scratch],
-        compiler_params=params(),
-        name="compose_chip",
-    )(pin(keep), pin(recv))
-
-    pair_recv = lax.ppermute(pair_send, "stream", [(i, i ^ 2) for i in range(sections)])
-    group, state = pl.pallas_call(
-        functools.partial(group_kernel, slots, nv),
-        out_shape=(one_shape, vec_shape),
-        in_specs=[VMEM, VMEM],
-        out_specs=(VMEM, VMEM),
-        scratch_shapes=[index_scratch],
-        compiler_params=params(),
-        name="compose_group",
-    )(pin(pair_keep), pin(pair_recv))
-
-    hop = pl.pallas_call(
-        functools.partial(hop_kernel, slots, nv),
-        out_shape=(vec_shape, vec_shape),
-        in_specs=[VMEM, VMEM, VMEM],
-        out_specs=(VMEM, VMEM),
-        scratch_shapes=[index_scratch],
-        compiler_params=params(),
-        name="hop",
-    )
-    inflow = jnp.zeros((slots, nv, nb), BF16)
-    for g in range(1, groups):
-        arrived = lax.ppermute(state, "stream", [(4 * g - 4 + r, 4 * g + r) for r in range(4)])
-        if g < groups - 1:
-            state, inflow = hop(pin(arrived), pin(group), pin(inflow))
-
-    shares = pl.pallas_call(
-        functools.partial(share_kernel, slots, nv),
-        out_shape=in_vmem((3, slots, nv, nb)),
-        in_specs=[VMEM] * 5,
-        out_specs=VMEM,
-        scratch_shapes=[pltpu.VMEM((slots, nv, nb), BF16), index_scratch],
-        compiler_params=params(),
-        name="share",
-    )(pin(arrived), pin(inflow), pin(pair_keep), pin(pair_recv), pin(group))
+    pair_keep, pair_send, pair_start = call(
+        pair_kernel, (one_shape, one_shape, in_vmem((2, slots, nv, nb))), "compose_chip", keep, recv)
+
+    arrived = lax.ppermute(pair_start, "stream", [(0, 2), (1, 3)])
+    recv_second = lax.ppermute(pair_send, "stream", [(i, i ^ 2) for i in range(4, 8)])
+    recv_later = lax.ppermute(pair_send, "stream", [(i, i ^ 2) for i in range(8, sections)])
+    front, back = call(first_kernel, (vec_shape, vec_shape), "first_group", arrived, pair_keep, pair_send, flops=STEP)
+    back = lax.ppermute(back, "stream", [(2, 6), (3, 7)])
+    front = lax.ppermute(front, "stream", [(2, 4), (3, 5)])
+    state, inflow = call(
+        second_kernel, (vec_shape, vec_shape), "second_group", front, back, pair_keep, recv_second, scratch=(vec_shape,), flops=STEP)
+    arrived = stream(state, (0, 1, 2), (1, 1, 2))
+    group = call(group_kernel, one_shape, "compose_group", pair_keep, recv_later, flops=STEP)
+
+    a, b = JOINED
+    join_recv = stream(group, (0, a, b), (1, b, a))
+    for g in range(2, a):
+        state, inflow = call(hop_kernel, (vec_shape, vec_shape), "hop", arrived, group, inflow, flops=STEP)
+        arrived = stream(state, (0, g, g + 1 if g + 1 < a else b), (1, g, g + 1))
+        if g == 2:
+            pair_send, arrived = lax.optimization_barrier((pair_send, arrived))
+            recv_first = lax.ppermute(pair_send, "stream", [(i, i ^ 2) for i in range(4)])
+    chain = call(join_kernel, one_shape, "compose_join", group, join_recv)
+    state, inflow = call(hop_kernel, (vec_shape, vec_shape), "hop", arrived, chain, inflow, flops=STEP)
+    arrived = stream(state, (0, b, b + 1), (1, a, b + 1))
+    passed = call(fill_kernel, vec_shape, "fill", inflow, chain, group)
+    filled = stream(passed, (0, a - 1, a), (1, a, b))
+
+    shares = call(
+        share_kernel, in_vmem((3, slots, nv, nb)), "share",
+        arrived, filled, inflow, join_recv, pair_keep, recv_first + recv_second + recv_later,
+        scratch=(vec_shape, vec_shape))
     shared = lax.all_gather(
         shares, "stream", axis_index_groups=[[4 * g + r for r in range(4)] for g in range(groups)]
     )

time: 75.3 us -> 69.9 us (0.928)
  the two profiles are of different devices: /device:TPU:464 before, /device:TPU:409 now
where the time goes in v3:
time: 69.9 us; the launch traced here: 69.5 us
  starting transfers between devices  23.1 us (33%)
  waiting for transfers between devices  21.2 us (30%)
  blocking collectives  15.9 us (23%)
  Pallas kernels  7.54 us (11%)
  between operations  0.9 us (1%)
  local copies, waits for them, and re-layouts  0.88 us (1%)
    all_gather x1, blocking collectives, local(): lax.all_gather(shares, 'stream', axis_index_groups=[[4 * g + r for r in r...  15.9 us
    ppermute x7, waiting for transfers between devices, stream(): return lax.ppermute(x, 'stream', pairs)  10.9 us
    ppermute x1, waiting for transfers between devices, local(): lax.ppermute(pair_send, 'stream', [(i, i ^ 2) for i in range(8, sections)])  7.13 us
    ppermute x7, starting transfers between devices, stream(): return lax.ppermute(x, 'stream', pairs)  6.53 us
    ppermute x1, starting transfers between devices, local(): above = lax.ppermute(previous[0, :1], 'span', down)  4.57 us
    ppermute x1, starting transfers between devices, local(): recv = lax.ppermute(send, 'stream', [(i, i ^ 1) for i in range(sections)])  4.03 us
    pallas_call x11, Pallas kernels, call(): pl.pallas_call(functools.partial(kernel, slots, nv), out_shape=outs, in_s...  3.29 us
    pallas_call x1, Pallas kernels, local(): pl.pallas_call(maps_kernel, out_shape=(half_shape, half_shape, in_vmem(bl...  3.16 us
  transfers between devices with their start and end apart: 16, of which 6 were waited for; matrix products, arithmetic and copies ran while one was open for 0% of the time, Pallas kernels for 7%

profile of v3, /device:TPU:409, one launch (start us, length us, event | category | flops | bytes accessed | tf_op | source)
XLA Modules:
  0.0 69.5 jit_solution(10191834634002300133)
XLA Ops:
  0.0 0.9 %slice_bitcast_fusion = (bf16[1,8,32,128]{3,2,1,0:T(8,128)(2,1)S(1)}, bf16[1,8,32,128]{3,2,1,0:T(8,128)(2,1)S(1)}) fusion(bf16[1,4,8,32,128]{4,3,2,1,0:T(8,128)(2,1)} %prev_hbm.1), kind=kLoop, calls=%fused_computation.1 | loop fusion | bytes 262144 | tf_op jit(solution)/shard_map/squeeze | solution.py:286
  0.9 4.6 %collective-permute-start.1 = (bf16[1,8,32,128]{3,2,1,0:T(8,128)(2,1)S(1)}, bf16[1,8,32,128]{3,2,1,0:T(8,128)(2,1)S(1)}, u32[]{:S(2)}, u32[]{:S(2)}) collective-permute-start(bf16[1,8,32,128]{3,2,1,0:T(8,128)(2,1)S(1)} %get-tuple-element.55), channel_id=1, source_target_pairs={{1,0},{2,1},{3,2},{4,3},{5,4},{6,5},{7,6},{8,7},{9,8},{10,9},{11,1... | collective-permute-start | bytes 196616 | tf_op jit(solution)/shard_map/ppermute | solution.py:286
  5.5 1.9 %collective-permute-start = (bf16[1,8,32,128]{3,2,1,0:T(8,128)(2,1)S(1)}, bf16[1,8,32,128]{3,2,1,0:T(8,128)(2,1)S(1)}, u32[]{:S(2)}, u32[]{:S(2)}) collective-permute-start(bf16[1,8,32,128]{3,2,1,0:T(8,128)(2,1)S(1)} %get-tuple-element.56), channel_id=1, source_target_pairs={{0,1},{1,2},{2,3},{3,4},{4,5},{5,6},{6,7},{7,8},{8,9},{9,10},{10,1... | collective-permute-start | bytes 196616 | tf_op jit(solution)/shard_map/ppermute | solution.py:285
  8.0 3.2 %section_maps.1 = (bf16[2,1296,128]{2,1,0:T(8,128)(2,1)S(1)}, bf16[2,1296,128]{2,1,0:T(8,128)(2,1)S(1)}, bf16[4,8,128,128]{3,2,1,0:T(8,128)(2,1)S(1)}, f32[4,8,3...) custom-call(s32[1]{0:T(128)S(6)} %copy.13.widths_hbm, ...), custom_call_target="tpu_custom_call" | custom-call | flops 134217728 | bytes 2097152 | tf_op jit(solution)/shard_map/section_maps/pallas_call | solution.py:294
  11.2 0.0 collective-permute-done.1.above
  11.2 1.4 %collective-permute-done.below = bf16[1,8,32,128]{3,2,1,0:T(8,128)(2,1)S(1)} collective-permute-done((bf16[1,8,32,128]{3,2,1,0:T(8,128)(2,1)S(1)}, bf16[1,8,32,128]{3,2,1,0:T(8,128)(2,1)S(1)}, u32[]{:S(2)}, u32[]{:S(2)}) %collective-permute-start) | collective-permute-done | bytes 65568 | tf_op jit(solution)/shard_map/ppermute | solution.py:285
  12.6 0.4 section_edges.1
  12.9 4.0 %collective-permute-start.2 = (bf16[2,1296,128]{2,1,0:T(8,128)(2,1)S(1)}, bf16[2,1296,128]{2,1,0:T(8,128)(2,1)S(1)}, u32[]{:S(2)}, u32[]{:S(2)}) collective-permute-start(bf16[2,1296,128]{2,1,0:T(8,128)(2,1)S(1)} %get-tuple-element.37.send), channel_id=1, source_target_pairs={{0,16},{16,0},{32,48},{48,32},{64,80},{80,64},{96,112},{112,96},{1... | collective-permute-start | bytes 1990664 | tf_op jit(solution)/shard_map/ppermute | solution.py:344
  17.0 1.7 %collective-permute-done.2.recv = bf16[2,1296,128]{2,1,0:T(8,128)(2,1)S(1)} collective-permute-done((bf16[2,1296,128]{2,1,0:T(8,128)(2,1)S(1)}, bf16[2,1296,128]{2,1,0:T(8,128)(2,1)S(1)}, u32[]{:S(2)}, u32[]{:S(2)}) %collective-permute-start.2) | collective-permute-done | bytes 663584 | tf_op jit(solution)/shard_map/ppermute | solution.py:344
  18.7 0.4 compose_chip.1
  19.1 0.7 collective-permute-start.3
  19.7 0.7 collective-permute-start.6
  20.4 0.0 collective-permute-done.3.arrived
  20.4 0.3 first_group.1
  20.7 0.7 collective-permute-start.4
  21.4 0.7 collective-permute-start.5
  22.1 2.6 %collective-permute-start.8 = (bf16[1296,128]{1,0:T(8,128)(2,1)S(1)}, bf16[1296,128]{1,0:T(8,128)(2,1)S(1)}, u32[]{:S(2)}, u32[]{:S(2)}) collective-permute-start(bf16[1296,128]{1,0:T(8,128)(2,1)S(1)} %get-tuple-element.54.send), channel_id=1, source_target_pairs={{128,160},{144,176},{160,128},{176,144},{192,224},{208,240},{224,1... | collective-permute-start | bytes 995336 | tf_op jit(solution)/shard_map/ppermute | solution.py:350
  24.7 0.0 collective-permute-done.4.front
  24.7 0.0 collective-permute-done.5.back
  24.7 0.0 collective-permute-done.6.recv
  24.7 0.4 second_group.1
  25.2 0.7 collective-permute-start.7
  25.8 7.1 %collective-permute-done.8.recv = bf16[1296,128]{1,0:T(8,128)(2,1)S(1)} collective-permute-done((bf16[1296,128]{1,0:T(8,128)(2,1)S(1)}, bf16[1296,128]{1,0:T(8,128)(2,1)S(1)}, u32[]{:S(2)}, u32[]{:S(2)}) %collective-permute-start.8) | collective-permute-done | bytes 331808 | tf_op jit(solution)/shard_map/ppermute | solution.py:350
  33.0 0.3 compose_group.1.chain.group
  33.2 0.0 collective-permute-done.7.recv
  33.2 0.2 hop.4
  33.5 0.7 collective-permute-start.9
  34.1 0.0 collective-permute-done.9.recv
  34.1 0.2 hop.5
  34.3 0.7 collective-permute-start.10
  35.0 1.3 %collective-permute-start.12 = (bf16[1296,128]{1,0:T(8,128)(2,1)S(1)}, bf16[1296,128]{1,0:T(8,128)(2,1)S(1)}, u32[]{:S(2)}, u32[]{:S(2)}) collective-permute-start(bf16[1296,128]{1,0:T(8,128)(2,1)S(1)} %compose_group.1.chain.group), channel_id=1, source_target_pairs={{320,384},{336,400},{416,352},{432,368},{321,385},{337,401},{417,3... | collective-permute-start | bytes 995336 | tf_op jit(solution)/shard_map/ppermute | solution.py:342
  36.3 0.0 collective-permute-done.10.recv
  36.3 0.2 hop.6
  36.5 1.3 %collective-permute-start.11 = (bf16[8,32,128]{2,1,0:T(8,128)(2,1)S(1)}, bf16[8,32,128]{2,1,0:T(8,128)(2,1)S(1)}, u32[]{:S(2)}, u32[]{:S(2)}) collective-permute-start(bf16[8,32,128]{2,1,0:T(8,128)(2,1)S(1)} %get-tuple-element.50), channel_id=1, source_target_pairs={{256,384},{272,400},{288,352},{304,368},{257,385},{273,401},{289,3... | collective-permute-start | bytes 196616 | tf_op jit(solution)/shard_map/ppermute | solution.py:342
  37.8 0.7 collective-permute-start.15
  38.5 8.6 %collective-permute-done.12.recv.joined = bf16[1296,128]{1,0:T(8,128)(2,1)S(1)} collective-permute-done((bf16[1296,128]{1,0:T(8,128)(2,1)S(1)}, bf16[1296,128]{1,0:T(8,128)(2,1)S(1)}, u32[]{:S(2)}, u32[]{:S(2)}) %collective-permute-start.12) | collective-permute-done | bytes 331808 | tf_op jit(solution)/shard_map/ppermute | solution.py:342
  47.1 0.3 compose_join.1.chain
  47.4 1.8 %collective-permute-done.11.recv = bf16[8,32,128]{2,1,0:T(8,128)(2,1)S(1)} collective-permute-done((bf16[8,32,128]{2,1,0:T(8,128)(2,1)S(1)}, bf16[8,32,128]{2,1,0:T(8,128)(2,1)S(1)}, u32[]{:S(2)}, u32[]{:S(2)}) %collective-permute-start.11) | collective-permute-done | bytes 65568 | tf_op jit(solution)/shard_map/ppermute | solution.py:342
  49.2 0.2 hop.7
  49.4 0.2 fill.1
  49.6 1.3 %collective-permute-start.13 = (bf16[8,32,128]{2,1,0:T(8,128)(2,1)S(1)}, bf16[8,32,128]{2,1,0:T(8,128)(2,1)S(1)}, u32[]{:S(2)}, u32[]{:S(2)}) collective-permute-start(bf16[8,32,128]{2,1,0:T(8,128)(2,1)S(1)} %get-tuple-element.52), channel_id=1, source_target_pairs={{384,448},{400,464},{352,480},{368,496},{385,449},{401,465},{353,4... | collective-permute-start | bytes 196616 | tf_op jit(solution)/shard_map/ppermute | solution.py:342
  50.9 0.7 collective-permute-start.14
  51.6 0.0 collective-permute-done.15
  51.6 0.1 add_add_fusion.recv
  51.6 0.6 collective-permute-done.13.arrived
  52.2 0.0 collective-permute-done.14.filled
  52.2 0.6 share.1
  52.9 15.9 %all-gather = bf16[12,8,32,128]{3,2,1,0:T(8,128)(2,1)S(1)} all-gather(bf16[3,8,32,128]{3,2,1,0:T(8,128)(2,1)S(1)} %share.1), channel_id=2, replica_groups={{0,16,32,48},{64,80,96,112},{128,144,160,176},{192,208,224,240},{256,27..., dimensions={0}, use_global_device_ids=true | all-gather | bytes 983040 | tf_op jit(solution)/shard_map/all_gather | solution.py:377
  68.7 0.7 %finish.1 = bf16[1,4,8,32,128]{4,3,2,1,0:T(8,128)(2,1)} custom-call(bf16[4,3,8,32,128]{4,3,2,1,0:T(8,128)(2,1)S(1)} %bitcast.5, bf16[2,1296,128]{2,1,0:T(8,128)(2,1)S(1)} %get-tuple-element.36.keep, bf16[2,1296,128]{2,1,0:T(8,128)(2,1)S(1)} %get-tuple-element.37.send), custom_call_target="tpu_custom_call" | custom-call | tf_op jit(solution)/shard_map/finish/pallas_call | solution.py:380
Async XLA Ops:
  0.9 10.3 %collective-permute-start.1 = (bf16[1,8,32,128]{3,2,1,0:T(8,128)(2,1)S(1)}, bf16[1,8,32,128]{3,2,1,0:T(8,128)(2,1)S(1)}, u32[]{:S(2)}, u32[]{:S(2)}) collective-permute-start(bf16[1,8,32,128]{3,2,1,0:T(8,128)(2,1)S(1)} %get-tuple-element.55), channel_id=1, source_target_pairs={{1,0},{2,1},{3,2},{4,3},{5,4},{6,5},{7,6},{8,7},{9,8},{10,9},{11,1... | collective-permute-start | bytes 196616 | tf_op jit(solution)/shard_map/ppermute | solution.py:286
  5.5 7.1 %collective-permute-start = (bf16[1,8,32,128]{3,2,1,0:T(8,128)(2,1)S(1)}, bf16[1,8,32,128]{3,2,1,0:T(8,128)(2,1)S(1)}, u32[]{:S(2)}, u32[]{:S(2)}) collective-permute-start(bf16[1,8,32,128]{3,2,1,0:T(8,128)(2,1)S(1)} %get-tuple-element.56), channel_id=1, source_target_pairs={{0,1},{1,2},{2,3},{3,4},{4,5},{5,6},{6,7},{7,8},{8,9},{9,10},{10,1... | collective-permute-start | bytes 196616 | tf_op jit(solution)/shard_map/ppermute | solution.py:285
  12.9 5.7 %collective-permute-start.2 = (bf16[2,1296,128]{2,1,0:T(8,128)(2,1)S(1)}, bf16[2,1296,128]{2,1,0:T(8,128)(2,1)S(1)}, u32[]{:S(2)}, u32[]{:S(2)}) collective-permute-start(bf16[2,1296,128]{2,1,0:T(8,128)(2,1)S(1)} %get-tuple-element.37.send), channel_id=1, source_target_pairs={{0,16},{16,0},{32,48},{48,32},{64,80},{80,64},{96,112},{112,96},{1... | collective-permute-start | bytes 1990664 | tf_op jit(solution)/shard_map/ppermute | solution.py:344
  19.1 1.4 %collective-permute-start.3 = (bf16[2,8,32,128]{3,2,1,0:T(8,128)(2,1)S(1)}, bf16[2,8,32,128]{3,2,1,0:T(8,128)(2,1)S(1)}, u32[]{:S(2)}, u32[]{:S(2)}) collective-permute-start(bf16[2,8,32,128]{3,2,1,0:T(8,128)(2,1)S(1)} %get-tuple-element.39), channel_id=1, source_target_pairs={{0,32},{16,48},{1,33},{17,49},{2,34},{18,50},{3,35},{19,51},{4,36}... | collective-permute-start | bytes 393224 | tf_op jit(solution)/shard_map/ppermute | solution.py:348
  19.7 5.0 %collective-permute-start.6 = (bf16[1296,128]{1,0:T(8,128)(2,1)S(1)}, bf16[1296,128]{1,0:T(8,128)(2,1)S(1)}, u32[]{:S(2)}, u32[]{:S(2)}) collective-permute-start(bf16[1296,128]{1,0:T(8,128)(2,1)S(1)} %get-tuple-element.54.send), channel_id=1, source_target_pairs={{64,96},{80,112},{96,64},{112,80},{65,97},{81,113},{97,65},{113,81... | collective-permute-start | bytes 995336 | tf_op jit(solution)/shard_map/ppermute | solution.py:349
  20.7 4.0 %collective-permute-start.4 = (bf16[8,32,128]{2,1,0:T(8,128)(2,1)S(1)}, bf16[8,32,128]{2,1,0:T(8,128)(2,1)S(1)}, u32[]{:S(2)}, u32[]{:S(2)}) collective-permute-start(bf16[8,32,128]{2,1,0:T(8,128)(2,1)S(1)} %get-tuple-element.41), channel_id=1, source_target_pairs={{32,64},{48,80},{33,65},{49,81},{34,66},{50,82},{35,67},{51,83},{3... | collective-permute-start | bytes 196616 | tf_op jit(solution)/shard_map/ppermute | solution.py:353
  21.4 3.3 %collective-permute-start.5 = (bf16[8,32,128]{2,1,0:T(8,128)(2,1)S(1)}, bf16[8,32,128]{2,1,0:T(8,128)(2,1)S(1)}, u32[]{:S(2)}, u32[]{:S(2)}) collective-permute-start(bf16[8,32,128]{2,1,0:T(8,128)(2,1)S(1)} %get-tuple-element.42), channel_id=1, source_target_pairs={{32,96},{48,112},{33,97},{49,113},{34,98},{50,114},{35,99},{51,115... | collective-permute-start | bytes 196616 | tf_op jit(solution)/shard_map/ppermute | solution.py:352
  22.1 10.9 %collective-permute-start.8 = (bf16[1296,128]{1,0:T(8,128)(2,1)S(1)}, bf16[1296,128]{1,0:T(8,128)(2,1)S(1)}, u32[]{:S(2)}, u32[]{:S(2)}) collective-permute-start(bf16[1296,128]{1,0:T(8,128)(2,1)S(1)} %get-tuple-element.54.send), channel_id=1, source_target_pairs={{128,160},{144,176},{160,128},{176,144},{192,224},{208,240},{224,1... | collective-permute-start | bytes 995336 | tf_op jit(solution)/shard_map/ppermute | solution.py:350
  25.2 8.1 %collective-permute-start.7 = (bf16[8,32,128]{2,1,0:T(8,128)(2,1)S(1)}, bf16[8,32,128]{2,1,0:T(8,128)(2,1)S(1)}, u32[]{:S(2)}, u32[]{:S(2)}) collective-permute-start(bf16[8,32,128]{2,1,0:T(8,128)(2,1)S(1)} %get-tuple-element.43), channel_id=1, source_target_pairs={{64,128},{80,144},{96,160},{112,176},{65,129},{81,145},{97,161},{1... | collective-permute-start | bytes 196616 | tf_op jit(solution)/shard_map/ppermute | solution.py:342
  33.5 0.7 collective-permute-start.9
  34.3 2.0 %collective-permute-start.10 = (bf16[8,32,128]{2,1,0:T(8,128)(2,1)S(1)}, bf16[8,32,128]{2,1,0:T(8,128)(2,1)S(1)}, u32[]{:S(2)}, u32[]{:S(2)}) collective-permute-start(bf16[8,32,128]{2,1,0:T(8,128)(2,1)S(1)} %get-tuple-element.48), channel_id=1, source_target_pairs={{192,256},{208,272},{224,288},{240,304},{193,257},{209,273},{225,2... | collective-permute-start | bytes 196616 | tf_op jit(solution)/shard_map/ppermute | solution.py:342
  35.0 12.1 %collective-permute-start.12 = (bf16[1296,128]{1,0:T(8,128)(2,1)S(1)}, bf16[1296,128]{1,0:T(8,128)(2,1)S(1)}, u32[]{:S(2)}, u32[]{:S(2)}) collective-permute-start(bf16[1296,128]{1,0:T(8,128)(2,1)S(1)} %compose_group.1.chain.group), channel_id=1, source_target_pairs={{320,384},{336,400},{416,352},{432,368},{321,385},{337,401},{417,3... | collective-permute-start | bytes 995336 | tf_op jit(solution)/shard_map/ppermute | solution.py:342
  36.5 12.6 %collective-permute-start.11 = (bf16[8,32,128]{2,1,0:T(8,128)(2,1)S(1)}, bf16[8,32,128]{2,1,0:T(8,128)(2,1)S(1)}, u32[]{:S(2)}, u32[]{:S(2)}) collective-permute-start(bf16[8,32,128]{2,1,0:T(8,128)(2,1)S(1)} %get-tuple-element.50), channel_id=1, source_target_pairs={{256,384},{272,400},{288,352},{304,368},{257,385},{273,401},{289,3... | collective-permute-start | bytes 196616 | tf_op jit(solution)/shard_map/ppermute | solution.py:342
  37.8 13.7 %collective-permute-start.15 = (bf16[1296,128]{1,0:T(8,128)(2,1)S(1)}, bf16[1296,128]{1,0:T(8,128)(2,1)S(1)}, u32[]{:S(2)}, u32[]{:S(2)}) collective-permute-start(bf16[1296,128]{1,0:T(8,128)(2,1)S(1)} %get-tuple-element.54.send), channel_id=1, source_target_pairs={{0,32},{16,48},{32,0},{48,16},{1,33},{17,49},{33,1},{49,17},{2,34}... | collective-permute-start | bytes 995336 | tf_op jit(solution)/shard_map/ppermute | solution.py:366
  49.6 2.6 %collective-permute-start.13 = (bf16[8,32,128]{2,1,0:T(8,128)(2,1)S(1)}, bf16[8,32,128]{2,1,0:T(8,128)(2,1)S(1)}, u32[]{:S(2)}, u32[]{:S(2)}) collective-permute-start(bf16[8,32,128]{2,1,0:T(8,128)(2,1)S(1)} %get-tuple-element.52), channel_id=1, source_target_pairs={{384,448},{400,464},{352,480},{368,496},{385,449},{401,465},{353,4... | collective-permute-start | bytes 196616 | tf_op jit(solution)/shard_map/ppermute | solution.py:342
  50.9 1.3 %collective-permute-start.14 = (bf16[8,32,128]{2,1,0:T(8,128)(2,1)S(1)}, bf16[8,32,128]{2,1,0:T(8,128)(2,1)S(1)}, u32[]{:S(2)}, u32[]{:S(2)}) collective-permute-start(bf16[8,32,128]{2,1,0:T(8,128)(2,1)S(1)} %fill.1), channel_id=1, source_target_pairs={{256,320},{272,336},{352,416},{368,432},{257,321},{273,337},{353,4... | collective-permute-start | bytes 196616 | tf_op jit(solution)/shard_map/ppermute | solution.py:342

commit v4 on v3

--- a/solution.py
+++ b/solution.py
@@ -13,7 +13,7 @@
 ANY = pl.BlockSpec(memory_space=pl.ANY)
 STEP = 4_600_000_000
 PAD = 16
-JOINED = (5, 6)
+JOINED = (4, 5)
 
 
 def pin(x):
@@ -51,6 +51,20 @@
 
 def back_half(chip, group):
     return jnp.logical_and(chip == 1, group == JOINED[0])
+
+
+def last_group(group):
+    return group == lax.div(lax.axis_size("stream"), 4) - 1
+
+
+def outer_kernel(prev, last, first, sem):
+    slabs = prev.shape[1]
+    copies = [pltpu.make_async_copy(prev.at[0, pl.ds(slabs - 1, 1)], last, sem.at[0]),
+              pltpu.make_async_copy(prev.at[0, pl.ds(0, 1)], first, sem.at[1])]
+    for copy in copies:
+        copy.start()
+    for copy in copies:
+        copy.wait()
 
 
 def maps_kernel(widths_hbm, rhs_hbm, prev_hbm, u_hbm, d_hbm, lower_hbm, upper_hbm, index_hbm, keep, send, d, partial,
@@ -169,6 +183,16 @@
         out[k] = (y + m[pl.ds(k * step, nv), :].astype(F32)).astype(BF16)
 
 
+def rest_kernel(slots, nv, even, odd, out, scratch):
+    core, _, _ = place()
+    half, _, nb = out.shape
+
+    @pl.when(core == 1)
+    def _():
+        for j in range(half):
+            compose(even.at[j], odd.at[j], out.at[j], scratch, slots, nv, nb)
+
+
 def first_kernel(slots, nv, arrived, keep, send, out_front, out_back, scratch):
     nb = keep.shape[-1]
     apply_map(arrived.at[0], send, out_front, scratch, slots, nv, nb)
@@ -226,50 +250,45 @@
             apply_map(inflow, maps, out, scratch, slots, nv, group.shape[-1])
 
 
-def share_kernel(slots, nv, arrived, filled, inflow, joined, keep, recv, out, total, middle, scratch):
+def share_kernel(slots, nv, arrived, passed, filled, inflow, joined, before_last, keep, recv, out, total, middle, scratch):
     _, chip, number = place()
     nb = keep.shape[-1]
-    total[...] = inflow[...] + arrived[...] + filled[...]
-
-    @pl.when(front_half(chip, number))
-    def _():
-        apply_map(total, joined, middle, scratch, slots, nv, nb)
-        total[...] = middle[...]
+    total[...] = inflow[...] + arrived[...] + passed[...] + filled[...]
+
+    for condition, maps in ((front_half(chip, number), joined), (last_group(number), before_last)):
+        @pl.when(condition)
+        def _():
+            apply_map(total, maps, middle, scratch, slots, nv, nb)
+            total[...] = middle[...]
 
     out[0] = total[...]
-    for here, lo, hi in ((0, keep, recv), (1, recv, keep)):
+    for here, lo in ((0, keep), (1, recv)):
         @pl.when(chip == here)
         def _():
-            apply_map(total, lo, middle, scratch, slots, nv, nb)
-            out[1] = middle[...]
-            apply_map(middle, hi, out.at[2], scratch, slots, nv, nb)
-
-
-def finish_kernel(slots, nv, shared, keep, send, out, result, scratch, sem):
+            apply_map(total, lo, out.at[1], scratch, slots, nv, nb)
+
+
+def finish_kernel(slots, nv, shared, keep, send, rest, pair_keep, pair_send, out, result, scratch, sem):
     core, chip, _ = place()
-    slabs = out.shape[1]
+    slabs, nb = out.shape[1], out.shape[-1]
     half = slabs // 2
-    nb = out.shape[-1]
-    owners = [2 * (m % 2) + m // 2 for m in range(slabs)]
-
-    @pl.when(core == 1)
-    def _():
-        copies = [pltpu.make_async_copy(shared.at[owners[m], 1 + chip], out.at[0, m], sem.at[m]) for m in range(slabs)]
-        for copy in copies:
-            copy.start()
-        for copy in copies:
-            copy.wait()
-
-    @pl.when(core == 0)
-    def _():
-        copies = []
-        for m in range(slabs):
-            maps = keep if m < half else send
-            apply_map(shared.at[owners[m], chip], maps.at[m % half], result.at[m], scratch, slots, nv, nb)
-            copies.append(pltpu.make_async_copy(result.at[m], out.at[0, m], sem.at[m]))
-            copies[-1].start()
-        for copy in copies:
-            copy.wait()
+    even = [(keep if m < half else send).at[m % half] for m in range(slabs)]
+    odd = [rest.at[m] for m in range(half)]
+    for condition, maps in (
+        (core == 0, even),
+        (jnp.logical_and(core == 1, chip == 0), [*odd, pair_keep, pair_send]),
+        (jnp.logical_and(core == 1, chip == 1), [*odd, pair_send, pair_keep]),
+    ):
+        @pl.when(condition)
+        def _():
+            copies = []
+            for m in range(slabs):
+                x = shared.at[2 * (m % 2) + m // 2, chip]
+                apply_map(x, maps[m], result.at[m], scratch, slots, nv, nb)
+                copies.append(pltpu.make_async_copy(result.at[m], out.at[0, m], sem.at[m]))
+                copies[-1].start()
+            for copy in copies:
+                copy.wait()
 
 
 def local(rhs, previous, inverse_blocks, upstream_blocks, lower_gain, upper_gain, widths, upstream_index):
@@ -277,13 +296,23 @@
     half = slabs // 2
     sections, peers = lax.axis_size("stream"), lax.axis_size("span")
     groups = sections // 4
-    assert groups == JOINED[1] + 2
+    assert groups > JOINED[1] + 2
     rows = slots * (nv + nb) + PAD
 
     up = [(i, i + 1) for i in range(peers - 1)]
     down = [(j, i) for i, j in up]
-    below = lax.ppermute(previous[0, slabs - 1 :], "span", up)
-    above = lax.ppermute(previous[0, :1], "span", down)
+    edge_shape = in_vmem((1, slots, nv, nb))
+    last_slab, first_slab = pl.pallas_call(
+        outer_kernel,
+        out_shape=(edge_shape, edge_shape),
+        in_specs=[ANY],
+        out_specs=(VMEM, VMEM),
+        scratch_shapes=[pltpu.SemaphoreType.DMA((2,))],
+        compiler_params=params(),
+        name="outer_slabs",
+    )(in_hbm(previous))
+    below = lax.ppermute(last_slab, "span", up)
+    above = lax.ppermute(first_slab, "span", down)
 
     half_shape = in_vmem((half, rows, nb))
     one_shape = in_vmem((rows, nb))
@@ -356,23 +385,33 @@
     arrived = stream(state, (0, 1, 2), (1, 1, 2))
     group = call(group_kernel, one_shape, "compose_group", pair_keep, recv_later, flops=STEP)
 
+    keep_again, state = lax.optimization_barrier((keep, state))
+    even = lax.ppermute(keep_again, "stream", [(i, i + 1) for i in range(0, sections, 2)])
+    rest = call(rest_kernel, half_shape, "compose_rest", even, send, flops=STEP)
+
     a, b = JOINED
+    last = groups - 1
     join_recv = stream(group, (0, a, b), (1, b, a))
-    for g in range(2, a):
-        state, inflow = call(hop_kernel, (vec_shape, vec_shape), "hop", arrived, group, inflow, flops=STEP)
-        arrived = stream(state, (0, g, g + 1 if g + 1 < a else b), (1, g, g + 1))
-        if g == 2:
-            pair_send, arrived = lax.optimization_barrier((pair_send, arrived))
-            recv_first = lax.ppermute(pair_send, "stream", [(i, i ^ 2) for i in range(4)])
+    last_recv = stream(group, (0, last - 1, last), (1, last - 1, last))
     chain = call(join_kernel, one_shape, "compose_join", group, join_recv)
-    state, inflow = call(hop_kernel, (vec_shape, vec_shape), "hop", arrived, chain, inflow, flops=STEP)
-    arrived = stream(state, (0, b, b + 1), (1, a, b + 1))
-    passed = call(fill_kernel, vec_shape, "fill", inflow, chain, group)
-    filled = stream(passed, (0, a - 1, a), (1, a, b))
+    chain, rest = lax.optimization_barrier((chain, rest))
+    steps = [(2, 2), *((g, g) for g in range(3, a)), (b, a), *((g, g) for g in range(b + 1, last - 1))]
+    for step, (front, back) in enumerate(steps):
+        maps = group if front < a else chain
+        state, inflow = call(hop_kernel, (vec_shape, vec_shape), "hop", arrived, maps, inflow, flops=STEP)
+        if step + 1 < len(steps):
+            arrived = stream(state, (0, front, steps[step + 1][0]), (1, back, steps[step + 1][1]))
+        else:
+            arrived = stream(state, (0, front, last), (1, back, last))
+            passed = stream(state, (0, front, last - 1), (1, back, last - 1))
+        if step == 0:
+            pair_send_later, arrived = lax.optimization_barrier((pair_send, arrived))
+            recv_first = lax.ppermute(pair_send_later, "stream", [(i, i ^ 2) for i in range(4)])
+    filled = stream(call(fill_kernel, vec_shape, "fill", inflow, chain, group), (0, a - 1, a), (1, a, b))
 
     shares = call(
-        share_kernel, in_vmem((3, slots, nv, nb)), "share",
-        arrived, filled, inflow, join_recv, pair_keep, recv_first + recv_second + recv_later,
+        share_kernel, in_vmem((2, slots, nv, nb)), "share",
+        arrived, passed, filled, inflow, join_recv, last_recv, pair_keep, recv_first + recv_second + recv_later,
         scratch=(vec_shape, vec_shape))
     shared = lax.all_gather(
         shares, "stream", axis_index_groups=[[4 * g + r for r in range(4)] for g in range(groups)]
@@ -380,7 +419,7 @@
     return pl.pallas_call(
         functools.partial(finish_kernel, slots, nv),
         out_shape=jax.ShapeDtypeStruct(rhs.shape, BF16),
-        in_specs=[VMEM, VMEM, VMEM],
+        in_specs=[VMEM] * 6,
         out_specs=ANY,
         scratch_shapes=[
             pltpu.VMEM((slabs, slots, nv, nb), BF16),
@@ -389,7 +428,7 @@
         ],
         compiler_params=params(),
         name="finish",
-    )(pin(shared), pin(keep), pin(send))
+    )(*(pin(x) for x in (shared, keep, send, rest, pair_keep, pair_send)))
 
 
 def solution(mesh):

time: 69.9 us -> 66.3 us (0.948)
  the two profiles are of different devices: /device:TPU:409 before, /device:TPU:489 now
where the time goes in v4:
time: 66.3 us; the launch traced here: 65.9 us
  starting transfers between devices  24.4 us (37%)
  waiting for transfers between devices  21.9 us (33%)
  blocking collectives  9.96 us (15%)
  Pallas kernels  8.61 us (13%)
  between operations  0.94 us (1%)
    ppermute x8, waiting for transfers between devices, stream(): return lax.ppermute(x, 'stream', pairs)  14.3 us
    all_gather x1, blocking collectives, local(): lax.all_gather(shares, 'stream', axis_index_groups=[[4 * g + r for r in r...  9.96 us
    ppermute x8, starting transfers between devices, stream(): return lax.ppermute(x, 'stream', pairs)  6.58 us
    ppermute x1, waiting for transfers between devices, local(): lax.ppermute(pair_send, 'stream', [(i, i ^ 2) for i in range(8, sections)])  5.84 us
    ppermute x1, starting transfers between devices, local(): above = lax.ppermute(first_slab, 'span', down)  4.27 us
    pallas_call x1, Pallas kernels, local(): pl.pallas_call(maps_kernel, out_shape=(half_shape, half_shape, in_vmem(bl...  3.16 us
    ppermute x1, starting transfers between devices, local(): recv = lax.ppermute(send, 'stream', [(i, i ^ 1) for i in range(sections)])  3.15 us
    ppermute x1, starting transfers between devices, local(): below = lax.ppermute(last_slab, 'span', up)  3.12 us
  transfers between devices with their start and end apart: 18, of which 3 were waited for; matrix products, arithmetic and copies ran while one was open for 0% of the time, Pallas kernels for 8%

profile of v4, /device:TPU:489, one launch (start us, length us, event | category | flops | bytes accessed | tf_op | source)
XLA Modules:
  0.0 65.9 jit_solution(17756112169959671402)
XLA Ops:
  0.0 0.9 %outer_slabs.1 = (bf16[1,8,32,128]{3,2,1,0:T(8,128)(2,1)S(1)}, bf16[1,8,32,128]{3,2,1,0:T(8,128)(2,1)S(1)}) custom-call(bf16[1,4,8,32,128]{4,3,2,1,0:T(8,128)(2,1)} %prev_hbm.1), custom_call_target="tpu_custom_call" | custom-call | tf_op jit(solution)/shard_map/outer_slabs/pallas_call | solution.py:305
  0.9 3.1 %collective-permute-start = (bf16[1,8,32,128]{3,2,1,0:T(8,128)(2,1)S(1)}, bf16[1,8,32,128]{3,2,1,0:T(8,128)(2,1)S(1)}, u32[]{:S(2)}, u32[]{:S(2)}) collective-permute-start(bf16[1,8,32,128]{3,2,1,0:T(8,128)(2,1)S(1)} %get-tuple-element.33), channel_id=1, source_target_pairs={{0,1},{1,2},{2,3},{3,4},{4,5},{5,6},{6,7},{7,8},{8,9},{9,10},{10,1... | collective-permute-start | bytes 196616 | tf_op jit(solution)/shard_map/ppermute | solution.py:314
  4.0 4.3 %collective-permute-start.1 = (bf16[1,8,32,128]{3,2,1,0:T(8,128)(2,1)S(1)}, bf16[1,8,32,128]{3,2,1,0:T(8,128)(2,1)S(1)}, u32[]{:S(2)}, u32[]{:S(2)}) collective-permute-start(bf16[1,8,32,128]{3,2,1,0:T(8,128)(2,1)S(1)} %get-tuple-element.34), channel_id=1, source_target_pairs={{1,0},{2,1},{3,2},{4,3},{5,4},{6,5},{7,6},{8,7},{9,8},{10,9},{11,1... | collective-permute-start | bytes 196616 | tf_op jit(solution)/shard_map/ppermute | solution.py:315
  8.9 3.2 %section_maps.1 = (bf16[2,1296,128]{2,1,0:T(8,128)(2,1)S(1)}, bf16[2,1296,128]{2,1,0:T(8,128)(2,1)S(1)}, bf16[4,8,128,128]{3,2,1,0:T(8,128)(2,1)S(1)}, f32[4,8,3...) custom-call(s32[1]{0:T(128)S(6)} %copy.13.widths_hbm, ...), custom_call_target="tpu_custom_call" | custom-call | flops 134217728 | bytes 2097152 | tf_op jit(solution)/shard_map/section_maps/pallas_call | solution.py:323
  12.1 0.0 collective-permute-done.below
  12.1 0.0 collective-permute-done.1.above
  12.1 0.4 section_edges.1
  12.5 3.2 %collective-permute-start.2 = (bf16[2,1296,128]{2,1,0:T(8,128)(2,1)S(1)}, bf16[2,1296,128]{2,1,0:T(8,128)(2,1)S(1)}, u32[]{:S(2)}, u32[]{:S(2)}) collective-permute-start(bf16[2,1296,128]{2,1,0:T(8,128)(2,1)S(1)} %get-tuple-element.42.odd.send), channel_id=1, source_target_pairs={{0,16},{16,0},{32,48},{48,32},{64,80},{80,64},{96,112},{112,96},{1... | collective-permute-start | bytes 1990664 | tf_op jit(solution)/shard_map/ppermute | solution.py:373
  15.7 1.7 %collective-permute-done.2.recv = bf16[2,1296,128]{2,1,0:T(8,128)(2,1)S(1)} collective-permute-done((bf16[2,1296,128]{2,1,0:T(8,128)(2,1)S(1)}, bf16[2,1296,128]{2,1,0:T(8,128)(2,1)S(1)}, u32[]{:S(2)}, u32[]{:S(2)}) %collective-permute-start.2) | collective-permute-done | bytes 663584 | tf_op jit(solution)/shard_map/ppermute | solution.py:373
  17.4 0.4 compose_chip.1
  17.8 0.7 %collective-permute-start.3 = (bf16[2,8,32,128]{3,2,1,0:T(8,128)(2,1)S(1)}, bf16[2,8,32,128]{3,2,1,0:T(8,128)(2,1)S(1)}, u32[]{:S(2)}, u32[]{:S(2)}) collective-permute-start(bf16[2,8,32,128]{3,2,1,0:T(8,128)(2,1)S(1)} %get-tuple-element.44), channel_id=1, source_target_pairs={{0,32},{16,48},{1,33},{17,49},{2,34},{18,50},{3,35},{19,51},{4,36}... | collective-permute-start | bytes 393224 | tf_op jit(solution)/shard_map/ppermute | solution.py:377
  18.4 0.7 %collective-permute-start.6 = (bf16[1296,128]{1,0:T(8,128)(2,1)S(1)}, bf16[1296,128]{1,0:T(8,128)(2,1)S(1)}, u32[]{:S(2)}, u32[]{:S(2)}) collective-permute-start(bf16[1296,128]{1,0:T(8,128)(2,1)S(1)} %get-tuple-element.59.send.pair_send), channel_id=1, source_target_pairs={{64,96},{80,112},{96,64},{112,80},{65,97},{81,113},{97,65},{113,81... | collective-permute-start | bytes 995336 | tf_op jit(solution)/shard_map/ppermute | solution.py:378
  19.1 0.0 collective-permute-done.3.arrived
  19.1 0.3 first_group.1
  19.4 0.7 %collective-permute-start.4 = (bf16[8,32,128]{2,1,0:T(8,128)(2,1)S(1)}, bf16[8,32,128]{2,1,0:T(8,128)(2,1)S(1)}, u32[]{:S(2)}, u32[]{:S(2)}) collective-permute-start(bf16[8,32,128]{2,1,0:T(8,128)(2,1)S(1)} %get-tuple-element.46), channel_id=1, source_target_pairs={{32,64},{48,80},{33,65},{49,81},{34,66},{50,82},{35,67},{51,83},{3... | collective-permute-start | bytes 196616 | tf_op jit(solution)/shard_map/ppermute | solution.py:382
  20.1 0.7 %collective-permute-start.5 = (bf16[8,32,128]{2,1,0:T(8,128)(2,1)S(1)}, bf16[8,32,128]{2,1,0:T(8,128)(2,1)S(1)}, u32[]{:S(2)}, u32[]{:S(2)}) collective-permute-start(bf16[8,32,128]{2,1,0:T(8,128)(2,1)S(1)} %get-tuple-element.47), channel_id=1, source_target_pairs={{32,96},{48,112},{33,97},{49,113},{34,98},{50,114},{35,99},{51,115... | collective-permute-start | bytes 196616 | tf_op jit(solution)/shard_map/ppermute | solution.py:381
  20.8 2.6 %collective-permute-start.8 = (bf16[1296,128]{1,0:T(8,128)(2,1)S(1)}, bf16[1296,128]{1,0:T(8,128)(2,1)S(1)}, u32[]{:S(2)}, u32[]{:S(2)}) collective-permute-start(bf16[1296,128]{1,0:T(8,128)(2,1)S(1)} %get-tuple-element.59.send.pair_send), channel_id=1, source_target_pairs={{128,160},{144,176},{160,128},{176,144},{192,224},{208,240},{224,1... | collective-permute-start | bytes 995336 | tf_op jit(solution)/shard_map/ppermute | solution.py:379
  23.4 0.0 collective-permute-done.4.front
  23.4 0.0 collective-permute-done.5.back
  23.4 0.0 collective-permute-done.6.recv
  23.4 0.4 second_group.1
  23.8 0.7 %collective-permute-start.7 = (bf16[8,32,128]{2,1,0:T(8,128)(2,1)S(1)}, bf16[8,32,128]{2,1,0:T(8,128)(2,1)S(1)}, u32[]{:S(2)}, u32[]{:S(2)}) collective-permute-start(bf16[8,32,128]{2,1,0:T(8,128)(2,1)S(1)} %get-tuple-element.48), channel_id=1, source_target_pairs={{64,128},{80,144},{96,160},{112,176},{65,129},{81,145},{97,161},{1... | collective-permute-start | bytes 196616 | tf_op jit(solution)/shard_map/ppermute | solution.py:371
  24.5 1.3 %collective-permute-start.12 = (bf16[2,1296,128]{2,1,0:T(8,128)(2,1)S(1)}, bf16[2,1296,128]{2,1,0:T(8,128)(2,1)S(1)}, u32[]{:S(2)}, u32[]{:S(2)}) collective-permute-start(bf16[2,1296,128]{2,1,0:T(8,128)(2,1)S(1)} %get-tuple-element.54.keep), channel_id=1, source_target_pairs={{0,16},{32,48},{64,80},{96,112},{128,144},{160,176},{192,208},{224... | collective-permute-start | bytes 1990664 | tf_op jit(solution)/shard_map/ppermute | solution.py:389
  25.8 5.8 %collective-permute-done.8.recv = bf16[1296,128]{1,0:T(8,128)(2,1)S(1)} collective-permute-done((bf16[1296,128]{1,0:T(8,128)(2,1)S(1)}, bf16[1296,128]{1,0:T(8,128)(2,1)S(1)}, u32[]{:S(2)}, u32[]{:S(2)}) %collective-permute-start.8) | collective-permute-done | bytes 331808 | tf_op jit(solution)/shard_map/ppermute | solution.py:379
  31.7 0.3 compose_group.1.chain.group
  31.9 0.0 collective-permute-done.7.recv
  31.9 0.2 hop.3
  32.2 0.7 %collective-permute-start.9 = (bf16[8,32,128]{2,1,0:T(8,128)(2,1)S(1)}, bf16[8,32,128]{2,1,0:T(8,128)(2,1)S(1)}, u32[]{:S(2)}, u32[]{:S(2)}) collective-permute-start(bf16[8,32,128]{2,1,0:T(8,128)(2,1)S(1)} %get-tuple-element.50), channel_id=1, source_target_pairs={{128,192},{144,208},{160,224},{176,240},{129,193},{145,209},{161,2... | collective-permute-start | bytes 196616 | tf_op jit(solution)/shard_map/ppermute | solution.py:371
  32.8 0.7 %collective-permute-start.11 = (bf16[1296,128]{1,0:T(8,128)(2,1)S(1)}, bf16[1296,128]{1,0:T(8,128)(2,1)S(1)}, u32[]{:S(2)}, u32[]{:S(2)}) collective-permute-start(bf16[1296,128]{1,0:T(8,128)(2,1)S(1)} %compose_group.1.chain.group), channel_id=1, source_target_pairs={{256,320},{272,336},{352,288},{368,304},{257,321},{273,337},{353,2... | collective-permute-start | bytes 995336 | tf_op jit(solution)/shard_map/ppermute | solution.py:371
  33.5 1.3 %collective-permute-start.16 = (bf16[1296,128]{1,0:T(8,128)(2,1)S(1)}, bf16[1296,128]{1,0:T(8,128)(2,1)S(1)}, u32[]{:S(2)}, u32[]{:S(2)}) collective-permute-start(bf16[1296,128]{1,0:T(8,128)(2,1)S(1)} %compose_group.1.chain.group), channel_id=1, source_target_pairs={{384,448},{400,464},{416,480},{432,496},{385,449},{401,465},{417,4... | collective-permute-start | bytes 995336 | tf_op jit(solution)/shard_map/ppermute | solution.py:371
  34.8 0.0 collective-permute-done.9.recv
  34.8 0.7 %collective-permute-start.17 = (bf16[1296,128]{1,0:T(8,128)(2,1)S(1)}, bf16[1296,128]{1,0:T(8,128)(2,1)S(1)}, u32[]{:S(2)}, u32[]{:S(2)}) collective-permute-start(bf16[1296,128]{1,0:T(8,128)(2,1)S(1)} %get-tuple-element.59.send.pair_send), channel_id=1, source_target_pairs={{0,32},{16,48},{32,0},{48,16},{1,33},{17,49},{33,1},{49,17},{2,34}... | collective-permute-start | bytes 995336 | tf_op jit(solution)/shard_map/ppermute | solution.py:409
  35.5 0.2 hop.4
  35.7 0.7 %collective-permute-start.10 = (bf16[8,32,128]{2,1,0:T(8,128)(2,1)S(1)}, bf16[8,32,128]{2,1,0:T(8,128)(2,1)S(1)}, u32[]{:S(2)}, u32[]{:S(2)}) collective-permute-start(bf16[8,32,128]{2,1,0:T(8,128)(2,1)S(1)} %get-tuple-element.53), channel_id=1, source_target_pairs={{192,320},{208,336},{224,288},{240,304},{193,321},{209,337},{225,2... | collective-permute-start | bytes 196616 | tf_op jit(solution)/shard_map/ppermute | solution.py:371
  36.4 0.0 collective-permute-done.11.recv.joined
  36.5 0.0 collective-permute-done.12.even
  36.5 0.4 compose_rest.1.rest
  36.9 0.0 collective-permute-done.10.recv
  36.9 0.2 hop.5
  37.1 1.3 %collective-permute-start.13 = (bf16[8,32,128]{2,1,0:T(8,128)(2,1)S(1)}, bf16[8,32,128]{2,1,0:T(8,128)(2,1)S(1)}, u32[]{:S(2)}, u32[]{:S(2)}) collective-permute-start(bf16[8,32,128]{2,1,0:T(8,128)(2,1)S(1)} %get-tuple-element.57), channel_id=1, source_target_pairs={{320,448},{336,464},{288,480},{304,496},{321,449},{337,465},{289,4... | collective-permute-start | bytes 196616 | tf_op jit(solution)/shard_map/ppermute | solution.py:371
  38.4 0.7 %collective-permute-start.14 = (bf16[8,32,128]{2,1,0:T(8,128)(2,1)S(1)}, bf16[8,32,128]{2,1,0:T(8,128)(2,1)S(1)}, u32[]{:S(2)}, u32[]{:S(2)}) collective-permute-start(bf16[8,32,128]{2,1,0:T(8,128)(2,1)S(1)} %get-tuple-element.57), channel_id=1, source_target_pairs={{320,384},{336,400},{288,416},{304,432},{321,385},{337,401},{289,4... | collective-permute-start | bytes 196616 | tf_op jit(solution)/shard_map/ppermute | solution.py:371
  39.0 0.2 fill.1
  39.3 0.7 %collective-permute-start.15 = (bf16[8,32,128]{2,1,0:T(8,128)(2,1)S(1)}, bf16[8,32,128]{2,1,0:T(8,128)(2,1)S(1)}, u32[]{:S(2)}, u32[]{:S(2)}) collective-permute-start(bf16[8,32,128]{2,1,0:T(8,128)(2,1)S(1)} %fill.1), channel_id=1, source_target_pairs={{192,256},{208,272},{288,352},{304,368},{193,257},{209,273},{289,3... | collective-permute-start | bytes 196616 | tf_op jit(solution)/shard_map/ppermute | solution.py:371
  39.9 0.0 collective-permute-done.17
  40.0 0.1 add_add_fusion.recv
  40.0 14.3 %collective-permute-done.16.before_last = bf16[1296,128]{1,0:T(8,128)(2,1)S(1)} collective-permute-done((bf16[1296,128]{1,0:T(8,128)(2,1)S(1)}, bf16[1296,128]{1,0:T(8,128)(2,1)S(1)}, u32[]{:S(2)}, u32[]{:S(2)}) %collective-permute-start.16) | collective-permute-done | bytes 331808 | tf_op jit(solution)/shard_map/ppermute | solution.py:371
  54.3 0.0 collective-permute-done.15.filled
  54.3 0.0 collective-permute-done.13.arrived
  54.3 0.0 collective-permute-done.14.passed
  54.3 0.5 share.1
  54.8 10.0 %all-gather = bf16[8,8,32,128]{3,2,1,0:T(8,128)(2,1)S(1)} all-gather(bf16[2,8,32,128]{3,2,1,0:T(8,128)(2,1)S(1)} %share.1), channel_id=2, replica_groups={{0,16,32,48},{64,80,96,112},{128,144,160,176},{192,208,224,240},{256,27..., dimensions={0}, use_global_device_ids=true | all-gather | bytes 655360 | tf_op jit(solution)/shard_map/all_gather | solution.py:416
  64.8 1.1 %finish.1 = bf16[1,4,8,32,128]{4,3,2,1,0:T(8,128)(2,1)} custom-call(bf16[4,2,8,32,128]{4,3,2,1,0:T(8,128)(2,1)S(1)} %bitcast.1, bf16[2,1296,128]{2,1,0:T(8,128)(2,1)S(1)} %get-tuple-element.54.keep, bf16[2,1296,128]{2,1,0:T(8,128)(2,1)S(1)} %get-tuple-element.42.odd.send, bf16[2,1296,128]{2,1,0:T(8,128)(2,1)S(1)} %compose_rest.1.rest, ...), custom_call_target="tpu_custom_call" | custom-call | tf_op jit(solution)/shard_map/finish/pallas_call | solution.py:419
  (1 shorter events, 0.0 us)
Async XLA Ops:
  0.9 11.2 %collective-permute-start = (bf16[1,8,32,128]{3,2,1,0:T(8,128)(2,1)S(1)}, bf16[1,8,32,128]{3,2,1,0:T(8,128)(2,1)S(1)}, u32[]{:S(2)}, u32[]{:S(2)}) collective-permute-start(bf16[1,8,32,128]{3,2,1,0:T(8,128)(2,1)S(1)} %get-tuple-element.33), channel_id=1, source_target_pairs={{0,1},{1,2},{2,3},{3,4},{4,5},{5,6},{6,7},{7,8},{8,9},{9,10},{10,1... | collective-permute-start | bytes 196616 | tf_op jit(solution)/shard_map/ppermute | solution.py:314
  4.0 8.1 %collective-permute-start.1 = (bf16[1,8,32,128]{3,2,1,0:T(8,128)(2,1)S(1)}, bf16[1,8,32,128]{3,2,1,0:T(8,128)(2,1)S(1)}, u32[]{:S(2)}, u32[]{:S(2)}) collective-permute-start(bf16[1,8,32,128]{3,2,1,0:T(8,128)(2,1)S(1)} %get-tuple-element.34), channel_id=1, source_target_pairs={{1,0},{2,1},{3,2},{4,3},{5,4},{6,5},{7,6},{8,7},{9,8},{10,9},{11,1... | collective-permute-start | bytes 196616 | tf_op jit(solution)/shard_map/ppermute | solution.py:315
  12.5 4.9 %collective-permute-start.2 = (bf16[2,1296,128]{2,1,0:T(8,128)(2,1)S(1)}, bf16[2,1296,128]{2,1,0:T(8,128)(2,1)S(1)}, u32[]{:S(2)}, u32[]{:S(2)}) collective-permute-start(bf16[2,1296,128]{2,1,0:T(8,128)(2,1)S(1)} %get-tuple-element.42.odd.send), channel_id=1, source_target_pairs={{0,16},{16,0},{32,48},{48,32},{64,80},{80,64},{96,112},{112,96},{1... | collective-permute-start | bytes 1990664 | tf_op jit(solution)/shard_map/ppermute | solution.py:373
  17.8 1.4 %collective-permute-start.3 = (bf16[2,8,32,128]{3,2,1,0:T(8,128)(2,1)S(1)}, bf16[2,8,32,128]{3,2,1,0:T(8,128)(2,1)S(1)}, u32[]{:S(2)}, u32[]{:S(2)}) collective-permute-start(bf16[2,8,32,128]{3,2,1,0:T(8,128)(2,1)S(1)} %get-tuple-element.44), channel_id=1, source_target_pairs={{0,32},{16,48},{1,33},{17,49},{2,34},{18,50},{3,35},{19,51},{4,36}... | collective-permute-start | bytes 393224 | tf_op jit(solution)/shard_map/ppermute | solution.py:377
  18.4 5.0 %collective-permute-start.6 = (bf16[1296,128]{1,0:T(8,128)(2,1)S(1)}, bf16[1296,128]{1,0:T(8,128)(2,1)S(1)}, u32[]{:S(2)}, u32[]{:S(2)}) collective-permute-start(bf16[1296,128]{1,0:T(8,128)(2,1)S(1)} %get-tuple-element.59.send.pair_send), channel_id=1, source_target_pairs={{64,96},{80,112},{96,64},{112,80},{65,97},{81,113},{97,65},{113,81... | collective-permute-start | bytes 995336 | tf_op jit(solution)/shard_map/ppermute | solution.py:378
  19.4 4.0 %collective-permute-start.4 = (bf16[8,32,128]{2,1,0:T(8,128)(2,1)S(1)}, bf16[8,32,128]{2,1,0:T(8,128)(2,1)S(1)}, u32[]{:S(2)}, u32[]{:S(2)}) collective-permute-start(bf16[8,32,128]{2,1,0:T(8,128)(2,1)S(1)} %get-tuple-element.46), channel_id=1, source_target_pairs={{32,64},{48,80},{33,65},{49,81},{34,66},{50,82},{35,67},{51,83},{3... | collective-permute-start | bytes 196616 | tf_op jit(solution)/shard_map/ppermute | solution.py:382
  20.1 3.3 %collective-permute-start.5 = (bf16[8,32,128]{2,1,0:T(8,128)(2,1)S(1)}, bf16[8,32,128]{2,1,0:T(8,128)(2,1)S(1)}, u32[]{:S(2)}, u32[]{:S(2)}) collective-permute-start(bf16[8,32,128]{2,1,0:T(8,128)(2,1)S(1)} %get-tuple-element.47), channel_id=1, source_target_pairs={{32,96},{48,112},{33,97},{49,113},{34,98},{50,114},{35,99},{51,115... | collective-permute-start | bytes 196616 | tf_op jit(solution)/shard_map/ppermute | solution.py:381
  20.8 10.9 %collective-permute-start.8 = (bf16[1296,128]{1,0:T(8,128)(2,1)S(1)}, bf16[1296,128]{1,0:T(8,128)(2,1)S(1)}, u32[]{:S(2)}, u32[]{:S(2)}) collective-permute-start(bf16[1296,128]{1,0:T(8,128)(2,1)S(1)} %get-tuple-element.59.send.pair_send), channel_id=1, source_target_pairs={{128,160},{144,176},{160,128},{176,144},{192,224},{208,240},{224,1... | collective-permute-start | bytes 995336 | tf_op jit(solution)/shard_map/ppermute | solution.py:379
  23.8 8.1 %collective-permute-start.7 = (bf16[8,32,128]{2,1,0:T(8,128)(2,1)S(1)}, bf16[8,32,128]{2,1,0:T(8,128)(2,1)S(1)}, u32[]{:S(2)}, u32[]{:S(2)}) collective-permute-start(bf16[8,32,128]{2,1,0:T(8,128)(2,1)S(1)} %get-tuple-element.48), channel_id=1, source_target_pairs={{64,128},{80,144},{96,160},{112,176},{65,129},{81,145},{97,161},{1... | collective-permute-start | bytes 196616 | tf_op jit(solution)/shard_map/ppermute | solution.py:371
  24.5 12.0 %collective-permute-start.12 = (bf16[2,1296,128]{2,1,0:T(8,128)(2,1)S(1)}, bf16[2,1296,128]{2,1,0:T(8,128)(2,1)S(1)}, u32[]{:S(2)}, u32[]{:S(2)}) collective-permute-start(bf16[2,1296,128]{2,1,0:T(8,128)(2,1)S(1)} %get-tuple-element.54.keep), channel_id=1, source_target_pairs={{0,16},{32,48},{64,80},{96,112},{128,144},{160,176},{192,208},{224... | collective-permute-start | bytes 1990664 | tf_op jit(solution)/shard_map/ppermute | solution.py:389
  32.2 2.7 %collective-permute-start.9 = (bf16[8,32,128]{2,1,0:T(8,128)(2,1)S(1)}, bf16[8,32,128]{2,1,0:T(8,128)(2,1)S(1)}, u32[]{:S(2)}, u32[]{:S(2)}) collective-permute-start(bf16[8,32,128]{2,1,0:T(8,128)(2,1)S(1)} %get-tuple-element.50), channel_id=1, source_target_pairs={{128,192},{144,208},{160,224},{176,240},{129,193},{145,209},{161,2... | collective-permute-start | bytes 196616 | tf_op jit(solution)/shard_map/ppermute | solution.py:371
  32.8 3.6 %collective-permute-start.11 = (bf16[1296,128]{1,0:T(8,128)(2,1)S(1)}, bf16[1296,128]{1,0:T(8,128)(2,1)S(1)}, u32[]{:S(2)}, u32[]{:S(2)}) collective-permute-start(bf16[1296,128]{1,0:T(8,128)(2,1)S(1)} %compose_group.1.chain.group), channel_id=1, source_target_pairs={{256,320},{272,336},{352,288},{368,304},{257,321},{273,337},{353,2... | collective-permute-start | bytes 995336 | tf_op jit(solution)/shard_map/ppermute | solution.py:371
  33.5 20.8 %collective-permute-start.16 = (bf16[1296,128]{1,0:T(8,128)(2,1)S(1)}, bf16[1296,128]{1,0:T(8,128)(2,1)S(1)}, u32[]{:S(2)}, u32[]{:S(2)}) collective-permute-start(bf16[1296,128]{1,0:T(8,128)(2,1)S(1)} %compose_group.1.chain.group), channel_id=1, source_target_pairs={{384,448},{400,464},{416,480},{432,496},{385,449},{401,465},{417,4... | collective-permute-start | bytes 995336 | tf_op jit(solution)/shard_map/ppermute | solution.py:371
  34.8 5.1 %collective-permute-start.17 = (bf16[1296,128]{1,0:T(8,128)(2,1)S(1)}, bf16[1296,128]{1,0:T(8,128)(2,1)S(1)}, u32[]{:S(2)}, u32[]{:S(2)}) collective-permute-start(bf16[1296,128]{1,0:T(8,128)(2,1)S(1)} %get-tuple-element.59.send.pair_send), channel_id=1, source_target_pairs={{0,32},{16,48},{32,0},{48,16},{1,33},{17,49},{33,1},{49,17},{2,34}... | collective-permute-start | bytes 995336 | tf_op jit(solution)/shard_map/ppermute | solution.py:409
  35.7 1.1 %collective-permute-start.10 = (bf16[8,32,128]{2,1,0:T(8,128)(2,1)S(1)}, bf16[8,32,128]{2,1,0:T(8,128)(2,1)S(1)}, u32[]{:S(2)}, u32[]{:S(2)}) collective-permute-start(bf16[8,32,128]{2,1,0:T(8,128)(2,1)S(1)} %get-tuple-element.53), channel_id=1, source_target_pairs={{192,320},{208,336},{224,288},{240,304},{193,321},{209,337},{225,2... | collective-permute-start | bytes 196616 | tf_op jit(solution)/shard_map/ppermute | solution.py:371
  37.1 17.3 %collective-permute-start.13 = (bf16[8,32,128]{2,1,0:T(8,128)(2,1)S(1)}, bf16[8,32,128]{2,1,0:T(8,128)(2,1)S(1)}, u32[]{:S(2)}, u32[]{:S(2)}) collective-permute-start(bf16[8,32,128]{2,1,0:T(8,128)(2,1)S(1)} %get-tuple-element.57), channel_id=1, source_target_pairs={{320,448},{336,464},{288,480},{304,496},{321,449},{337,465},{289,4... | collective-permute-start | bytes 196616 | tf_op jit(solution)/shard_map/ppermute | solution.py:371
  38.4 16.0 %collective-permute-start.14 = (bf16[8,32,128]{2,1,0:T(8,128)(2,1)S(1)}, bf16[8,32,128]{2,1,0:T(8,128)(2,1)S(1)}, u32[]{:S(2)}, u32[]{:S(2)}) collective-permute-start(bf16[8,32,128]{2,1,0:T(8,128)(2,1)S(1)} %get-tuple-element.57), channel_id=1, source_target_pairs={{320,384},{336,400},{288,416},{304,432},{321,385},{337,401},{289,4... | collective-permute-start | bytes 196616 | tf_op jit(solution)/shard_map/ppermute | solution.py:371
  39.3 15.1 %collective-permute-start.15 = (bf16[8,32,128]{2,1,0:T(8,128)(2,1)S(1)}, bf16[8,32,128]{2,1,0:T(8,128)(2,1)S(1)}, u32[]{:S(2)}, u32[]{:S(2)}) collective-permute-start(bf16[8,32,128]{2,1,0:T(8,128)(2,1)S(1)} %fill.1), channel_id=1, source_target_pairs={{192,256},{208,272},{288,352},{304,368},{193,257},{209,273},{289,3... | collective-permute-start | bytes 196616 | tf_op jit(solution)/shard_map/ppermute | solution.py:371

commit v5 on v4

--- a/solution.py
+++ b/solution.py
@@ -11,7 +11,7 @@
 BF16 = jnp.bfloat16
 VMEM = pl.BlockSpec(memory_space=pltpu.VMEM)
 ANY = pl.BlockSpec(memory_space=pl.ANY)
-STEP = 4_600_000_000
+STEP = 2_300_000_000
 PAD = 16
 JOINED = (4, 5)
 
@@ -385,7 +385,8 @@
     arrived = stream(state, (0, 1, 2), (1, 1, 2))
     group = call(group_kernel, one_shape, "compose_group", pair_keep, recv_later, flops=STEP)
 
-    keep_again, state = lax.optimization_barrier((keep, state))
+    keep_again, pair_send_again, state = lax.optimization_barrier((keep, pair_send, state))
+    recv_first = lax.ppermute(pair_send_again, "stream", [(i, i ^ 2) for i in range(4)])
     even = lax.ppermute(keep_again, "stream", [(i, i + 1) for i in range(0, sections, 2)])
     rest = call(rest_kernel, half_shape, "compose_rest", even, send, flops=STEP)
 
@@ -404,9 +405,6 @@
         else:
             arrived = stream(state, (0, front, last), (1, back, last))
             passed = stream(state, (0, front, last - 1), (1, back, last - 1))
-        if step == 0:
-            pair_send_later, arrived = lax.optimization_barrier((pair_send, arrived))
-            recv_first = lax.ppermute(pair_send_later, "stream", [(i, i ^ 2) for i in range(4)])
     filled = stream(call(fill_kernel, vec_shape, "fill", inflow, chain, group), (0, a - 1, a), (1, a, b))
 
     shares = call(

time: 66.3 us -> 64 us (0.965)
  the two profiles are of different devices: /device:TPU:489 before, /device:TPU:497 now
where the time goes in v5:
time: 64 us; the launch traced here: 63.6 us
  starting transfers between devices  24.4 us (38%)
  waiting for transfers between devices  20.7 us (32%)
  blocking collectives  8.88 us (14%)
  Pallas kernels  8.6 us (13%)
  between operations  0.94 us (1%)
    ppermute x8, waiting for transfers between devices, stream(): return lax.ppermute(x, 'stream', pairs)  14.7 us
    all_gather x1, blocking collectives, local(): lax.all_gather(shares, 'stream', axis_index_groups=[[4 * g + r for r in r...  8.88 us
    ppermute x8, starting transfers between devices, stream(): return lax.ppermute(x, 'stream', pairs)  6.58 us
    ppermute x1, starting transfers between devices, local(): above = lax.ppermute(first_slab, 'span', down)  4.27 us
    ppermute x1, waiting for transfers between devices, local(): lax.ppermute(pair_send, 'stream', [(i, i ^ 2) for i in range(8, sections)])  4.21 us
    pallas_call x1, Pallas kernels, local(): pl.pallas_call(maps_kernel, out_shape=(half_shape, half_shape, in_vmem(bl...  3.16 us
    ppermute x1, starting transfers between devices, local(): recv = lax.ppermute(send, 'stream', [(i, i ^ 1) for i in range(sections)])  3.16 us
    ppermute x1, starting transfers between devices, local(): below = lax.ppermute(last_slab, 'span', up)  3.12 us
  transfers between devices with their start and end apart: 18, of which 3 were waited for; matrix products, arithmetic and copies ran while one was open for 0% of the time, Pallas kernels for 8%

profile of v5, /device:TPU:497, one launch (start us, length us, event | category | flops | bytes accessed | tf_op | source)
XLA Modules:
  0.0 63.6 jit_solution(1610561571931079481)
XLA Ops:
  0.0 0.9 %outer_slabs.1 = (bf16[1,8,32,128]{3,2,1,0:T(8,128)(2,1)S(1)}, bf16[1,8,32,128]{3,2,1,0:T(8,128)(2,1)S(1)}) custom-call(bf16[1,4,8,32,128]{4,3,2,1,0:T(8,128)(2,1)} %prev_hbm.1), custom_call_target="tpu_custom_call" | custom-call | tf_op jit(solution)/shard_map/outer_slabs/pallas_call | solution.py:305
  0.9 3.1 %collective-permute-start = (bf16[1,8,32,128]{3,2,1,0:T(8,128)(2,1)S(1)}, bf16[1,8,32,128]{3,2,1,0:T(8,128)(2,1)S(1)}, u32[]{:S(2)}, u32[]{:S(2)}) collective-permute-start(bf16[1,8,32,128]{3,2,1,0:T(8,128)(2,1)S(1)} %get-tuple-element.32), channel_id=1, source_target_pairs={{0,1},{1,2},{2,3},{3,4},{4,5},{5,6},{6,7},{7,8},{8,9},{9,10},{10,1... | collective-permute-start | bytes 196616 | tf_op jit(solution)/shard_map/ppermute | solution.py:314
  4.0 4.3 %collective-permute-start.1 = (bf16[1,8,32,128]{3,2,1,0:T(8,128)(2,1)S(1)}, bf16[1,8,32,128]{3,2,1,0:T(8,128)(2,1)S(1)}, u32[]{:S(2)}, u32[]{:S(2)}) collective-permute-start(bf16[1,8,32,128]{3,2,1,0:T(8,128)(2,1)S(1)} %get-tuple-element.33), channel_id=1, source_target_pairs={{1,0},{2,1},{3,2},{4,3},{5,4},{6,5},{7,6},{8,7},{9,8},{10,9},{11,1... | collective-permute-start | bytes 196616 | tf_op jit(solution)/shard_map/ppermute | solution.py:315
  8.9 3.2 %section_maps.1 = (bf16[2,1296,128]{2,1,0:T(8,128)(2,1)S(1)}, bf16[2,1296,128]{2,1,0:T(8,128)(2,1)S(1)}, bf16[4,8,128,128]{3,2,1,0:T(8,128)(2,1)S(1)}, f32[4,8,3...) custom-call(s32[1]{0:T(128)S(6)} %copy.13.widths_hbm, ...), custom_call_target="tpu_custom_call" | custom-call | flops 134217728 | bytes 2097152 | tf_op jit(solution)/shard_map/section_maps/pallas_call | solution.py:323
  12.1 0.0 collective-permute-done.below
  12.1 0.0 collective-permute-done.1.above
  12.1 0.4 section_edges.1
  12.5 3.2 %collective-permute-start.2 = (bf16[2,1296,128]{2,1,0:T(8,128)(2,1)S(1)}, bf16[2,1296,128]{2,1,0:T(8,128)(2,1)S(1)}, u32[]{:S(2)}, u32[]{:S(2)}) collective-permute-start(bf16[2,1296,128]{2,1,0:T(8,128)(2,1)S(1)} %get-tuple-element.41.odd.send), channel_id=1, source_target_pairs={{0,16},{16,0},{32,48},{48,32},{64,80},{80,64},{96,112},{112,96},{1... | collective-permute-start | bytes 1990664 | tf_op jit(solution)/shard_map/ppermute | solution.py:373
  15.7 1.7 %collective-permute-done.2.recv = bf16[2,1296,128]{2,1,0:T(8,128)(2,1)S(1)} collective-permute-done((bf16[2,1296,128]{2,1,0:T(8,128)(2,1)S(1)}, bf16[2,1296,128]{2,1,0:T(8,128)(2,1)S(1)}, u32[]{:S(2)}, u32[]{:S(2)}) %collective-permute-start.2) | collective-permute-done | bytes 663584 | tf_op jit(solution)/shard_map/ppermute | solution.py:373
  17.4 0.4 compose_chip.1
  17.8 0.7 %collective-permute-start.3 = (bf16[2,8,32,128]{3,2,1,0:T(8,128)(2,1)S(1)}, bf16[2,8,32,128]{3,2,1,0:T(8,128)(2,1)S(1)}, u32[]{:S(2)}, u32[]{:S(2)}) collective-permute-start(bf16[2,8,32,128]{3,2,1,0:T(8,128)(2,1)S(1)} %get-tuple-element.42), channel_id=1, source_target_pairs={{0,32},{16,48},{1,33},{17,49},{2,34},{18,50},{3,35},{19,51},{4,36}... | collective-permute-start | bytes 393224 | tf_op jit(solution)/shard_map/ppermute | solution.py:377
  18.4 0.7 %collective-permute-start.6 = (bf16[1296,128]{1,0:T(8,128)(2,1)S(1)}, bf16[1296,128]{1,0:T(8,128)(2,1)S(1)}, u32[]{:S(2)}, u32[]{:S(2)}) collective-permute-start(bf16[1296,128]{1,0:T(8,128)(2,1)S(1)} %get-tuple-element.57.send.pair_send), channel_id=1, source_target_pairs={{64,96},{80,112},{96,64},{112,80},{65,97},{81,113},{97,65},{113,81... | collective-permute-start | bytes 995336 | tf_op jit(solution)/shard_map/ppermute | solution.py:378
  19.1 2.6 %collective-permute-start.8 = (bf16[1296,128]{1,0:T(8,128)(2,1)S(1)}, bf16[1296,128]{1,0:T(8,128)(2,1)S(1)}, u32[]{:S(2)}, u32[]{:S(2)}) collective-permute-start(bf16[1296,128]{1,0:T(8,128)(2,1)S(1)} %get-tuple-element.57.send.pair_send), channel_id=1, source_target_pairs={{128,160},{144,176},{160,128},{176,144},{192,224},{208,240},{224,1... | collective-permute-start | bytes 995336 | tf_op jit(solution)/shard_map/ppermute | solution.py:379
  21.8 0.0 collective-permute-done.3.arrived
  21.8 0.3 first_group.1
  22.1 0.7 %collective-permute-start.4 = (bf16[8,32,128]{2,1,0:T(8,128)(2,1)S(1)}, bf16[8,32,128]{2,1,0:T(8,128)(2,1)S(1)}, u32[]{:S(2)}, u32[]{:S(2)}) collective-permute-start(bf16[8,32,128]{2,1,0:T(8,128)(2,1)S(1)} %get-tuple-element.45), channel_id=1, source_target_pairs={{32,64},{48,80},{33,65},{49,81},{34,66},{50,82},{35,67},{51,83},{3... | collective-permute-start | bytes 196616 | tf_op jit(solution)/shard_map/ppermute | solution.py:382
  22.7 0.7 %collective-permute-start.5 = (bf16[8,32,128]{2,1,0:T(8,128)(2,1)S(1)}, bf16[8,32,128]{2,1,0:T(8,128)(2,1)S(1)}, u32[]{:S(2)}, u32[]{:S(2)}) collective-permute-start(bf16[8,32,128]{2,1,0:T(8,128)(2,1)S(1)} %get-tuple-element.46), channel_id=1, source_target_pairs={{32,96},{48,112},{33,97},{49,113},{34,98},{50,114},{35,99},{51,115... | collective-permute-start | bytes 196616 | tf_op jit(solution)/shard_map/ppermute | solution.py:381
  23.4 0.0 collective-permute-done.4.front
  23.4 0.0 collective-permute-done.5.back
  23.4 0.0 collective-permute-done.6.recv
  23.4 0.4 second_group.1
  23.8 0.7 %collective-permute-start.7 = (bf16[8,32,128]{2,1,0:T(8,128)(2,1)S(1)}, bf16[8,32,128]{2,1,0:T(8,128)(2,1)S(1)}, u32[]{:S(2)}, u32[]{:S(2)}) collective-permute-start(bf16[8,32,128]{2,1,0:T(8,128)(2,1)S(1)} %get-tuple-element.47), channel_id=1, source_target_pairs={{64,128},{80,144},{96,160},{112,176},{65,129},{81,145},{97,161},{1... | collective-permute-start | bytes 196616 | tf_op jit(solution)/shard_map/ppermute | solution.py:371
  24.5 1.3 %collective-permute-start.12 = (bf16[2,1296,128]{2,1,0:T(8,128)(2,1)S(1)}, bf16[2,1296,128]{2,1,0:T(8,128)(2,1)S(1)}, u32[]{:S(2)}, u32[]{:S(2)}) collective-permute-start(bf16[2,1296,128]{2,1,0:T(8,128)(2,1)S(1)} %get-tuple-element.52.keep), channel_id=1, source_target_pairs={{0,16},{32,48},{64,80},{96,112},{128,144},{160,176},{192,208},{224... | collective-permute-start | bytes 1990664 | tf_op jit(solution)/shard_map/ppermute | solution.py:390
  25.8 4.2 %collective-permute-done.8.recv = bf16[1296,128]{1,0:T(8,128)(2,1)S(1)} collective-permute-done((bf16[1296,128]{1,0:T(8,128)(2,1)S(1)}, bf16[1296,128]{1,0:T(8,128)(2,1)S(1)}, u32[]{:S(2)}, u32[]{:S(2)}) %collective-permute-start.8) | collective-permute-done | bytes 331808 | tf_op jit(solution)/shard_map/ppermute | solution.py:379
  30.0 0.3 compose_group.1.chain.group
  30.3 0.7 %collective-permute-start.11 = (bf16[1296,128]{1,0:T(8,128)(2,1)S(1)}, bf16[1296,128]{1,0:T(8,128)(2,1)S(1)}, u32[]{:S(2)}, u32[]{:S(2)}) collective-permute-start(bf16[1296,128]{1,0:T(8,128)(2,1)S(1)} %compose_group.1.chain.group), channel_id=1, source_target_pairs={{256,320},{272,336},{352,288},{368,304},{257,321},{273,337},{353,2... | collective-permute-start | bytes 995336 | tf_op jit(solution)/shard_map/ppermute | solution.py:371
  31.0 0.0 collective-permute-done.7.recv
  31.0 0.2 hop.3
  31.2 0.7 %collective-permute-start.9 = (bf16[8,32,128]{2,1,0:T(8,128)(2,1)S(1)}, bf16[8,32,128]{2,1,0:T(8,128)(2,1)S(1)}, u32[]{:S(2)}, u32[]{:S(2)}) collective-permute-start(bf16[8,32,128]{2,1,0:T(8,128)(2,1)S(1)} %get-tuple-element.49), channel_id=1, source_target_pairs={{128,192},{144,208},{160,224},{176,240},{129,193},{145,209},{161,2... | collective-permute-start | bytes 196616 | tf_op jit(solution)/shard_map/ppermute | solution.py:371
  31.9 1.3 %collective-permute-start.16 = (bf16[1296,128]{1,0:T(8,128)(2,1)S(1)}, bf16[1296,128]{1,0:T(8,128)(2,1)S(1)}, u32[]{:S(2)}, u32[]{:S(2)}) collective-permute-start(bf16[1296,128]{1,0:T(8,128)(2,1)S(1)} %compose_group.1.chain.group), channel_id=1, source_target_pairs={{384,448},{400,464},{416,480},{432,496},{385,449},{401,465},{417,4... | collective-permute-start | bytes 995336 | tf_op jit(solution)/shard_map/ppermute | solution.py:371
  33.2 0.7 %collective-permute-start.17 = (bf16[1296,128]{1,0:T(8,128)(2,1)S(1)}, bf16[1296,128]{1,0:T(8,128)(2,1)S(1)}, u32[]{:S(2)}, u32[]{:S(2)}) collective-permute-start(bf16[1296,128]{1,0:T(8,128)(2,1)S(1)} %get-tuple-element.57.send.pair_send), channel_id=1, source_target_pairs={{0,32},{16,48},{32,0},{48,16},{1,33},{17,49},{33,1},{49,17},{2,34}... | collective-permute-start | bytes 995336 | tf_op jit(solution)/shard_map/ppermute | solution.py:389
  33.9 0.0 collective-permute-done.9.recv
  33.9 0.2 hop.4
  34.1 0.7 %collective-permute-start.10 = (bf16[8,32,128]{2,1,0:T(8,128)(2,1)S(1)}, bf16[8,32,128]{2,1,0:T(8,128)(2,1)S(1)}, u32[]{:S(2)}, u32[]{:S(2)}) collective-permute-start(bf16[8,32,128]{2,1,0:T(8,128)(2,1)S(1)} %get-tuple-element.51), channel_id=1, source_target_pairs={{192,320},{208,336},{224,288},{240,304},{193,321},{209,337},{225,2... | collective-permute-start | bytes 196616 | tf_op jit(solution)/shard_map/ppermute | solution.py:371
  34.8 0.0 collective-permute-done.11.recv.joined
  34.8 0.0 collective-permute-done.12.even
  34.8 0.4 compose_rest.1.rest
  35.2 0.0 collective-permute-done.10.recv
  35.2 0.2 hop.5
  35.4 1.3 %collective-permute-start.13 = (bf16[8,32,128]{2,1,0:T(8,128)(2,1)S(1)}, bf16[8,32,128]{2,1,0:T(8,128)(2,1)S(1)}, u32[]{:S(2)}, u32[]{:S(2)}) collective-permute-start(bf16[8,32,128]{2,1,0:T(8,128)(2,1)S(1)} %get-tuple-element.55), channel_id=1, source_target_pairs={{320,448},{336,464},{288,480},{304,496},{321,449},{337,465},{289,4... | collective-permute-start | bytes 196616 | tf_op jit(solution)/shard_map/ppermute | solution.py:371
  36.7 0.7 %collective-permute-start.14 = (bf16[8,32,128]{2,1,0:T(8,128)(2,1)S(1)}, bf16[8,32,128]{2,1,0:T(8,128)(2,1)S(1)}, u32[]{:S(2)}, u32[]{:S(2)}) collective-permute-start(bf16[8,32,128]{2,1,0:T(8,128)(2,1)S(1)} %get-tuple-element.55), channel_id=1, source_target_pairs={{320,384},{336,400},{288,416},{304,432},{321,385},{337,401},{289,4... | collective-permute-start | bytes 196616 | tf_op jit(solution)/shard_map/ppermute | solution.py:371
  37.4 0.2 fill.1
  37.6 0.7 %collective-permute-start.15 = (bf16[8,32,128]{2,1,0:T(8,128)(2,1)S(1)}, bf16[8,32,128]{2,1,0:T(8,128)(2,1)S(1)}, u32[]{:S(2)}, u32[]{:S(2)}) collective-permute-start(bf16[8,32,128]{2,1,0:T(8,128)(2,1)S(1)} %fill.1), channel_id=1, source_target_pairs={{192,256},{208,272},{288,352},{304,368},{193,257},{209,273},{289,3... | collective-permute-start | bytes 196616 | tf_op jit(solution)/shard_map/ppermute | solution.py:371
  38.3 0.0 collective-permute-done.17
  38.3 0.1 add_add_fusion.recv
  38.4 14.7 %collective-permute-done.16.before_last = bf16[1296,128]{1,0:T(8,128)(2,1)S(1)} collective-permute-done((bf16[1296,128]{1,0:T(8,128)(2,1)S(1)}, bf16[1296,128]{1,0:T(8,128)(2,1)S(1)}, u32[]{:S(2)}, u32[]{:S(2)}) %collective-permute-start.16) | collective-permute-done | bytes 331808 | tf_op jit(solution)/shard_map/ppermute | solution.py:371
  53.1 0.0 collective-permute-done.15.filled
  53.1 0.0 collective-permute-done.13.arrived
  53.1 0.0 collective-permute-done.14.passed
  53.1 0.5 share.1
  53.6 8.9 %all-gather = bf16[8,8,32,128]{3,2,1,0:T(8,128)(2,1)S(1)} all-gather(bf16[2,8,32,128]{3,2,1,0:T(8,128)(2,1)S(1)} %share.1), channel_id=2, replica_groups={{0,16,32,48},{64,80,96,112},{128,144,160,176},{192,208,224,240},{256,27..., dimensions={0}, use_global_device_ids=true | all-gather | bytes 655360 | tf_op jit(solution)/shard_map/all_gather | solution.py:414
  62.4 1.1 %finish.1 = bf16[1,4,8,32,128]{4,3,2,1,0:T(8,128)(2,1)} custom-call(bf16[4,2,8,32,128]{4,3,2,1,0:T(8,128)(2,1)S(1)} %bitcast.1, bf16[2,1296,128]{2,1,0:T(8,128)(2,1)S(1)} %get-tuple-element.52.keep, bf16[2,1296,128]{2,1,0:T(8,128)(2,1)S(1)} %get-tuple-element.41.odd.send, bf16[2,1296,128]{2,1,0:T(8,128)(2,1)S(1)} %compose_rest.1.rest, ...), custom_call_target="tpu_custom_call" | custom-call | tf_op jit(solution)/shard_map/finish/pallas_call | solution.py:417
  (1 shorter events, 0.0 us)
Async XLA Ops:
  0.9 11.2 %collective-permute-start = (bf16[1,8,32,128]{3,2,1,0:T(8,128)(2,1)S(1)}, bf16[1,8,32,128]{3,2,1,0:T(8,128)(2,1)S(1)}, u32[]{:S(2)}, u32[]{:S(2)}) collective-permute-start(bf16[1,8,32,128]{3,2,1,0:T(8,128)(2,1)S(1)} %get-tuple-element.32), channel_id=1, source_target_pairs={{0,1},{1,2},{2,3},{3,4},{4,5},{5,6},{6,7},{7,8},{8,9},{9,10},{10,1... | collective-permute-start | bytes 196616 | tf_op jit(solution)/shard_map/ppermute | solution.py:314
  4.0 8.1 %collective-permute-start.1 = (bf16[1,8,32,128]{3,2,1,0:T(8,128)(2,1)S(1)}, bf16[1,8,32,128]{3,2,1,0:T(8,128)(2,1)S(1)}, u32[]{:S(2)}, u32[]{:S(2)}) collective-permute-start(bf16[1,8,32,128]{3,2,1,0:T(8,128)(2,1)S(1)} %get-tuple-element.33), channel_id=1, source_target_pairs={{1,0},{2,1},{3,2},{4,3},{5,4},{6,5},{7,6},{8,7},{9,8},{10,9},{11,1... | collective-permute-start | bytes 196616 | tf_op jit(solution)/shard_map/ppermute | solution.py:315
  12.5 4.9 %collective-permute-start.2 = (bf16[2,1296,128]{2,1,0:T(8,128)(2,1)S(1)}, bf16[2,1296,128]{2,1,0:T(8,128)(2,1)S(1)}, u32[]{:S(2)}, u32[]{:S(2)}) collective-permute-start(bf16[2,1296,128]{2,1,0:T(8,128)(2,1)S(1)} %get-tuple-element.41.odd.send), channel_id=1, source_target_pairs={{0,16},{16,0},{32,48},{48,32},{64,80},{80,64},{96,112},{112,96},{1... | collective-permute-start | bytes 1990664 | tf_op jit(solution)/shard_map/ppermute | solution.py:373
  17.8 4.0 %collective-permute-start.3 = (bf16[2,8,32,128]{3,2,1,0:T(8,128)(2,1)S(1)}, bf16[2,8,32,128]{3,2,1,0:T(8,128)(2,1)S(1)}, u32[]{:S(2)}, u32[]{:S(2)}) collective-permute-start(bf16[2,8,32,128]{3,2,1,0:T(8,128)(2,1)S(1)} %get-tuple-element.42), channel_id=1, source_target_pairs={{0,32},{16,48},{1,33},{17,49},{2,34},{18,50},{3,35},{19,51},{4,36}... | collective-permute-start | bytes 393224 | tf_op jit(solution)/shard_map/ppermute | solution.py:377
  18.4 5.0 %collective-permute-start.6 = (bf16[1296,128]{1,0:T(8,128)(2,1)S(1)}, bf16[1296,128]{1,0:T(8,128)(2,1)S(1)}, u32[]{:S(2)}, u32[]{:S(2)}) collective-permute-start(bf16[1296,128]{1,0:T(8,128)(2,1)S(1)} %get-tuple-element.57.send.pair_send), channel_id=1, source_target_pairs={{64,96},{80,112},{96,64},{112,80},{65,97},{81,113},{97,65},{113,81... | collective-permute-start | bytes 995336 | tf_op jit(solution)/shard_map/ppermute | solution.py:378
  19.1 10.9 %collective-permute-start.8 = (bf16[1296,128]{1,0:T(8,128)(2,1)S(1)}, bf16[1296,128]{1,0:T(8,128)(2,1)S(1)}, u32[]{:S(2)}, u32[]{:S(2)}) collective-permute-start(bf16[1296,128]{1,0:T(8,128)(2,1)S(1)} %get-tuple-element.57.send.pair_send), channel_id=1, source_target_pairs={{128,160},{144,176},{160,128},{176,144},{192,224},{208,240},{224,1... | collective-permute-start | bytes 995336 | tf_op jit(solution)/shard_map/ppermute | solution.py:379
  22.1 1.3 %collective-permute-start.4 = (bf16[8,32,128]{2,1,0:T(8,128)(2,1)S(1)}, bf16[8,32,128]{2,1,0:T(8,128)(2,1)S(1)}, u32[]{:S(2)}, u32[]{:S(2)}) collective-permute-start(bf16[8,32,128]{2,1,0:T(8,128)(2,1)S(1)} %get-tuple-element.45), channel_id=1, source_target_pairs={{32,64},{48,80},{33,65},{49,81},{34,66},{50,82},{35,67},{51,83},{3... | collective-permute-start | bytes 196616 | tf_op jit(solution)/shard_map/ppermute | solution.py:382
  22.7 0.7 %collective-permute-start.5 = (bf16[8,32,128]{2,1,0:T(8,128)(2,1)S(1)}, bf16[8,32,128]{2,1,0:T(8,128)(2,1)S(1)}, u32[]{:S(2)}, u32[]{:S(2)}) collective-permute-start(bf16[8,32,128]{2,1,0:T(8,128)(2,1)S(1)} %get-tuple-element.46), channel_id=1, source_target_pairs={{32,96},{48,112},{33,97},{49,113},{34,98},{50,114},{35,99},{51,115... | collective-permute-start | bytes 196616 | tf_op jit(solution)/shard_map/ppermute | solution.py:381
  23.8 7.2 %collective-permute-start.7 = (bf16[8,32,128]{2,1,0:T(8,128)(2,1)S(1)}, bf16[8,32,128]{2,1,0:T(8,128)(2,1)S(1)}, u32[]{:S(2)}, u32[]{:S(2)}) collective-permute-start(bf16[8,32,128]{2,1,0:T(8,128)(2,1)S(1)} %get-tuple-element.47), channel_id=1, source_target_pairs={{64,128},{80,144},{96,160},{112,176},{65,129},{81,145},{97,161},{1... | collective-permute-start | bytes 196616 | tf_op jit(solution)/shard_map/ppermute | solution.py:371
  24.5 10.3 %collective-permute-start.12 = (bf16[2,1296,128]{2,1,0:T(8,128)(2,1)S(1)}, bf16[2,1296,128]{2,1,0:T(8,128)(2,1)S(1)}, u32[]{:S(2)}, u32[]{:S(2)}) collective-permute-start(bf16[2,1296,128]{2,1,0:T(8,128)(2,1)S(1)} %get-tuple-element.52.keep), channel_id=1, source_target_pairs={{0,16},{32,48},{64,80},{96,112},{128,144},{160,176},{192,208},{224... | collective-permute-start | bytes 1990664 | tf_op jit(solution)/shard_map/ppermute | solution.py:390
  30.3 4.5 %collective-permute-start.11 = (bf16[1296,128]{1,0:T(8,128)(2,1)S(1)}, bf16[1296,128]{1,0:T(8,128)(2,1)S(1)}, u32[]{:S(2)}, u32[]{:S(2)}) collective-permute-start(bf16[1296,128]{1,0:T(8,128)(2,1)S(1)} %compose_group.1.chain.group), channel_id=1, source_target_pairs={{256,320},{272,336},{352,288},{368,304},{257,321},{273,337},{353,2... | collective-permute-start | bytes 995336 | tf_op jit(solution)/shard_map/ppermute | solution.py:371
  31.2 2.7 %collective-permute-start.9 = (bf16[8,32,128]{2,1,0:T(8,128)(2,1)S(1)}, bf16[8,32,128]{2,1,0:T(8,128)(2,1)S(1)}, u32[]{:S(2)}, u32[]{:S(2)}) collective-permute-start(bf16[8,32,128]{2,1,0:T(8,128)(2,1)S(1)} %get-tuple-element.49), channel_id=1, source_target_pairs={{128,192},{144,208},{160,224},{176,240},{129,193},{145,209},{161,2... | collective-permute-start | bytes 196616 | tf_op jit(solution)/shard_map/ppermute | solution.py:371
  31.9 21.2 %collective-permute-start.16 = (bf16[1296,128]{1,0:T(8,128)(2,1)S(1)}, bf16[1296,128]{1,0:T(8,128)(2,1)S(1)}, u32[]{:S(2)}, u32[]{:S(2)}) collective-permute-start(bf16[1296,128]{1,0:T(8,128)(2,1)S(1)} %compose_group.1.chain.group), channel_id=1, source_target_pairs={{384,448},{400,464},{416,480},{432,496},{385,449},{401,465},{417,4... | collective-permute-start | bytes 995336 | tf_op jit(solution)/shard_map/ppermute | solution.py:371
  33.2 5.1 %collective-permute-start.17 = (bf16[1296,128]{1,0:T(8,128)(2,1)S(1)}, bf16[1296,128]{1,0:T(8,128)(2,1)S(1)}, u32[]{:S(2)}, u32[]{:S(2)}) collective-permute-start(bf16[1296,128]{1,0:T(8,128)(2,1)S(1)} %get-tuple-element.57.send.pair_send), channel_id=1, source_target_pairs={{0,32},{16,48},{32,0},{48,16},{1,33},{17,49},{33,1},{49,17},{2,34}... | collective-permute-start | bytes 995336 | tf_op jit(solution)/shard_map/ppermute | solution.py:389
  34.1 1.1 %collective-permute-start.10 = (bf16[8,32,128]{2,1,0:T(8,128)(2,1)S(1)}, bf16[8,32,128]{2,1,0:T(8,128)(2,1)S(1)}, u32[]{:S(2)}, u32[]{:S(2)}) collective-permute-start(bf16[8,32,128]{2,1,0:T(8,128)(2,1)S(1)} %get-tuple-element.51), channel_id=1, source_target_pairs={{192,320},{208,336},{224,288},{240,304},{193,321},{209,337},{225,2... | collective-permute-start | bytes 196616 | tf_op jit(solution)/shard_map/ppermute | solution.py:371
  35.4 17.6 %collective-permute-start.13 = (bf16[8,32,128]{2,1,0:T(8,128)(2,1)S(1)}, bf16[8,32,128]{2,1,0:T(8,128)(2,1)S(1)}, u32[]{:S(2)}, u32[]{:S(2)}) collective-permute-start(bf16[8,32,128]{2,1,0:T(8,128)(2,1)S(1)} %get-tuple-element.55), channel_id=1, source_target_pairs={{320,448},{336,464},{288,480},{304,496},{321,449},{337,465},{289,4... | collective-permute-start | bytes 196616 | tf_op jit(solution)/shard_map/ppermute | solution.py:371
  36.7 16.3 %collective-permute-start.14 = (bf16[8,32,128]{2,1,0:T(8,128)(2,1)S(1)}, bf16[8,32,128]{2,1,0:T(8,128)(2,1)S(1)}, u32[]{:S(2)}, u32[]{:S(2)}) collective-permute-start(bf16[8,32,128]{2,1,0:T(8,128)(2,1)S(1)} %get-tuple-element.55), channel_id=1, source_target_pairs={{320,384},{336,400},{288,416},{304,432},{321,385},{337,401},{289,4... | collective-permute-start | bytes 196616 | tf_op jit(solution)/shard_map/ppermute | solution.py:371
  37.6 15.4 %collective-permute-start.15 = (bf16[8,32,128]{2,1,0:T(8,128)(2,1)S(1)}, bf16[8,32,128]{2,1,0:T(8,128)(2,1)S(1)}, u32[]{:S(2)}, u32[]{:S(2)}) collective-permute-start(bf16[8,32,128]{2,1,0:T(8,128)(2,1)S(1)} %fill.1), channel_id=1, source_target_pairs={{192,256},{208,272},{288,352},{304,368},{193,257},{209,273},{289,3... | collective-permute-start | bytes 196616 | tf_op jit(solution)/shard_map/ppermute | solution.py:371

commit v6 on v5

--- a/solution.py
+++ b/solution.py
@@ -10,6 +10,7 @@
 F32 = jnp.float32
 BF16 = jnp.bfloat16
 VMEM = pl.BlockSpec(memory_space=pltpu.VMEM)
+SMEM = pl.BlockSpec(memory_space=pltpu.SMEM)
 ANY = pl.BlockSpec(memory_space=pl.ANY)
 STEP = 2_300_000_000
 PAD = 16
@@ -57,87 +58,86 @@
     return group == lax.div(lax.axis_size("stream"), 4) - 1
 
 
-def outer_kernel(prev, last, first, sem):
-    slabs = prev.shape[1]
-    copies = [pltpu.make_async_copy(prev.at[0, pl.ds(slabs - 1, 1)], last, sem.at[0]),
-              pltpu.make_async_copy(prev.at[0, pl.ds(0, 1)], first, sem.at[1])]
+def half_of(core, kept):
+    return core if kept else 1 - core
+
+
+def outer_kernel(prev, for_sent, for_kept, sem):
+    core, _, _ = place()
+    last = prev.shape[1] - 1
+    copies = [pltpu.make_async_copy(prev.at[0, pl.ds(core * last, 1)], for_sent, sem.at[0]),
+              pltpu.make_async_copy(prev.at[0, pl.ds((1 - core) * last, 1)], for_kept, sem.at[1])]
     for copy in copies:
         copy.start()
     for copy in copies:
         copy.wait()
 
 
-def maps_kernel(widths_hbm, rhs_hbm, prev_hbm, u_hbm, d_hbm, lower_hbm, upper_hbm, index_hbm, keep, send, d, partial,
-                lower, upper, u, rhs, prev, lower_in, upper_in, index, widths, u_sem, d_sem, sem):
-    core, _, _ = place()
-    slabs, slots, nv, nb = rhs.shape
-    half = slabs // 2
+def maps_of_half(upper_half, halo, hbm, out, edge, u, d, rhs, prev, lower, upper, index, u_sem, d_sem, sem):
+    rhs_hbm, prev_hbm, u_hbm, d_hbm, lower_hbm, upper_hbm, index_hbm = hbm
+    half, slots, nv, nb = rhs.shape
+    first = upper_half * half
+    step = nv + nb
     small = [
-        pltpu.make_async_copy(widths_hbm, widths, sem.at[5]),
-        pltpu.make_async_copy(index_hbm.at[0], index, sem.at[1]),
-        pltpu.make_async_copy(lower_hbm.at[0], lower_in, sem.at[2]),
-        pltpu.make_async_copy(upper_hbm.at[0], upper_in, sem.at[3]),
-        pltpu.make_async_copy(prev_hbm.at[0], prev.at[pl.ds(1, slabs)], sem.at[4]),
-        pltpu.make_async_copy(rhs_hbm.at[0], rhs, sem.at[0]),
+        pltpu.make_async_copy(index_hbm.at[0, pl.ds(first, half)], index, sem.at[0]),
+        pltpu.make_async_copy(lower_hbm.at[0, pl.ds(first, half)], lower, sem.at[1]),
+        pltpu.make_async_copy(upper_hbm.at[0, pl.ds(first, half)], upper, sem.at[2]),
+        pltpu.make_async_copy(
+            prev_hbm.at[0, pl.ds(upper_half * (half - 1), half + 1)], prev.at[pl.ds(1 - upper_half, half + 1)], sem.at[3]),
+        pltpu.make_async_copy(rhs_hbm.at[0, pl.ds(first, half)], rhs, sem.at[4]),
     ]
-
-    def block_copies(m):
-        return (pltpu.make_async_copy(u_hbm.at[0, m], u.at[m], u_sem.at[m]),
-                pltpu.make_async_copy(d_hbm.at[0, m], d.at[m], d_sem.at[m]))
-
-    for copy in small:
+    blocks = [(pltpu.make_async_copy(u_hbm.at[0, first + j], u.at[j], u_sem.at[j]),
+               pltpu.make_async_copy(d_hbm.at[0, first + j], d.at[j], d_sem.at[j])) for j in range(half)]
+    for copy in (*blocks[0], *small, *blocks[1]):
         copy.start()
-    for j in range(half):
-        for first in ((1 - core) * half, core * half):
-            for copy in block_copies(first + j):
-                copy.start()
-    prev[0] = jnp.zeros_like(prev[0])
-    prev[slabs + 1] = jnp.zeros_like(prev[0])
+    prev[upper_half * (half + 1)] = jnp.zeros((slots, nv, nb), BF16) if halo is None else halo[0]
     for copy in small:
         copy.wait()
-    width = widths[0]
     rows = lax.broadcasted_iota(jnp.int32, (PAD, nb), 0)
-    active = lax.broadcasted_iota(jnp.int32, (slots, nb), 0) < width
-
-    def body(j, _):
-        for out, first in ((send, (1 - core) * half), (keep, core * half)):
-            m = first + j
-            for copy in block_copies(m):
-                copy.wait()
-            tile = jnp.zeros((PAD, nb), F32)
-            lo = jnp.where(active, lower_in[m], 0.0)
-            up = jnp.where(active, upper_in[m], 0.0)
-            lower[m], upper[m] = lo, up
-            for k in range(slots):
-                side = lo[k : k + 1, :] * prev[m, k].astype(F32) + up[k : k + 1, :] * prev[m + 2, k].astype(F32)
-                part = jnp.where(k < width, rhs[m, k].astype(F32) - side, 0.0)
-                partial[m, k] = part
-                c = dot(part.astype(BF16), d[m, k], ((1,), (1,)))
-                b = jnp.where(k < width, -dot(u[m, k], d[m, k], ((0,), (1,))), 0.0)
-                out[j, pl.ds(k * (nv + nb), nv), :] = c.astype(BF16)
-                out[j, pl.ds(k * (nv + nb) + nv, nb), :] = b.astype(BF16)
-                tile = tile + jnp.where(rows == k, index[m, k].astype(F32), 0.0)
-            out[j, pl.ds(slots * (nv + nb), PAD), :] = tile.astype(BF16)
-        return 0
-
-    lax.fori_loop(0, half, body, 0)
-
-
-def edges_kernel(below, above, d, partial, lower, upper, keep_in, send_in, keep, send):
+    for j in range(half):
+        for copy in blocks[j]:
+            copy.wait()
+        tile = jnp.zeros((PAD, nb), F32)
+        for k in range(slots):
+            side = (lower[j, k : k + 1, :] * prev[j, k].astype(F32)
+                    + upper[j, k : k + 1, :] * prev[j + 2, k].astype(F32))
+            part = rhs[j, k].astype(F32) - side
+            c = dot(part.astype(BF16), d[j, k], ((1,), (1,)))
+            b = -dot(u[j, k], d[j, k], ((0,), (1,)))
+            out[j, pl.ds(k * step, nv), :] = c.astype(BF16)
+            out[j, pl.ds(k * step + nv, nb), :] = b.astype(BF16)
+            tile = tile + jnp.where(rows == k, index[j, k].astype(F32), 0.0)
+        out[j, pl.ds(slots * step, PAD), :] = tile.astype(BF16)
+    if edge is None:
+        return
+    edge_d, edge_part, edge_gain = edge
+    j = upper_half * (half - 1)
+    edge_d[...] = d[j]
+    edge_gain[...] = jnp.where(upper_half == 1, upper[j], lower[j])
+    for k in range(slots):
+        side = (lower[j, pl.ds(k, 1), :] * prev[j, k].astype(F32)
+                + upper[j, pl.ds(k, 1), :] * prev[j + 2, k].astype(F32))
+        edge_part[k] = rhs[j, k].astype(F32) - side
+
+
+def sent_kernel(*refs):
     core, _, _ = place()
-    slabs, slots, nv, nb = partial.shape
-    step = nv + nb
-
-    def edge(out, j, m, gain, halo):
-        for k in range(slots):
-            part = partial[m, k] - gain[m, pl.ds(k, 1), :] * halo[0, k].astype(F32)
-            out[j, pl.ds(k * step, nv), :] = dot(part.astype(BF16), d[m, k], ((1,), (1,))).astype(BF16)
-
-    for here, first, last in ((0, keep, send), (1, send, keep)):
-        @pl.when(core == here)
-        def _():
-            edge(first, 0, 0, lower, below)
-            edge(last, slabs // 2 - 1, slabs - 1, upper, above)
+    maps_of_half(half_of(core, False), None, refs[:7], refs[7], refs[8:11], *refs[11:])
+
+
+def kept_kernel(halo, *refs):
+    core, _, _ = place()
+    maps_of_half(half_of(core, True), halo, refs[:7], refs[7], None, *refs[8:])
+
+
+def edge_kernel(halo, edge_d, edge_part, edge_gain, maps_in, maps):
+    core, _, _ = place()
+    slots, nv, nb = edge_part.shape
+    j = half_of(core, False) * (maps.shape[0] - 1)
+    for k in range(slots):
+        part = edge_part[k] - edge_gain[pl.ds(k, 1), :] * halo[0, k].astype(F32)
+        c = dot(part.astype(BF16), edge_d[k], ((1,), (1,)))
+        maps[j, pl.ds(k * (nv + nb), nv), :] = c.astype(BF16)
 
 
 def slot_scalars(tile, scratch, slots):
@@ -175,17 +175,20 @@
         start[1 - chip, k] = out_send[pl.ds(k * (nv + nb), nv), :]
 
 
-def apply_map(x, m, out, scratch, slots, nv, nb):
+def apply_map(x, m, out, scratch, slots, nv, nb, active=None):
     step = nv + nb
     picks = slot_scalars(m[pl.ds(slots * step, PAD), :].astype(F32), scratch, slots)
     for k in range(slots):
-        y = dot(x[picks[k]], m[pl.ds(k * step + nv, nb), :])
-        out[k] = (y + m[pl.ds(k * step, nv), :].astype(F32)).astype(BF16)
-
-
-def rest_kernel(slots, nv, even, odd, out, scratch):
+        y = dot(x[picks[k]], m[pl.ds(k * step + nv, nb), :]) + m[pl.ds(k * step, nv), :].astype(F32)
+        if active is not None:
+            y = jnp.where(active[pl.ds(k, 1), :] > 0.0, y, 0.0)
+        out[k] = y.astype(BF16)
+
+
+def rest_kernel(slots, nv, widths, even, odd, out, active, scratch):
     core, _, _ = place()
     half, _, nb = out.shape
+    active[...] = jnp.where(lax.broadcasted_iota(jnp.int32, (slots, nb), 0) < widths[0], 1.0, 0.0)
 
     @pl.when(core == 1)
     def _():
@@ -268,7 +271,7 @@
             apply_map(total, lo, out.at[1], scratch, slots, nv, nb)
 
 
-def finish_kernel(slots, nv, shared, keep, send, rest, pair_keep, pair_send, out, result, scratch, sem):
+def finish_kernel(slots, nv, active, shared, keep, send, rest, pair_keep, pair_send, out, result, scratch, sem):
     core, chip, _ = place()
     slabs, nb = out.shape[1], out.shape[-1]
     half = slabs // 2
@@ -284,7 +287,7 @@
             copies = []
             for m in range(slabs):
                 x = shared.at[2 * (m % 2) + m // 2, chip]
-                apply_map(x, maps[m], result.at[m], scratch, slots, nv, nb)
+                apply_map(x, maps[m], result.at[m], scratch.at[m], slots, nv, nb, active)
                 copies.append(pltpu.make_async_copy(result.at[m], out.at[0, m], sem.at[m]))
                 copies[-1].start()
             for copy in copies:
@@ -299,10 +302,14 @@
     assert groups > JOINED[1] + 2
     rows = slots * (nv + nb) + PAD
 
-    up = [(i, i + 1) for i in range(peers - 1)]
-    down = [(j, i) for i, j in up]
+    half_shape = in_vmem((half, rows, nb))
+    one_shape = in_vmem((rows, nb))
+    vec_shape = in_vmem((slots, nv, nb))
     edge_shape = in_vmem((1, slots, nv, nb))
-    last_slab, first_slab = pl.pallas_call(
+    index_scratch = pltpu.VMEM((PAD, nb), jnp.int32)
+    block_shape, gain_shape = (half, slots, nb, nb), (half, slots, nb)
+
+    for_sent, for_kept = pl.pallas_call(
         outer_kernel,
         out_shape=(edge_shape, edge_shape),
         in_specs=[ANY],
@@ -311,46 +318,59 @@
         compiler_params=params(),
         name="outer_slabs",
     )(in_hbm(previous))
-    below = lax.ppermute(last_slab, "span", up)
-    above = lax.ppermute(first_slab, "span", down)
-
-    half_shape = in_vmem((half, rows, nb))
-    one_shape = in_vmem((rows, nb))
-    vec_shape = in_vmem((slots, nv, nb))
-    index_scratch = pltpu.VMEM((PAD, nb), jnp.int32)
-    block_shape, gain_shape = (slabs, slots, nb, nb), (slabs, slots, nb)
-
-    keep, send, d, partial, lower, upper = pl.pallas_call(
-        maps_kernel,
-        out_shape=(half_shape, half_shape, in_vmem(block_shape), in_vmem((slabs, slots, nv, nb), F32),
-                   in_vmem(gain_shape, F32), in_vmem(gain_shape, F32)),
-        in_specs=[ANY] * 8,
-        out_specs=(VMEM,) * 6,
-        scratch_shapes=[
-            pltpu.VMEM(block_shape, BF16),
-            pltpu.VMEM((slabs, slots, nv, nb), BF16),
-            pltpu.VMEM((slabs + 2, slots, nv, nb), BF16),
-            pltpu.VMEM(gain_shape, F32),
-            pltpu.VMEM(gain_shape, F32),
-            pltpu.SMEM((slabs, slots), jnp.int32),
-            pltpu.SMEM((1,), jnp.int32),
-            pltpu.SemaphoreType.DMA((slabs,)),
-            pltpu.SemaphoreType.DMA((slabs,)),
-            pltpu.SemaphoreType.DMA((6,)),
-        ],
-        compiler_params=params(),
-        cost_estimate=cost(2 * slabs * slots * nb**3, 4 * slabs * slots * nb * nb),
-        name="section_maps",
-    )(widths, *(in_hbm(x) for x in (rhs, previous, upstream_blocks, inverse_blocks, lower_gain, upper_gain, upstream_index)))
-    keep, send = pl.pallas_call(
-        edges_kernel,
-        out_shape=(half_shape, half_shape),
-        in_specs=[VMEM] * 8,
-        out_specs=(VMEM, VMEM),
-        input_output_aliases={6: 0, 7: 1},
-        compiler_params=params(),
-        name="section_edges",
-    )(*(pin(x) for x in (below, above, d, partial, lower, upper, keep, send)))
+
+    def beside(x, kept):
+        pairs = []
+        for i in range(sections):
+            for s in range(peers - 1):
+                here, above = i * peers + s, i * peers + s + 1
+                pairs.append((above, here) if half_of(i % 2, kept) == 1 else (here, above))
+        return lax.ppermute(x, ("stream", "span"), pairs)
+
+    operands = [in_hbm(x) for x in (
+        rhs, previous, upstream_blocks, inverse_blocks, lower_gain, upper_gain, upstream_index)]
+    maps_scratch = [
+        pltpu.VMEM(block_shape, BF16),
+        pltpu.VMEM(block_shape, BF16),
+        pltpu.VMEM((half, slots, nv, nb), BF16),
+        pltpu.VMEM((half + 2, slots, nv, nb), BF16),
+        pltpu.VMEM(gain_shape, F32),
+        pltpu.VMEM(gain_shape, F32),
+        pltpu.SMEM((half, slots), jnp.int32),
+        pltpu.SemaphoreType.DMA((half,)),
+        pltpu.SemaphoreType.DMA((half,)),
+        pltpu.SemaphoreType.DMA((5,)),
+    ]
+    halo_sent, halo_kept = beside(for_sent, False), beside(for_kept, True)
+    send, *edge = pl.pallas_call(
+        sent_kernel,
+        out_shape=(half_shape, in_vmem((slots, nb, nb)), in_vmem((slots, nv, nb), F32), in_vmem((slots, nb), F32)),
+        in_specs=[ANY] * 7,
+        out_specs=(VMEM,) * 4,
+        scratch_shapes=maps_scratch,
+        compiler_params=params(),
+        cost_estimate=cost(STEP, 0),
+        name="maps_sent",
+    )(*operands)
+    send = pl.pallas_call(
+        edge_kernel,
+        out_shape=half_shape,
+        in_specs=[VMEM] * 5,
+        out_specs=VMEM,
+        input_output_aliases={4: 0},
+        compiler_params=params(),
+        name="edge_sent",
+    )(*(pin(x) for x in (halo_sent, *edge, send)))
+    keep = pl.pallas_call(
+        kept_kernel,
+        out_shape=half_shape,
+        in_specs=[VMEM] + [ANY] * 7,
+        out_specs=VMEM,
+        scratch_shapes=maps_scratch,
+        compiler_params=params(),
+        cost_estimate=cost(10 * STEP, 0),
+        name="maps_kept",
+    )(pin(halo_kept), *operands)
 
     def call(kernel, outs, name, *args, scratch=(), flops=0):
         return pl.pallas_call(
@@ -388,7 +408,16 @@
     keep_again, pair_send_again, state = lax.optimization_barrier((keep, pair_send, state))
     recv_first = lax.ppermute(pair_send_again, "stream", [(i, i ^ 2) for i in range(4)])
     even = lax.ppermute(keep_again, "stream", [(i, i + 1) for i in range(0, sections, 2)])
-    rest = call(rest_kernel, half_shape, "compose_rest", even, send, flops=STEP)
+    rest, active = pl.pallas_call(
+        functools.partial(rest_kernel, slots, nv),
+        out_shape=(half_shape, in_vmem((slots, nb), F32)),
+        in_specs=[SMEM, VMEM, VMEM],
+        out_specs=(VMEM, VMEM),
+        scratch_shapes=[index_scratch],
+        compiler_params=params(),
+        cost_estimate=cost(STEP, 0),
+        name="compose_rest",
+    )(widths, pin(even), pin(send))
 
     a, b = JOINED
     last = groups - 1
@@ -417,16 +446,16 @@
     return pl.pallas_call(
         functools.partial(finish_kernel, slots, nv),
         out_shape=jax.ShapeDtypeStruct(rhs.shape, BF16),
-        in_specs=[VMEM] * 6,
+        in_specs=[VMEM] * 7,
         out_specs=ANY,
         scratch_shapes=[
             pltpu.VMEM((slabs, slots, nv, nb), BF16),
-            index_scratch,
+            pltpu.VMEM((slabs, PAD, nb), jnp.int32),
             pltpu.SemaphoreType.DMA((slabs,)),
         ],
         compiler_params=params(),
         name="finish",
-    )(*(pin(x) for x in (shared, keep, send, rest, pair_keep, pair_send)))
+    )(*(pin(x) for x in (active, shared, keep, send, rest, pair_keep, pair_send)))
 
 
 def solution(mesh):

time: 64 us -> 63 us (0.984)
  the two profiles are of different devices: /device:TPU:497 before, /device:TPU:423 now
where the time goes in v6:
time: 63 us; the launch traced here: 62.6 us
  starting transfers between devices  26.2 us (42%)
  waiting for transfers between devices  15.1 us (24%)
  blocking collectives  10.8 us (17%)
  Pallas kernels  9.42 us (15%)
  between operations  0.96 us (2%)
    all_gather x1, blocking collectives, local(): lax.all_gather(shares, 'stream', axis_index_groups=[[4 * g + r for r in r...  10.8 us
    ppermute x8, waiting for transfers between devices, stream(): return lax.ppermute(x, 'stream', pairs)  10.4 us
    ppermute x8, starting transfers between devices, stream(): return lax.ppermute(x, 'stream', pairs)  8.4 us
    ppermute x2, starting transfers between devices, beside(): return lax.ppermute(x, ('stream', 'span'), pairs)  5.28 us
    ppermute x1, starting transfers between devices, local(): recv = lax.ppermute(send, 'stream', [(i, i ^ 1) for i in range(sections)])  5.27 us
    ppermute x1, waiting for transfers between devices, local(): lax.ppermute(pair_send, 'stream', [(i, i ^ 2) for i in range(8, sections)])  4.64 us
    ppermute x1, starting transfers between devices, local(): lax.ppermute(pair_send, 'stream', [(i, i ^ 2) for i in range(8, sections)])  2.63 us
    pallas_call x10, Pallas kernels, call(): pl.pallas_call(functools.partial(kernel, slots, nv), out_shape=outs, in_s...  2.5 us
  transfers between devices with their start and end apart: 18, of which 2 were waited for; matrix products, arithmetic and copies ran while one was open for 0% of the time, Pallas kernels for 11%

profile of v6, /device:TPU:423, one launch (start us, length us, event | category | flops | bytes accessed | tf_op | source)
XLA Modules:
  0.0 62.6 jit_solution(6506996292154991097)
XLA Ops:
  0.0 0.9 %outer_slabs.1 = (bf16[1,8,32,128]{3,2,1,0:T(8,128)(2,1)S(1)}, bf16[1,8,32,128]{3,2,1,0:T(8,128)(2,1)S(1)}) custom-call(bf16[1,4,8,32,128]{4,3,2,1,0:T(8,128)(2,1)} %refs_1_.3), custom_call_target="tpu_custom_call" | custom-call | tf_op jit(solution)/shard_map/outer_slabs/pallas_call | solution.py:312
  0.9 3.1 %collective-permute-start.1 = (bf16[1,8,32,128]{3,2,1,0:T(8,128)(2,1)S(1)}, bf16[1,8,32,128]{3,2,1,0:T(8,128)(2,1)S(1)}, u32[]{:S(2)}, u32[]{:S(2)}) collective-permute-start(bf16[1,8,32,128]{3,2,1,0:T(8,128)(2,1)S(1)} %get-tuple-element.31), channel_id=1, source_target_pairs={{1,0},{2,1},{3,2},{4,3},{5,4},{6,5},{7,6},{8,7},{9,8},{10,9},{11,1... | collective-permute-start | bytes 196616 | tf_op jit(solution)/shard_map/ppermute | solution.py:328
  4.0 2.2 %collective-permute-start = (bf16[1,8,32,128]{3,2,1,0:T(8,128)(2,1)S(1)}, bf16[1,8,32,128]{3,2,1,0:T(8,128)(2,1)S(1)}, u32[]{:S(2)}, u32[]{:S(2)}) collective-permute-start(bf16[1,8,32,128]{3,2,1,0:T(8,128)(2,1)S(1)} %get-tuple-element.30), channel_id=1, source_target_pairs={{0,1},{1,2},{2,3},{3,4},{4,5},{5,6},{6,7},{7,8},{8,9},{9,10},{10,1... | collective-permute-start | bytes 196616 | tf_op jit(solution)/shard_map/ppermute | solution.py:328
  6.2 2.2 %maps_sent.1 = (bf16[2,1296,128]{2,1,0:T(8,128)(2,1)S(1)}, bf16[8,128,128]{2,1,0:T(8,128)(2,1)S(1)}, f32[8,32,128]{2,1,0:T(8,128)S(1)}, f32[8,128]{1,0:T(8,128)S(1)}) custom-call(bf16[1,4,8,32,128]{4,3,2,1,0:T(8,128)(2,1)} %refs_0_.3, bf16[1,4,8,32,128]{4,3,2,1,0:T(8,128)(2,1)} %refs_1_.3, bf16[1,4,8,128,128]{4,3,2,1,0:T(8,128)(2,1)} %refs_2_.3, ...), custom_call_target="tpu_custom_call" | custom-call | flops 2300000000 | tf_op jit(solution)/shard_map/maps_sent/pallas_call | solution.py:345
  8.4 0.0 collective-permute-done.1.halo
  8.4 0.2 edge_sent.1.odd.send
  8.6 5.3 %collective-permute-start.2 = (bf16[2,1296,128]{2,1,0:T(8,128)(2,1)S(1)}, bf16[2,1296,128]{2,1,0:T(8,128)(2,1)S(1)}, u32[]{:S(2)}, u32[]{:S(2)}) collective-permute-start(bf16[2,1296,128]{2,1,0:T(8,128)(2,1)S(1)} %edge_sent.1.odd.send), channel_id=1, source_target_pairs={{0,16},{16,0},{32,48},{48,32},{64,80},{80,64},{96,112},{112,96},{1... | collective-permute-start | bytes 1990664 | tf_op jit(solution)/shard_map/ppermute | solution.py:393
  13.9 0.0 collective-permute-done.halo
  13.9 2.2 %maps_kept.1.keep = bf16[2,1296,128]{2,1,0:T(8,128)(2,1)S(1)} custom-call(bf16[1,8,32,128]{3,2,1,0:T(8,128)(2,1)S(1)} %collective-permute-done.halo, bf16[1,4,8,32,128]{4,3,2,1,0:T(8,128)(2,1)} %refs_0_.3, bf16[1,4,8,32,128]{4,3,2,1,0:T(8,128)(2,1)} %refs_1_.3, bf16[1,4,8,128,128]{4,3,2,1,0:T(8,128)(2,1)} %refs_2_.3, bf16[1,4,8,128,128]{4,3,2,1,0:T(8,128)(2,1)} %refs_3_.3, ...), custom_call_target="tpu_custom_call" | custom-call | flops 23000000512 | tf_op jit(solution)/shard_map/maps_kept/pallas_call | solution.py:364
  16.1 0.0 collective-permute-done.2.recv
  16.1 0.4 compose_chip.1
  16.5 0.7 %collective-permute-start.3 = (bf16[2,8,32,128]{3,2,1,0:T(8,128)(2,1)S(1)}, bf16[2,8,32,128]{3,2,1,0:T(8,128)(2,1)S(1)}, u32[]{:S(2)}, u32[]{:S(2)}) collective-permute-start(bf16[2,8,32,128]{3,2,1,0:T(8,128)(2,1)S(1)} %get-tuple-element.37), channel_id=1, source_target_pairs={{0,32},{16,48},{1,33},{17,49},{2,34},{18,50},{3,35},{19,51},{4,36}... | collective-permute-start | bytes 393224 | tf_op jit(solution)/shard_map/ppermute | solution.py:397
  17.1 0.7 %collective-permute-start.6 = (bf16[1296,128]{1,0:T(8,128)(2,1)S(1)}, bf16[1296,128]{1,0:T(8,128)(2,1)S(1)}, u32[]{:S(2)}, u32[]{:S(2)}) collective-permute-start(bf16[1296,128]{1,0:T(8,128)(2,1)S(1)} %get-tuple-element.53.send.pair_send), channel_id=1, source_target_pairs={{64,96},{80,112},{96,64},{112,80},{65,97},{81,113},{97,65},{113,81... | collective-permute-start | bytes 995336 | tf_op jit(solution)/shard_map/ppermute | solution.py:398
  17.8 2.6 %collective-permute-start.9 = (bf16[1296,128]{1,0:T(8,128)(2,1)S(1)}, bf16[1296,128]{1,0:T(8,128)(2,1)S(1)}, u32[]{:S(2)}, u32[]{:S(2)}) collective-permute-start(bf16[1296,128]{1,0:T(8,128)(2,1)S(1)} %get-tuple-element.53.send.pair_send), channel_id=1, source_target_pairs={{128,160},{144,176},{160,128},{176,144},{192,224},{208,240},{224,1... | collective-permute-start | bytes 995336 | tf_op jit(solution)/shard_map/ppermute | solution.py:399
  20.5 0.0 collective-permute-done.3.arrived
  20.5 0.3 first_group.1
  20.8 0.7 %collective-permute-start.4 = (bf16[8,32,128]{2,1,0:T(8,128)(2,1)S(1)}, bf16[8,32,128]{2,1,0:T(8,128)(2,1)S(1)}, u32[]{:S(2)}, u32[]{:S(2)}) collective-permute-start(bf16[8,32,128]{2,1,0:T(8,128)(2,1)S(1)} %get-tuple-element.39), channel_id=1, source_target_pairs={{32,64},{48,80},{33,65},{49,81},{34,66},{50,82},{35,67},{51,83},{3... | collective-permute-start | bytes 196616 | tf_op jit(solution)/shard_map/ppermute | solution.py:402
  21.4 0.7 %collective-permute-start.5 = (bf16[8,32,128]{2,1,0:T(8,128)(2,1)S(1)}, bf16[8,32,128]{2,1,0:T(8,128)(2,1)S(1)}, u32[]{:S(2)}, u32[]{:S(2)}) collective-permute-start(bf16[8,32,128]{2,1,0:T(8,128)(2,1)S(1)} %get-tuple-element.40), channel_id=1, source_target_pairs={{32,96},{48,112},{33,97},{49,113},{34,98},{50,114},{35,99},{51,115... | collective-permute-start | bytes 196616 | tf_op jit(solution)/shard_map/ppermute | solution.py:401
  22.1 0.0 collective-permute-done.4.front
  22.1 0.0 collective-permute-done.5.back
  22.1 0.0 collective-permute-done.6.recv
  22.1 0.4 second_group.1
  22.5 0.7 %collective-permute-start.8 = (bf16[8,32,128]{2,1,0:T(8,128)(2,1)S(1)}, bf16[8,32,128]{2,1,0:T(8,128)(2,1)S(1)}, u32[]{:S(2)}, u32[]{:S(2)}) collective-permute-start(bf16[8,32,128]{2,1,0:T(8,128)(2,1)S(1)} %get-tuple-element.41), channel_id=1, source_target_pairs={{64,128},{80,144},{96,160},{112,176},{65,129},{81,145},{97,161},{1... | collective-permute-start | bytes 196616 | tf_op jit(solution)/shard_map/ppermute | solution.py:391
  23.2 1.3 %collective-permute-start.7 = (bf16[2,1296,128]{2,1,0:T(8,128)(2,1)S(1)}, bf16[2,1296,128]{2,1,0:T(8,128)(2,1)S(1)}, u32[]{:S(2)}, u32[]{:S(2)}) collective-permute-start(bf16[2,1296,128]{2,1,0:T(8,128)(2,1)S(1)} %maps_kept.1.keep), channel_id=1, source_target_pairs={{0,16},{32,48},{64,80},{96,112},{128,144},{160,176},{192,208},{224... | collective-permute-start | bytes 1990664 | tf_op jit(solution)/shard_map/ppermute | solution.py:410
  24.5 4.6 %collective-permute-done.9.recv = bf16[1296,128]{1,0:T(8,128)(2,1)S(1)} collective-permute-done((bf16[1296,128]{1,0:T(8,128)(2,1)S(1)}, bf16[1296,128]{1,0:T(8,128)(2,1)S(1)}, u32[]{:S(2)}, u32[]{:S(2)}) %collective-permute-start.9) | collective-permute-done | bytes 331808 | tf_op jit(solution)/shard_map/ppermute | solution.py:399
  29.1 0.3 compose_group.1.chain.group
  29.4 0.7 %collective-permute-start.12 = (bf16[1296,128]{1,0:T(8,128)(2,1)S(1)}, bf16[1296,128]{1,0:T(8,128)(2,1)S(1)}, u32[]{:S(2)}, u32[]{:S(2)}) collective-permute-start(bf16[1296,128]{1,0:T(8,128)(2,1)S(1)} %compose_group.1.chain.group), channel_id=1, source_target_pairs={{256,320},{272,336},{352,288},{368,304},{257,321},{273,337},{353,2... | collective-permute-start | bytes 995336 | tf_op jit(solution)/shard_map/ppermute | solution.py:391
  30.1 0.0 collective-permute-done.8.recv
  30.1 0.2 hop.3
  30.3 0.7 %collective-permute-start.10 = (bf16[8,32,128]{2,1,0:T(8,128)(2,1)S(1)}, bf16[8,32,128]{2,1,0:T(8,128)(2,1)S(1)}, u32[]{:S(2)}, u32[]{:S(2)}) collective-permute-start(bf16[8,32,128]{2,1,0:T(8,128)(2,1)S(1)} %get-tuple-element.45), channel_id=1, source_target_pairs={{128,192},{144,208},{160,224},{176,240},{129,193},{145,209},{161,2... | collective-permute-start | bytes 196616 | tf_op jit(solution)/shard_map/ppermute | solution.py:391
  31.6 3.1 %collective-permute-start.16 = (bf16[1296,128]{1,0:T(8,128)(2,1)S(1)}, bf16[1296,128]{1,0:T(8,128)(2,1)S(1)}, u32[]{:S(2)}, u32[]{:S(2)}) collective-permute-start(bf16[1296,128]{1,0:T(8,128)(2,1)S(1)} %compose_group.1.chain.group), channel_id=1, source_target_pairs={{384,448},{400,464},{416,480},{432,496},{385,449},{401,465},{417,4... | collective-permute-start | bytes 995336 | tf_op jit(solution)/shard_map/ppermute | solution.py:391
  34.8 0.7 %collective-permute-start.17 = (bf16[1296,128]{1,0:T(8,128)(2,1)S(1)}, bf16[1296,128]{1,0:T(8,128)(2,1)S(1)}, u32[]{:S(2)}, u32[]{:S(2)}) collective-permute-start(bf16[1296,128]{1,0:T(8,128)(2,1)S(1)} %get-tuple-element.53.send.pair_send), channel_id=1, source_target_pairs={{0,32},{16,48},{32,0},{48,16},{1,33},{17,49},{33,1},{49,17},{2,34}... | collective-permute-start | bytes 995336 | tf_op jit(solution)/shard_map/ppermute | solution.py:409
  35.5 0.0 collective-permute-done.10.recv
  35.5 0.2 hop.4
  35.7 0.7 %collective-permute-start.11 = (bf16[8,32,128]{2,1,0:T(8,128)(2,1)S(1)}, bf16[8,32,128]{2,1,0:T(8,128)(2,1)S(1)}, u32[]{:S(2)}, u32[]{:S(2)}) collective-permute-start(bf16[8,32,128]{2,1,0:T(8,128)(2,1)S(1)} %get-tuple-element.47), channel_id=1, source_target_pairs={{192,320},{208,336},{224,288},{240,304},{193,321},{209,337},{225,2... | collective-permute-start | bytes 196616 | tf_op jit(solution)/shard_map/ppermute | solution.py:391
  36.4 0.0 collective-permute-done.12.recv.joined
  36.4 0.0 collective-permute-done.7.even
  36.4 0.4 compose_rest.1
  36.8 0.0 collective-permute-done.11.recv
  36.8 0.2 hop.5
  37.0 0.7 %collective-permute-start.13 = (bf16[8,32,128]{2,1,0:T(8,128)(2,1)S(1)}, bf16[8,32,128]{2,1,0:T(8,128)(2,1)S(1)}, u32[]{:S(2)}, u32[]{:S(2)}) collective-permute-start(bf16[8,32,128]{2,1,0:T(8,128)(2,1)S(1)} %get-tuple-element.51), channel_id=1, source_target_pairs={{320,448},{336,464},{288,480},{304,496},{321,449},{337,465},{289,4... | collective-permute-start | bytes 196616 | tf_op jit(solution)/shard_map/ppermute | solution.py:391
  37.7 1.3 %collective-permute-start.14 = (bf16[8,32,128]{2,1,0:T(8,128)(2,1)S(1)}, bf16[8,32,128]{2,1,0:T(8,128)(2,1)S(1)}, u32[]{:S(2)}, u32[]{:S(2)}) collective-permute-start(bf16[8,32,128]{2,1,0:T(8,128)(2,1)S(1)} %get-tuple-element.51), channel_id=1, source_target_pairs={{320,384},{336,400},{288,416},{304,432},{321,385},{337,401},{289,4... | collective-permute-start | bytes 196616 | tf_op jit(solution)/shard_map/ppermute | solution.py:391
  39.0 0.2 fill.1
  39.2 0.7 %collective-permute-start.15 = (bf16[8,32,128]{2,1,0:T(8,128)(2,1)S(1)}, bf16[8,32,128]{2,1,0:T(8,128)(2,1)S(1)}, u32[]{:S(2)}, u32[]{:S(2)}) collective-permute-start(bf16[8,32,128]{2,1,0:T(8,128)(2,1)S(1)} %fill.1), channel_id=1, source_target_pairs={{192,256},{208,272},{288,352},{304,368},{193,257},{209,273},{289,3... | collective-permute-start | bytes 196616 | tf_op jit(solution)/shard_map/ppermute | solution.py:391
  39.9 0.0 collective-permute-done.17
  39.9 0.1 add_add_fusion.recv
  40.0 10.4 %collective-permute-done.16.before_last = bf16[1296,128]{1,0:T(8,128)(2,1)S(1)} collective-permute-done((bf16[1296,128]{1,0:T(8,128)(2,1)S(1)}, bf16[1296,128]{1,0:T(8,128)(2,1)S(1)}, u32[]{:S(2)}, u32[]{:S(2)}) %collective-permute-start.16) | collective-permute-done | bytes 331808 | tf_op jit(solution)/shard_map/ppermute | solution.py:391
  50.4 0.0 collective-permute-done.15.filled
  50.4 0.0 collective-permute-done.13.arrived
  50.4 0.0 collective-permute-done.14.passed
  50.4 0.2 share.1
  50.7 10.8 %all-gather = bf16[8,8,32,128]{3,2,1,0:T(8,128)(2,1)S(1)} all-gather(bf16[2,8,32,128]{3,2,1,0:T(8,128)(2,1)S(1)} %share.1), channel_id=2, replica_groups={{0,16,32,48},{64,80,96,112},{128,144,160,176},{192,208,224,240},{256,27..., dimensions={0}, use_global_device_ids=true | all-gather | bytes 655360 | tf_op jit(solution)/shard_map/all_gather | solution.py:443
  61.4 1.1 %finish.1 = bf16[1,4,8,32,128]{4,3,2,1,0:T(8,128)(2,1)} custom-call(f32[8,128]{1,0:T(8,128)S(1)} %get-tuple-element.43.active, bf16[4,2,8,32,128]{4,3,2,1,0:T(8,128)(2,1)S(1)} %bitcast.1, bf16[2,1296,128]{2,1,0:T(8,128)(2,1)S(1)} %maps_kept.1.keep, bf16[2,1296,128]{2,1,0:T(8,128)(2,1)S(1)} %edge_sent.1.odd.send, ...), custom_call_target="tpu_custom_call" | custom-call | tf_op jit(solution)/shard_map/finish/pallas_call | solution.py:446
  (1 shorter events, 0.0 us)
Async XLA Ops:
  0.9 7.5 %collective-permute-start.1 = (bf16[1,8,32,128]{3,2,1,0:T(8,128)(2,1)S(1)}, bf16[1,8,32,128]{3,2,1,0:T(8,128)(2,1)S(1)}, u32[]{:S(2)}, u32[]{:S(2)}) collective-permute-start(bf16[1,8,32,128]{3,2,1,0:T(8,128)(2,1)S(1)} %get-tuple-element.31), channel_id=1, source_target_pairs={{1,0},{2,1},{3,2},{4,3},{5,4},{6,5},{7,6},{8,7},{9,8},{10,9},{11,1... | collective-permute-start | bytes 196616 | tf_op jit(solution)/shard_map/ppermute | solution.py:328
  4.0 9.9 %collective-permute-start = (bf16[1,8,32,128]{3,2,1,0:T(8,128)(2,1)S(1)}, bf16[1,8,32,128]{3,2,1,0:T(8,128)(2,1)S(1)}, u32[]{:S(2)}, u32[]{:S(2)}) collective-permute-start(bf16[1,8,32,128]{3,2,1,0:T(8,128)(2,1)S(1)} %get-tuple-element.30), channel_id=1, source_target_pairs={{0,1},{1,2},{2,3},{3,4},{4,5},{5,6},{6,7},{7,8},{8,9},{9,10},{10,1... | collective-permute-start | bytes 196616 | tf_op jit(solution)/shard_map/ppermute | solution.py:328
  8.6 7.5 %collective-permute-start.2 = (bf16[2,1296,128]{2,1,0:T(8,128)(2,1)S(1)}, bf16[2,1296,128]{2,1,0:T(8,128)(2,1)S(1)}, u32[]{:S(2)}, u32[]{:S(2)}) collective-permute-start(bf16[2,1296,128]{2,1,0:T(8,128)(2,1)S(1)} %edge_sent.1.odd.send), channel_id=1, source_target_pairs={{0,16},{16,0},{32,48},{48,32},{64,80},{80,64},{96,112},{112,96},{1... | collective-permute-start | bytes 1990664 | tf_op jit(solution)/shard_map/ppermute | solution.py:393
  16.5 4.0 %collective-permute-start.3 = (bf16[2,8,32,128]{3,2,1,0:T(8,128)(2,1)S(1)}, bf16[2,8,32,128]{3,2,1,0:T(8,128)(2,1)S(1)}, u32[]{:S(2)}, u32[]{:S(2)}) collective-permute-start(bf16[2,8,32,128]{3,2,1,0:T(8,128)(2,1)S(1)} %get-tuple-element.37), channel_id=1, source_target_pairs={{0,32},{16,48},{1,33},{17,49},{2,34},{18,50},{3,35},{19,51},{4,36}... | collective-permute-start | bytes 393224 | tf_op jit(solution)/shard_map/ppermute | solution.py:397
  17.1 5.0 %collective-permute-start.6 = (bf16[1296,128]{1,0:T(8,128)(2,1)S(1)}, bf16[1296,128]{1,0:T(8,128)(2,1)S(1)}, u32[]{:S(2)}, u32[]{:S(2)}) collective-permute-start(bf16[1296,128]{1,0:T(8,128)(2,1)S(1)} %get-tuple-element.53.send.pair_send), channel_id=1, source_target_pairs={{64,96},{80,112},{96,64},{112,80},{65,97},{81,113},{97,65},{113,81... | collective-permute-start | bytes 995336 | tf_op jit(solution)/shard_map/ppermute | solution.py:398
  17.8 11.3 %collective-permute-start.9 = (bf16[1296,128]{1,0:T(8,128)(2,1)S(1)}, bf16[1296,128]{1,0:T(8,128)(2,1)S(1)}, u32[]{:S(2)}, u32[]{:S(2)}) collective-permute-start(bf16[1296,128]{1,0:T(8,128)(2,1)S(1)} %get-tuple-element.53.send.pair_send), channel_id=1, source_target_pairs={{128,160},{144,176},{160,128},{176,144},{192,224},{208,240},{224,1... | collective-permute-start | bytes 995336 | tf_op jit(solution)/shard_map/ppermute | solution.py:399
  20.8 1.3 %collective-permute-start.4 = (bf16[8,32,128]{2,1,0:T(8,128)(2,1)S(1)}, bf16[8,32,128]{2,1,0:T(8,128)(2,1)S(1)}, u32[]{:S(2)}, u32[]{:S(2)}) collective-permute-start(bf16[8,32,128]{2,1,0:T(8,128)(2,1)S(1)} %get-tuple-element.39), channel_id=1, source_target_pairs={{32,64},{48,80},{33,65},{49,81},{34,66},{50,82},{35,67},{51,83},{3... | collective-permute-start | bytes 196616 | tf_op jit(solution)/shard_map/ppermute | solution.py:402
  21.4 0.7 %collective-permute-start.5 = (bf16[8,32,128]{2,1,0:T(8,128)(2,1)S(1)}, bf16[8,32,128]{2,1,0:T(8,128)(2,1)S(1)}, u32[]{:S(2)}, u32[]{:S(2)}) collective-permute-start(bf16[8,32,128]{2,1,0:T(8,128)(2,1)S(1)} %get-tuple-element.40), channel_id=1, source_target_pairs={{32,96},{48,112},{33,97},{49,113},{34,98},{50,114},{35,99},{51,115... | collective-permute-start | bytes 196616 | tf_op jit(solution)/shard_map/ppermute | solution.py:401
  22.5 7.6 %collective-permute-start.8 = (bf16[8,32,128]{2,1,0:T(8,128)(2,1)S(1)}, bf16[8,32,128]{2,1,0:T(8,128)(2,1)S(1)}, u32[]{:S(2)}, u32[]{:S(2)}) collective-permute-start(bf16[8,32,128]{2,1,0:T(8,128)(2,1)S(1)} %get-tuple-element.41), channel_id=1, source_target_pairs={{64,128},{80,144},{96,160},{112,176},{65,129},{81,145},{97,161},{1... | collective-permute-start | bytes 196616 | tf_op jit(solution)/shard_map/ppermute | solution.py:391
  23.2 13.2 %collective-permute-start.7 = (bf16[2,1296,128]{2,1,0:T(8,128)(2,1)S(1)}, bf16[2,1296,128]{2,1,0:T(8,128)(2,1)S(1)}, u32[]{:S(2)}, u32[]{:S(2)}) collective-permute-start(bf16[2,1296,128]{2,1,0:T(8,128)(2,1)S(1)} %maps_kept.1.keep), channel_id=1, source_target_pairs={{0,16},{32,48},{64,80},{96,112},{128,144},{160,176},{192,208},{224... | collective-permute-start | bytes 1990664 | tf_op jit(solution)/shard_map/ppermute | solution.py:410
  29.4 6.9 %collective-permute-start.12 = (bf16[1296,128]{1,0:T(8,128)(2,1)S(1)}, bf16[1296,128]{1,0:T(8,128)(2,1)S(1)}, u32[]{:S(2)}, u32[]{:S(2)}) collective-permute-start(bf16[1296,128]{1,0:T(8,128)(2,1)S(1)} %compose_group.1.chain.group), channel_id=1, source_target_pairs={{256,320},{272,336},{352,288},{368,304},{257,321},{273,337},{353,2... | collective-permute-start | bytes 995336 | tf_op jit(solution)/shard_map/ppermute | solution.py:391
  30.3 5.1 %collective-permute-start.10 = (bf16[8,32,128]{2,1,0:T(8,128)(2,1)S(1)}, bf16[8,32,128]{2,1,0:T(8,128)(2,1)S(1)}, u32[]{:S(2)}, u32[]{:S(2)}) collective-permute-start(bf16[8,32,128]{2,1,0:T(8,128)(2,1)S(1)} %get-tuple-element.45), channel_id=1, source_target_pairs={{128,192},{144,208},{160,224},{176,240},{129,193},{145,209},{161,2... | collective-permute-start | bytes 196616 | tf_op jit(solution)/shard_map/ppermute | solution.py:391
  31.6 18.8 %collective-permute-start.16 = (bf16[1296,128]{1,0:T(8,128)(2,1)S(1)}, bf16[1296,128]{1,0:T(8,128)(2,1)S(1)}, u32[]{:S(2)}, u32[]{:S(2)}) collective-permute-start(bf16[1296,128]{1,0:T(8,128)(2,1)S(1)} %compose_group.1.chain.group), channel_id=1, source_target_pairs={{384,448},{400,464},{416,480},{432,496},{385,449},{401,465},{417,4... | collective-permute-start | bytes 995336 | tf_op jit(solution)/shard_map/ppermute | solution.py:391
  34.8 5.1 %collective-permute-start.17 = (bf16[1296,128]{1,0:T(8,128)(2,1)S(1)}, bf16[1296,128]{1,0:T(8,128)(2,1)S(1)}, u32[]{:S(2)}, u32[]{:S(2)}) collective-permute-start(bf16[1296,128]{1,0:T(8,128)(2,1)S(1)} %get-tuple-element.53.send.pair_send), channel_id=1, source_target_pairs={{0,32},{16,48},{32,0},{48,16},{1,33},{17,49},{33,1},{49,17},{2,34}... | collective-permute-start | bytes 995336 | tf_op jit(solution)/shard_map/ppermute | solution.py:409
  35.7 1.1 %collective-permute-start.11 = (bf16[8,32,128]{2,1,0:T(8,128)(2,1)S(1)}, bf16[8,32,128]{2,1,0:T(8,128)(2,1)S(1)}, u32[]{:S(2)}, u32[]{:S(2)}) collective-permute-start(bf16[8,32,128]{2,1,0:T(8,128)(2,1)S(1)} %get-tuple-element.47), channel_id=1, source_target_pairs={{192,320},{208,336},{224,288},{240,304},{193,321},{209,337},{225,2... | collective-permute-start | bytes 196616 | tf_op jit(solution)/shard_map/ppermute | solution.py:391
  37.0 13.4 %collective-permute-start.13 = (bf16[8,32,128]{2,1,0:T(8,128)(2,1)S(1)}, bf16[8,32,128]{2,1,0:T(8,128)(2,1)S(1)}, u32[]{:S(2)}, u32[]{:S(2)}) collective-permute-start(bf16[8,32,128]{2,1,0:T(8,128)(2,1)S(1)} %get-tuple-element.51), channel_id=1, source_target_pairs={{320,448},{336,464},{288,480},{304,496},{321,449},{337,465},{289,4... | collective-permute-start | bytes 196616 | tf_op jit(solution)/shard_map/ppermute | solution.py:391
  37.7 12.7 %collective-permute-start.14 = (bf16[8,32,128]{2,1,0:T(8,128)(2,1)S(1)}, bf16[8,32,128]{2,1,0:T(8,128)(2,1)S(1)}, u32[]{:S(2)}, u32[]{:S(2)}) collective-permute-start(bf16[8,32,128]{2,1,0:T(8,128)(2,1)S(1)} %get-tuple-element.51), channel_id=1, source_target_pairs={{320,384},{336,400},{288,416},{304,432},{321,385},{337,401},{289,4... | collective-permute-start | bytes 196616 | tf_op jit(solution)/shard_map/ppermute | solution.py:391
  39.2 11.2 %collective-permute-start.15 = (bf16[8,32,128]{2,1,0:T(8,128)(2,1)S(1)}, bf16[8,32,128]{2,1,0:T(8,128)(2,1)S(1)}, u32[]{:S(2)}, u32[]{:S(2)}) collective-permute-start(bf16[8,32,128]{2,1,0:T(8,128)(2,1)S(1)} %fill.1), channel_id=1, source_target_pairs={{192,256},{208,272},{288,352},{304,368},{193,257},{209,273},{289,3... | collective-permute-start | bytes 196616 | tf_op jit(solution)/shard_map/ppermute | solution.py:391

commit v7 on v6

--- a/solution.py
+++ b/solution.py
@@ -12,7 +12,7 @@
 VMEM = pl.BlockSpec(memory_space=pltpu.VMEM)
 SMEM = pl.BlockSpec(memory_space=pltpu.SMEM)
 ANY = pl.BlockSpec(memory_space=pl.ANY)
-STEP = 2_300_000_000
+MICRO = 1_150_000_000
 PAD = 16
 JOINED = (4, 5)
 
@@ -175,9 +175,14 @@
         start[1 - chip, k] = out_send[pl.ds(k * (nv + nb), nv), :]
 
 
-def apply_map(x, m, out, scratch, slots, nv, nb, active=None):
+def picks_of(m, scratch, slots, step):
+    return slot_scalars(m[pl.ds(slots * step, PAD), :].astype(F32), scratch, slots)
+
+
+def apply_map(x, m, out, scratch, slots, nv, nb, active=None, picks=None):
     step = nv + nb
-    picks = slot_scalars(m[pl.ds(slots * step, PAD), :].astype(F32), scratch, slots)
+    if picks is None:
+        picks = picks_of(m, scratch, slots, step)
     for k in range(slots):
         y = dot(x[picks[k]], m[pl.ds(k * step + nv, nb), :]) + m[pl.ds(k * step, nv), :].astype(F32)
         if active is not None:
@@ -285,9 +290,10 @@
         @pl.when(condition)
         def _():
             copies = []
+            picks = [picks_of(maps[m], scratch.at[m], slots, nv + nb) for m in range(slabs)]
             for m in range(slabs):
                 x = shared.at[2 * (m % 2) + m // 2, chip]
-                apply_map(x, maps[m], result.at[m], scratch.at[m], slots, nv, nb, active)
+                apply_map(x, maps[m], result.at[m], None, slots, nv, nb, active, picks[m])
                 copies.append(pltpu.make_async_copy(result.at[m], out.at[0, m], sem.at[m]))
                 copies[-1].start()
             for copy in copies:
@@ -349,7 +355,7 @@
         out_specs=(VMEM,) * 4,
         scratch_shapes=maps_scratch,
         compiler_params=params(),
-        cost_estimate=cost(STEP, 0),
+        cost_estimate=cost(2 * MICRO, 0),
         name="maps_sent",
     )(*operands)
     send = pl.pallas_call(
@@ -368,7 +374,7 @@
         out_specs=VMEM,
         scratch_shapes=maps_scratch,
         compiler_params=params(),
-        cost_estimate=cost(10 * STEP, 0),
+        cost_estimate=cost(20 * MICRO, 0),
         name="maps_kept",
     )(pin(halo_kept), *operands)
 
@@ -397,13 +403,13 @@
     arrived = lax.ppermute(pair_start, "stream", [(0, 2), (1, 3)])
     recv_second = lax.ppermute(pair_send, "stream", [(i, i ^ 2) for i in range(4, 8)])
     recv_later = lax.ppermute(pair_send, "stream", [(i, i ^ 2) for i in range(8, sections)])
-    front, back = call(first_kernel, (vec_shape, vec_shape), "first_group", arrived, pair_keep, pair_send, flops=STEP)
+    front, back = call(first_kernel, (vec_shape, vec_shape), "first_group", arrived, pair_keep, pair_send, flops=MICRO)
     back = lax.ppermute(back, "stream", [(2, 6), (3, 7)])
     front = lax.ppermute(front, "stream", [(2, 4), (3, 5)])
     state, inflow = call(
-        second_kernel, (vec_shape, vec_shape), "second_group", front, back, pair_keep, recv_second, scratch=(vec_shape,), flops=STEP)
+        second_kernel, (vec_shape, vec_shape), "second_group", front, back, pair_keep, recv_second, scratch=(vec_shape,), flops=2 * MICRO)
     arrived = stream(state, (0, 1, 2), (1, 1, 2))
-    group = call(group_kernel, one_shape, "compose_group", pair_keep, recv_later, flops=STEP)
+    group = call(group_kernel, one_shape, "compose_group", pair_keep, recv_later, flops=4 * MICRO)
 
     keep_again, pair_send_again, state = lax.optimization_barrier((keep, pair_send, state))
     recv_first = lax.ppermute(pair_send_again, "stream", [(i, i ^ 2) for i in range(4)])
@@ -415,7 +421,7 @@
         out_specs=(VMEM, VMEM),
         scratch_shapes=[index_scratch],
         compiler_params=params(),
-        cost_estimate=cost(STEP, 0),
+        cost_estimate=cost(MICRO, 0),
         name="compose_rest",
     )(widths, pin(even), pin(send))
 
@@ -424,11 +430,12 @@
     join_recv = stream(group, (0, a, b), (1, b, a))
     last_recv = stream(group, (0, last - 1, last), (1, last - 1, last))
     chain = call(join_kernel, one_shape, "compose_join", group, join_recv)
-    chain, rest = lax.optimization_barrier((chain, rest))
     steps = [(2, 2), *((g, g) for g in range(3, a)), (b, a), *((g, g) for g in range(b + 1, last - 1))]
     for step, (front, back) in enumerate(steps):
         maps = group if front < a else chain
-        state, inflow = call(hop_kernel, (vec_shape, vec_shape), "hop", arrived, maps, inflow, flops=STEP)
+        if step == 1:
+            rest, arrived = lax.optimization_barrier((rest, arrived))
+        state, inflow = call(hop_kernel, (vec_shape, vec_shape), "hop", arrived, maps, inflow, flops=3 * MICRO)
         if step + 1 < len(steps):
             arrived = stream(state, (0, front, steps[step + 1][0]), (1, back, steps[step + 1][1]))
         else:

time: 63 us -> 64.5 us (1.024)
  the two profiles are of different devices: /device:TPU:423 before, /device:TPU:463 now
where the time goes in v7:
time: 64.5 us; the launch traced here: 64 us
  starting transfers between devices  24.4 us (38%)
  blocking collectives  14.7 us (23%)
  waiting for transfers between devices  14.2 us (22%)
  Pallas kernels  9.62 us (15%)
  between operations  0.97 us (2%)
    all_gather x1, blocking collectives, local(): lax.all_gather(shares, 'stream', axis_index_groups=[[4 * g + r for r in r...  14.7 us
    ppermute x8, waiting for transfers between devices, stream(): return lax.ppermute(x, 'stream', pairs)  10.2 us
    ppermute x8, starting transfers between devices, stream(): return lax.ppermute(x, 'stream', pairs)  6.58 us
    ppermute x2, starting transfers between devices, beside(): return lax.ppermute(x, ('stream', 'span'), pairs)  5.28 us
    ppermute x1, starting transfers between devices, local(): recv = lax.ppermute(send, 'stream', [(i, i ^ 1) for i in range(sections)])  5.27 us
    ppermute x1, waiting for transfers between devices, local(): lax.ppermute(pair_send, 'stream', [(i, i ^ 2) for i in range(8, sections)])  3.96 us
    pallas_call x10, Pallas kernels, call(): pl.pallas_call(functools.partial(kernel, slots, nv), out_shape=outs, in_s...  2.7 us
    ppermute x1, starting transfers between devices, local(): lax.ppermute(pair_send, 'stream', [(i, i ^ 2) for i in range(8, sections)])  2.65 us
  transfers between devices with their start and end apart: 18, of which 3 were waited for; matrix products, arithmetic and copies ran while one was open for 0% of the time, Pallas kernels for 11%

profile of v7, /device:TPU:463, one launch (start us, length us, event | category | flops | bytes accessed | tf_op | source)
XLA Modules:
  0.0 64.0 jit_solution(6567977073509739333)
XLA Ops:
  0.0 0.9 %outer_slabs.1 = (bf16[1,8,32,128]{3,2,1,0:T(8,128)(2,1)S(1)}, bf16[1,8,32,128]{3,2,1,0:T(8,128)(2,1)S(1)}) custom-call(bf16[1,4,8,32,128]{4,3,2,1,0:T(8,128)(2,1)} %refs_1_.3), custom_call_target="tpu_custom_call" | custom-call | tf_op jit(solution)/shard_map/outer_slabs/pallas_call | solution.py:318
  0.9 3.1 %collective-permute-start.1 = (bf16[1,8,32,128]{3,2,1,0:T(8,128)(2,1)S(1)}, bf16[1,8,32,128]{3,2,1,0:T(8,128)(2,1)S(1)}, u32[]{:S(2)}, u32[]{:S(2)}) collective-permute-start(bf16[1,8,32,128]{3,2,1,0:T(8,128)(2,1)S(1)} %get-tuple-element.31), channel_id=1, source_target_pairs={{1,0},{2,1},{3,2},{4,3},{5,4},{6,5},{7,6},{8,7},{9,8},{10,9},{11,1... | collective-permute-start | bytes 196616 | tf_op jit(solution)/shard_map/ppermute | solution.py:334
  4.0 2.2 %collective-permute-start = (bf16[1,8,32,128]{3,2,1,0:T(8,128)(2,1)S(1)}, bf16[1,8,32,128]{3,2,1,0:T(8,128)(2,1)S(1)}, u32[]{:S(2)}, u32[]{:S(2)}) collective-permute-start(bf16[1,8,32,128]{3,2,1,0:T(8,128)(2,1)S(1)} %get-tuple-element.30), channel_id=1, source_target_pairs={{0,1},{1,2},{2,3},{3,4},{4,5},{5,6},{6,7},{7,8},{8,9},{9,10},{10,1... | collective-permute-start | bytes 196616 | tf_op jit(solution)/shard_map/ppermute | solution.py:334
  6.2 2.2 %maps_sent.1 = (bf16[2,1296,128]{2,1,0:T(8,128)(2,1)S(1)}, bf16[8,128,128]{2,1,0:T(8,128)(2,1)S(1)}, f32[8,32,128]{2,1,0:T(8,128)S(1)}, f32[8,128]{1,0:T(8,128)S(1)}) custom-call(bf16[1,4,8,32,128]{4,3,2,1,0:T(8,128)(2,1)} %refs_0_.3, bf16[1,4,8,32,128]{4,3,2,1,0:T(8,128)(2,1)} %refs_1_.3, bf16[1,4,8,128,128]{4,3,2,1,0:T(8,128)(2,1)} %refs_2_.3, ...), custom_call_target="tpu_custom_call" | custom-call | flops 2300000000 | tf_op jit(solution)/shard_map/maps_sent/pallas_call | solution.py:351
  8.4 0.0 collective-permute-done.1.halo
  8.4 0.2 edge_sent.1.odd.send
  8.6 5.3 %collective-permute-start.2 = (bf16[2,1296,128]{2,1,0:T(8,128)(2,1)S(1)}, bf16[2,1296,128]{2,1,0:T(8,128)(2,1)S(1)}, u32[]{:S(2)}, u32[]{:S(2)}) collective-permute-start(bf16[2,1296,128]{2,1,0:T(8,128)(2,1)S(1)} %edge_sent.1.odd.send), channel_id=1, source_target_pairs={{0,16},{16,0},{32,48},{48,32},{64,80},{80,64},{96,112},{112,96},{1... | collective-permute-start | bytes 1990664 | tf_op jit(solution)/shard_map/ppermute | solution.py:399
  13.9 0.0 collective-permute-done.halo
  13.9 2.2 %maps_kept.1.keep = bf16[2,1296,128]{2,1,0:T(8,128)(2,1)S(1)} custom-call(bf16[1,8,32,128]{3,2,1,0:T(8,128)(2,1)S(1)} %collective-permute-done.halo, bf16[1,4,8,32,128]{4,3,2,1,0:T(8,128)(2,1)} %refs_0_.3, bf16[1,4,8,32,128]{4,3,2,1,0:T(8,128)(2,1)} %refs_1_.3, bf16[1,4,8,128,128]{4,3,2,1,0:T(8,128)(2,1)} %refs_2_.3, bf16[1,4,8,128,128]{4,3,2,1,0:T(8,128)(2,1)} %refs_3_.3, ...), custom_call_target="tpu_custom_call" | custom-call | flops 23000000512 | tf_op jit(solution)/shard_map/maps_kept/pallas_call | solution.py:370
  16.1 0.0 collective-permute-done.2.recv
  16.1 0.4 compose_chip.1
  16.5 0.7 %collective-permute-start.6 = (bf16[1296,128]{1,0:T(8,128)(2,1)S(1)}, bf16[1296,128]{1,0:T(8,128)(2,1)S(1)}, u32[]{:S(2)}, u32[]{:S(2)}) collective-permute-start(bf16[1296,128]{1,0:T(8,128)(2,1)S(1)} %get-tuple-element.53.send.pair_send), channel_id=1, source_target_pairs={{64,96},{80,112},{96,64},{112,80},{65,97},{81,113},{97,65},{113,81... | collective-permute-start | bytes 995336 | tf_op jit(solution)/shard_map/ppermute | solution.py:404
  17.1 0.7 %collective-permute-start.3 = (bf16[2,8,32,128]{3,2,1,0:T(8,128)(2,1)S(1)}, bf16[2,8,32,128]{3,2,1,0:T(8,128)(2,1)S(1)}, u32[]{:S(2)}, u32[]{:S(2)}) collective-permute-start(bf16[2,8,32,128]{3,2,1,0:T(8,128)(2,1)S(1)} %get-tuple-element.37), channel_id=1, source_target_pairs={{0,32},{16,48},{1,33},{17,49},{2,34},{18,50},{3,35},{19,51},{4,36}... | collective-permute-start | bytes 393224 | tf_op jit(solution)/shard_map/ppermute | solution.py:403
  17.8 2.6 %collective-permute-start.9 = (bf16[1296,128]{1,0:T(8,128)(2,1)S(1)}, bf16[1296,128]{1,0:T(8,128)(2,1)S(1)}, u32[]{:S(2)}, u32[]{:S(2)}) collective-permute-start(bf16[1296,128]{1,0:T(8,128)(2,1)S(1)} %get-tuple-element.53.send.pair_send), channel_id=1, source_target_pairs={{128,160},{144,176},{160,128},{176,144},{192,224},{208,240},{224,1... | collective-permute-start | bytes 995336 | tf_op jit(solution)/shard_map/ppermute | solution.py:405
  20.5 0.0 collective-permute-done.3.arrived
  20.5 0.3 first_group.1
  20.8 0.7 %collective-permute-start.4 = (bf16[8,32,128]{2,1,0:T(8,128)(2,1)S(1)}, bf16[8,32,128]{2,1,0:T(8,128)(2,1)S(1)}, u32[]{:S(2)}, u32[]{:S(2)}) collective-permute-start(bf16[8,32,128]{2,1,0:T(8,128)(2,1)S(1)} %get-tuple-element.39), channel_id=1, source_target_pairs={{32,64},{48,80},{33,65},{49,81},{34,66},{50,82},{35,67},{51,83},{3... | collective-permute-start | bytes 196616 | tf_op jit(solution)/shard_map/ppermute | solution.py:408
  21.4 0.7 %collective-permute-start.5 = (bf16[8,32,128]{2,1,0:T(8,128)(2,1)S(1)}, bf16[8,32,128]{2,1,0:T(8,128)(2,1)S(1)}, u32[]{:S(2)}, u32[]{:S(2)}) collective-permute-start(bf16[8,32,128]{2,1,0:T(8,128)(2,1)S(1)} %get-tuple-element.40), channel_id=1, source_target_pairs={{32,96},{48,112},{33,97},{49,113},{34,98},{50,114},{35,99},{51,115... | collective-permute-start | bytes 196616 | tf_op jit(solution)/shard_map/ppermute | solution.py:407
  22.8 0.0 collective-permute-done.4.front
  22.8 0.0 collective-permute-done.5.back
  22.8 0.0 collective-permute-done.6.recv
  22.8 0.4 second_group.1
  23.2 0.7 %collective-permute-start.8 = (bf16[8,32,128]{2,1,0:T(8,128)(2,1)S(1)}, bf16[8,32,128]{2,1,0:T(8,128)(2,1)S(1)}, u32[]{:S(2)}, u32[]{:S(2)}) collective-permute-start(bf16[8,32,128]{2,1,0:T(8,128)(2,1)S(1)} %get-tuple-element.41), channel_id=1, source_target_pairs={{64,128},{80,144},{96,160},{112,176},{65,129},{81,145},{97,161},{1... | collective-permute-start | bytes 196616 | tf_op jit(solution)/shard_map/ppermute | solution.py:397
  23.9 1.3 %collective-permute-start.7 = (bf16[2,1296,128]{2,1,0:T(8,128)(2,1)S(1)}, bf16[2,1296,128]{2,1,0:T(8,128)(2,1)S(1)}, u32[]{:S(2)}, u32[]{:S(2)}) collective-permute-start(bf16[2,1296,128]{2,1,0:T(8,128)(2,1)S(1)} %maps_kept.1.keep), channel_id=1, source_target_pairs={{0,16},{32,48},{64,80},{96,112},{128,144},{160,176},{192,208},{224... | collective-permute-start | bytes 1990664 | tf_op jit(solution)/shard_map/ppermute | solution.py:416
  25.2 4.0 %collective-permute-done.9.recv = bf16[1296,128]{1,0:T(8,128)(2,1)S(1)} collective-permute-done((bf16[1296,128]{1,0:T(8,128)(2,1)S(1)}, bf16[1296,128]{1,0:T(8,128)(2,1)S(1)}, u32[]{:S(2)}, u32[]{:S(2)}) %collective-permute-start.9) | collective-permute-done | bytes 331808 | tf_op jit(solution)/shard_map/ppermute | solution.py:405
  29.1 0.3 compose_group.1.chain.group
  29.4 0.7 %collective-permute-start.12 = (bf16[1296,128]{1,0:T(8,128)(2,1)S(1)}, bf16[1296,128]{1,0:T(8,128)(2,1)S(1)}, u32[]{:S(2)}, u32[]{:S(2)}) collective-permute-start(bf16[1296,128]{1,0:T(8,128)(2,1)S(1)} %compose_group.1.chain.group), channel_id=1, source_target_pairs={{256,320},{272,336},{352,288},{368,304},{257,321},{273,337},{353,2... | collective-permute-start | bytes 995336 | tf_op jit(solution)/shard_map/ppermute | solution.py:397
  30.1 0.0 collective-permute-done.8.recv
  30.1 0.2 hop.3
  30.3 0.7 %collective-permute-start.10 = (bf16[8,32,128]{2,1,0:T(8,128)(2,1)S(1)}, bf16[8,32,128]{2,1,0:T(8,128)(2,1)S(1)}, u32[]{:S(2)}, u32[]{:S(2)}) collective-permute-start(bf16[8,32,128]{2,1,0:T(8,128)(2,1)S(1)} %get-tuple-element.46), channel_id=1, source_target_pairs={{128,192},{144,208},{160,224},{176,240},{129,193},{145,209},{161,2... | collective-permute-start | bytes 196616 | tf_op jit(solution)/shard_map/ppermute | solution.py:397
  31.0 0.0 collective-permute-done.7.even
  31.0 0.4 compose_rest.1
  31.4 0.0 collective-permute-done.10.recv
  31.4 0.2 hop.4
  31.6 0.7 %collective-permute-start.11 = (bf16[8,32,128]{2,1,0:T(8,128)(2,1)S(1)}, bf16[8,32,128]{2,1,0:T(8,128)(2,1)S(1)}, u32[]{:S(2)}, u32[]{:S(2)}) collective-permute-start(bf16[8,32,128]{2,1,0:T(8,128)(2,1)S(1)} %get-tuple-element.49), channel_id=1, source_target_pairs={{192,320},{208,336},{224,288},{240,304},{193,321},{209,337},{225,2... | collective-permute-start | bytes 196616 | tf_op jit(solution)/shard_map/ppermute | solution.py:397
  32.3 0.7 %collective-permute-start.17 = (bf16[1296,128]{1,0:T(8,128)(2,1)S(1)}, bf16[1296,128]{1,0:T(8,128)(2,1)S(1)}, u32[]{:S(2)}, u32[]{:S(2)}) collective-permute-start(bf16[1296,128]{1,0:T(8,128)(2,1)S(1)} %get-tuple-element.53.send.pair_send), channel_id=1, source_target_pairs={{0,32},{16,48},{32,0},{48,16},{1,33},{17,49},{33,1},{49,17},{2,34}... | collective-permute-start | bytes 995336 | tf_op jit(solution)/shard_map/ppermute | solution.py:415
  33.0 1.3 %collective-permute-start.16 = (bf16[1296,128]{1,0:T(8,128)(2,1)S(1)}, bf16[1296,128]{1,0:T(8,128)(2,1)S(1)}, u32[]{:S(2)}, u32[]{:S(2)}) collective-permute-start(bf16[1296,128]{1,0:T(8,128)(2,1)S(1)} %compose_group.1.chain.group), channel_id=1, source_target_pairs={{384,448},{400,464},{416,480},{432,496},{385,449},{401,465},{417,4... | collective-permute-start | bytes 995336 | tf_op jit(solution)/shard_map/ppermute | solution.py:397
  34.3 0.0 collective-permute-done.12.recv.joined
  34.3 0.0 collective-permute-done.11.recv
  34.3 0.2 hop.5
  34.6 1.3 %collective-permute-start.13 = (bf16[8,32,128]{2,1,0:T(8,128)(2,1)S(1)}, bf16[8,32,128]{2,1,0:T(8,128)(2,1)S(1)}, u32[]{:S(2)}, u32[]{:S(2)}) collective-permute-start(bf16[8,32,128]{2,1,0:T(8,128)(2,1)S(1)} %get-tuple-element.51), channel_id=1, source_target_pairs={{320,448},{336,464},{288,480},{304,496},{321,449},{337,465},{289,4... | collective-permute-start | bytes 196616 | tf_op jit(solution)/shard_map/ppermute | solution.py:397
  35.9 0.7 %collective-permute-start.14 = (bf16[8,32,128]{2,1,0:T(8,128)(2,1)S(1)}, bf16[8,32,128]{2,1,0:T(8,128)(2,1)S(1)}, u32[]{:S(2)}, u32[]{:S(2)}) collective-permute-start(bf16[8,32,128]{2,1,0:T(8,128)(2,1)S(1)} %get-tuple-element.51), channel_id=1, source_target_pairs={{320,384},{336,400},{288,416},{304,432},{321,385},{337,401},{289,4... | collective-permute-start | bytes 196616 | tf_op jit(solution)/shard_map/ppermute | solution.py:397
  36.5 0.2 fill.1
  36.8 0.7 %collective-permute-start.15 = (bf16[8,32,128]{2,1,0:T(8,128)(2,1)S(1)}, bf16[8,32,128]{2,1,0:T(8,128)(2,1)S(1)}, u32[]{:S(2)}, u32[]{:S(2)}) collective-permute-start(bf16[8,32,128]{2,1,0:T(8,128)(2,1)S(1)} %fill.1), channel_id=1, source_target_pairs={{192,256},{208,272},{288,352},{304,368},{193,257},{209,273},{289,3... | collective-permute-start | bytes 196616 | tf_op jit(solution)/shard_map/ppermute | solution.py:397
  37.4 0.0 collective-permute-done.17
  37.4 0.1 add_add_fusion.recv
  37.5 7.2 %collective-permute-done.16.before_last = bf16[1296,128]{1,0:T(8,128)(2,1)S(1)} collective-permute-done((bf16[1296,128]{1,0:T(8,128)(2,1)S(1)}, bf16[1296,128]{1,0:T(8,128)(2,1)S(1)}, u32[]{:S(2)}, u32[]{:S(2)}) %collective-permute-start.16) | collective-permute-done | bytes 331808 | tf_op jit(solution)/shard_map/ppermute | solution.py:397
  44.7 0.0 collective-permute-done.15.filled
  44.7 3.0 %collective-permute-done.13.arrived = bf16[8,32,128]{2,1,0:T(8,128)(2,1)S(1)} collective-permute-done((bf16[8,32,128]{2,1,0:T(8,128)(2,1)S(1)}, bf16[8,32,128]{2,1,0:T(8,128)(2,1)S(1)}, u32[]{:S(2)}, u32[]{:S(2)}) %collective-permute-start.13) | collective-permute-done | bytes 65568 | tf_op jit(solution)/shard_map/ppermute | solution.py:397
  47.7 0.0 collective-permute-done.14.passed
  47.7 0.5 share.1
  48.2 14.7 %all-gather = bf16[8,8,32,128]{3,2,1,0:T(8,128)(2,1)S(1)} all-gather(bf16[2,8,32,128]{3,2,1,0:T(8,128)(2,1)S(1)} %share.1), channel_id=2, replica_groups={{0,16,32,48},{64,80,96,112},{128,144,160,176},{192,208,224,240},{256,27..., dimensions={0}, use_global_device_ids=true | all-gather | bytes 655360 | tf_op jit(solution)/shard_map/all_gather | solution.py:450
  62.9 1.1 %finish.1 = bf16[1,4,8,32,128]{4,3,2,1,0:T(8,128)(2,1)} custom-call(f32[8,128]{1,0:T(8,128)S(1)} %get-tuple-element.43.active, bf16[4,2,8,32,128]{4,3,2,1,0:T(8,128)(2,1)S(1)} %bitcast.1, bf16[2,1296,128]{2,1,0:T(8,128)(2,1)S(1)} %maps_kept.1.keep, bf16[2,1296,128]{2,1,0:T(8,128)(2,1)S(1)} %edge_sent.1.odd.send, ...), custom_call_target="tpu_custom_call" | custom-call | tf_op jit(solution)/shard_map/finish/pallas_call | solution.py:453
  (1 shorter events, 0.0 us)
Async XLA Ops:
  0.9 7.5 %collective-permute-start.1 = (bf16[1,8,32,128]{3,2,1,0:T(8,128)(2,1)S(1)}, bf16[1,8,32,128]{3,2,1,0:T(8,128)(2,1)S(1)}, u32[]{:S(2)}, u32[]{:S(2)}) collective-permute-start(bf16[1,8,32,128]{3,2,1,0:T(8,128)(2,1)S(1)} %get-tuple-element.31), channel_id=1, source_target_pairs={{1,0},{2,1},{3,2},{4,3},{5,4},{6,5},{7,6},{8,7},{9,8},{10,9},{11,1... | collective-permute-start | bytes 196616 | tf_op jit(solution)/shard_map/ppermute | solution.py:334
  4.0 9.9 %collective-permute-start = (bf16[1,8,32,128]{3,2,1,0:T(8,128)(2,1)S(1)}, bf16[1,8,32,128]{3,2,1,0:T(8,128)(2,1)S(1)}, u32[]{:S(2)}, u32[]{:S(2)}) collective-permute-start(bf16[1,8,32,128]{3,2,1,0:T(8,128)(2,1)S(1)} %get-tuple-element.30), channel_id=1, source_target_pairs={{0,1},{1,2},{2,3},{3,4},{4,5},{5,6},{6,7},{7,8},{8,9},{9,10},{10,1... | collective-permute-start | bytes 196616 | tf_op jit(solution)/shard_map/ppermute | solution.py:334
  8.6 7.5 %collective-permute-start.2 = (bf16[2,1296,128]{2,1,0:T(8,128)(2,1)S(1)}, bf16[2,1296,128]{2,1,0:T(8,128)(2,1)S(1)}, u32[]{:S(2)}, u32[]{:S(2)}) collective-permute-start(bf16[2,1296,128]{2,1,0:T(8,128)(2,1)S(1)} %edge_sent.1.odd.send), channel_id=1, source_target_pairs={{0,16},{16,0},{32,48},{48,32},{64,80},{80,64},{96,112},{112,96},{1... | collective-permute-start | bytes 1990664 | tf_op jit(solution)/shard_map/ppermute | solution.py:399
  16.5 6.3 %collective-permute-start.6 = (bf16[1296,128]{1,0:T(8,128)(2,1)S(1)}, bf16[1296,128]{1,0:T(8,128)(2,1)S(1)}, u32[]{:S(2)}, u32[]{:S(2)}) collective-permute-start(bf16[1296,128]{1,0:T(8,128)(2,1)S(1)} %get-tuple-element.53.send.pair_send), channel_id=1, source_target_pairs={{64,96},{80,112},{96,64},{112,80},{65,97},{81,113},{97,65},{113,81... | collective-permute-start | bytes 995336 | tf_op jit(solution)/shard_map/ppermute | solution.py:404
  17.1 3.3 %collective-permute-start.3 = (bf16[2,8,32,128]{3,2,1,0:T(8,128)(2,1)S(1)}, bf16[2,8,32,128]{3,2,1,0:T(8,128)(2,1)S(1)}, u32[]{:S(2)}, u32[]{:S(2)}) collective-permute-start(bf16[2,8,32,128]{3,2,1,0:T(8,128)(2,1)S(1)} %get-tuple-element.37), channel_id=1, source_target_pairs={{0,32},{16,48},{1,33},{17,49},{2,34},{18,50},{3,35},{19,51},{4,36}... | collective-permute-start | bytes 393224 | tf_op jit(solution)/shard_map/ppermute | solution.py:403
  17.8 11.3 %collective-permute-start.9 = (bf16[1296,128]{1,0:T(8,128)(2,1)S(1)}, bf16[1296,128]{1,0:T(8,128)(2,1)S(1)}, u32[]{:S(2)}, u32[]{:S(2)}) collective-permute-start(bf16[1296,128]{1,0:T(8,128)(2,1)S(1)} %get-tuple-element.53.send.pair_send), channel_id=1, source_target_pairs={{128,160},{144,176},{160,128},{176,144},{192,224},{208,240},{224,1... | collective-permute-start | bytes 995336 | tf_op jit(solution)/shard_map/ppermute | solution.py:405
  20.8 2.0 %collective-permute-start.4 = (bf16[8,32,128]{2,1,0:T(8,128)(2,1)S(1)}, bf16[8,32,128]{2,1,0:T(8,128)(2,1)S(1)}, u32[]{:S(2)}, u32[]{:S(2)}) collective-permute-start(bf16[8,32,128]{2,1,0:T(8,128)(2,1)S(1)} %get-tuple-element.39), channel_id=1, source_target_pairs={{32,64},{48,80},{33,65},{49,81},{34,66},{50,82},{35,67},{51,83},{3... | collective-permute-start | bytes 196616 | tf_op jit(solution)/shard_map/ppermute | solution.py:408
  21.4 1.3 %collective-permute-start.5 = (bf16[8,32,128]{2,1,0:T(8,128)(2,1)S(1)}, bf16[8,32,128]{2,1,0:T(8,128)(2,1)S(1)}, u32[]{:S(2)}, u32[]{:S(2)}) collective-permute-start(bf16[8,32,128]{2,1,0:T(8,128)(2,1)S(1)} %get-tuple-element.40), channel_id=1, source_target_pairs={{32,96},{48,112},{33,97},{49,113},{34,98},{50,114},{35,99},{51,115... | collective-permute-start | bytes 196616 | tf_op jit(solution)/shard_map/ppermute | solution.py:407
  23.2 6.9 %collective-permute-start.8 = (bf16[8,32,128]{2,1,0:T(8,128)(2,1)S(1)}, bf16[8,32,128]{2,1,0:T(8,128)(2,1)S(1)}, u32[]{:S(2)}, u32[]{:S(2)}) collective-permute-start(bf16[8,32,128]{2,1,0:T(8,128)(2,1)S(1)} %get-tuple-element.41), channel_id=1, source_target_pairs={{64,128},{80,144},{96,160},{112,176},{65,129},{81,145},{97,161},{1... | collective-permute-start | bytes 196616 | tf_op jit(solution)/shard_map/ppermute | solution.py:397
  23.9 7.1 %collective-permute-start.7 = (bf16[2,1296,128]{2,1,0:T(8,128)(2,1)S(1)}, bf16[2,1296,128]{2,1,0:T(8,128)(2,1)S(1)}, u32[]{:S(2)}, u32[]{:S(2)}) collective-permute-start(bf16[2,1296,128]{2,1,0:T(8,128)(2,1)S(1)} %maps_kept.1.keep), channel_id=1, source_target_pairs={{0,16},{32,48},{64,80},{96,112},{128,144},{160,176},{192,208},{224... | collective-permute-start | bytes 1990664 | tf_op jit(solution)/shard_map/ppermute | solution.py:416
  29.4 4.9 %collective-permute-start.12 = (bf16[1296,128]{1,0:T(8,128)(2,1)S(1)}, bf16[1296,128]{1,0:T(8,128)(2,1)S(1)}, u32[]{:S(2)}, u32[]{:S(2)}) collective-permute-start(bf16[1296,128]{1,0:T(8,128)(2,1)S(1)} %compose_group.1.chain.group), channel_id=1, source_target_pairs={{256,320},{272,336},{352,288},{368,304},{257,321},{273,337},{353,2... | collective-permute-start | bytes 995336 | tf_op jit(solution)/shard_map/ppermute | solution.py:397
  30.3 1.1 %collective-permute-start.10 = (bf16[8,32,128]{2,1,0:T(8,128)(2,1)S(1)}, bf16[8,32,128]{2,1,0:T(8,128)(2,1)S(1)}, u32[]{:S(2)}, u32[]{:S(2)}) collective-permute-start(bf16[8,32,128]{2,1,0:T(8,128)(2,1)S(1)} %get-tuple-element.46), channel_id=1, source_target_pairs={{128,192},{144,208},{160,224},{176,240},{129,193},{145,209},{161,2... | collective-permute-start | bytes 196616 | tf_op jit(solution)/shard_map/ppermute | solution.py:397
  31.6 2.7 %collective-permute-start.11 = (bf16[8,32,128]{2,1,0:T(8,128)(2,1)S(1)}, bf16[8,32,128]{2,1,0:T(8,128)(2,1)S(1)}, u32[]{:S(2)}, u32[]{:S(2)}) collective-permute-start(bf16[8,32,128]{2,1,0:T(8,128)(2,1)S(1)} %get-tuple-element.49), channel_id=1, source_target_pairs={{192,320},{208,336},{224,288},{240,304},{193,321},{209,337},{225,2... | collective-permute-start | bytes 196616 | tf_op jit(solution)/shard_map/ppermute | solution.py:397
  32.3 5.2 %collective-permute-start.17 = (bf16[1296,128]{1,0:T(8,128)(2,1)S(1)}, bf16[1296,128]{1,0:T(8,128)(2,1)S(1)}, u32[]{:S(2)}, u32[]{:S(2)}) collective-permute-start(bf16[1296,128]{1,0:T(8,128)(2,1)S(1)} %get-tuple-element.53.send.pair_send), channel_id=1, source_target_pairs={{0,32},{16,48},{32,0},{48,16},{1,33},{17,49},{33,1},{49,17},{2,34}... | collective-permute-start | bytes 995336 | tf_op jit(solution)/shard_map/ppermute | solution.py:415
  33.0 11.8 %collective-permute-start.16 = (bf16[1296,128]{1,0:T(8,128)(2,1)S(1)}, bf16[1296,128]{1,0:T(8,128)(2,1)S(1)}, u32[]{:S(2)}, u32[]{:S(2)}) collective-permute-start(bf16[1296,128]{1,0:T(8,128)(2,1)S(1)} %compose_group.1.chain.group), channel_id=1, source_target_pairs={{384,448},{400,464},{416,480},{432,496},{385,449},{401,465},{417,4... | collective-permute-start | bytes 995336 | tf_op jit(solution)/shard_map/ppermute | solution.py:397
  34.6 13.2 %collective-permute-start.13 = (bf16[8,32,128]{2,1,0:T(8,128)(2,1)S(1)}, bf16[8,32,128]{2,1,0:T(8,128)(2,1)S(1)}, u32[]{:S(2)}, u32[]{:S(2)}) collective-permute-start(bf16[8,32,128]{2,1,0:T(8,128)(2,1)S(1)} %get-tuple-element.51), channel_id=1, source_target_pairs={{320,448},{336,464},{288,480},{304,496},{321,449},{337,465},{289,4... | collective-permute-start | bytes 196616 | tf_op jit(solution)/shard_map/ppermute | solution.py:397
  35.9 11.9 %collective-permute-start.14 = (bf16[8,32,128]{2,1,0:T(8,128)(2,1)S(1)}, bf16[8,32,128]{2,1,0:T(8,128)(2,1)S(1)}, u32[]{:S(2)}, u32[]{:S(2)}) collective-permute-start(bf16[8,32,128]{2,1,0:T(8,128)(2,1)S(1)} %get-tuple-element.51), channel_id=1, source_target_pairs={{320,384},{336,400},{288,416},{304,432},{321,385},{337,401},{289,4... | collective-permute-start | bytes 196616 | tf_op jit(solution)/shard_map/ppermute | solution.py:397
  36.8 8.0 %collective-permute-start.15 = (bf16[8,32,128]{2,1,0:T(8,128)(2,1)S(1)}, bf16[8,32,128]{2,1,0:T(8,128)(2,1)S(1)}, u32[]{:S(2)}, u32[]{:S(2)}) collective-permute-start(bf16[8,32,128]{2,1,0:T(8,128)(2,1)S(1)} %fill.1), channel_id=1, source_target_pairs={{192,256},{208,272},{288,352},{304,368},{193,257},{209,273},{289,3... | collective-permute-start | bytes 196616 | tf_op jit(solution)/shard_map/ppermute | solution.py:397
